TPU v7x, 256 devices: a whole 4x4x8 slice. The times are simulated.
256 devices in a mesh: rows: 32 (over x_lo, z, core), cols: 8 (over y, x_hi).
Axes of the slice: x: 4 (x_hi: 2, x_lo: 2; x = x_hi * 2 + x_lo), y: 4, z: 8, core: 2. Of those that a mesh axis runs over, the one named last changes fastest.
Arguments:
- density: float32 [8192, 8192], P('rows', 'cols'), may hold values from 0.25 to 4
- value_field: float32 [8192, 8192], P('rows', 'cols'), may hold values from -6 to 6
- potential: float32 [8192, 8192], P('rows', 'cols'), may hold values from -6 to 6
- kern_rows: float32 [256], replicated, may hold values from -0.375 to 0.375
- kern_cols: float32 [256], replicated, may hold values from -0.375 to 0.375
Outputs:
- density_out: float32 [8192, 8192], P('rows', 'cols')
- value_out: float32 [8192, 8192], P('rows', 'cols')
All inputs are finite; a program needn't handle non-finite values.
Results may differ from a plain program's by a relative error of at most 0.0001.
Values sent between devices are 32-bit elements; how exact they have to be, the bound alone decides.
No kernel may reach another device: no remote copies, remote signals or barrier semaphores. Data moves between devices by JAX's collectives and lax.ppermute only.
A program may use at most 64 MiB of HBM per device.

v0:
```python
import math

import jax
import jax.numpy as jnp
from jax import lax
from jax.sharding import PartitionSpec as P

STEPS = 2


diffusion = 0.5
time_step = 0.1


def extended(block, sides, width):
    for axis, dim in sides:
        count = lax.axis_size(axis)
        forward = [(i, i + 1) for i in range(count - 1)]
        forward.append((count - 1, 0))
        backward = [(target, source) for source, target in forward]
        low = lax.ppermute(
            lax.slice_in_dim(block, block.shape[dim] - width, None, axis=dim), axis, forward
        )
        high = lax.ppermute(lax.slice_in_dim(block, 0, width, axis=dim), axis, backward)
        block = jnp.concatenate([low, block, high], axis=dim)
    return block


def offset_view(padded, row_step, col_step):
    row_count = padded.shape[0] - 2
    col_count = padded.shape[1] - 2
    return padded[1 + row_step : 1 + row_step + row_count, 1 + col_step : 1 + col_step + col_count]


def density_step(dens_pad, value_pad):
    here_cell = offset_view(dens_pad, 0, 0)
    cell_up = offset_view(dens_pad, -1, 0)
    cell_down = offset_view(dens_pad, 1, 0)
    cell_left = offset_view(dens_pad, 0, -1)
    cell_right = offset_view(dens_pad, 0, 1)
    level_here = offset_view(value_pad, 0, 0)
    level_up = offset_view(value_pad, -1, 0)
    level_down = offset_view(value_pad, 1, 0)
    level_left = offset_view(value_pad, 0, -1)
    level_right = offset_view(value_pad, 0, 1)
    speed_down = level_here - level_down
    flux_down = jnp.maximum(speed_down, 0.0) * here_cell + jnp.minimum(speed_down, 0.0) * cell_down
    speed_up = level_up - level_here
    flux_up = jnp.maximum(speed_up, 0.0) * cell_up + jnp.minimum(speed_up, 0.0) * here_cell
    speed_right = level_here - level_right
    flux_right = (
        jnp.maximum(speed_right, 0.0) * here_cell + jnp.minimum(speed_right, 0.0) * cell_right
    )
    speed_left = level_left - level_here
    flux_left = jnp.maximum(speed_left, 0.0) * cell_left + jnp.minimum(speed_left, 0.0) * here_cell
    laplace = cell_up + cell_down + cell_left + cell_right - 4.0 * here_cell
    return here_cell + time_step * (
        diffusion * laplace - (flux_down - flux_up) - (flux_right - flux_left)
    )


def value_step(value_pad, running_cost):
    level_here = offset_view(value_pad, 0, 0)
    level_up = offset_view(value_pad, -1, 0)
    level_down = offset_view(value_pad, 1, 0)
    level_left = offset_view(value_pad, 0, -1)
    level_right = offset_view(value_pad, 0, 1)
    grad_sq = jnp.square(jnp.maximum(level_here - level_up, 0.0)) + jnp.square(
        jnp.minimum(level_down - level_here, 0.0)
    )
    grad_sq = (
        grad_sq
        + jnp.square(jnp.maximum(level_here - level_left, 0.0))
        + jnp.square(jnp.minimum(level_right - level_here, 0.0))
    )
    laplace = level_up + level_down + level_left + level_right - 4.0 * level_here
    return level_here + time_step * (diffusion * laplace - 0.5 * grad_sq + running_cost)


def contract(form, left, right):
    return jnp.einsum(form, left, right, precision=lax.Precision.HIGHEST)


def trig_table(first_size, second_size, length):
    products = (
        lax.iota(jnp.int32, first_size)[:, None]
        * lax.iota(jnp.int32, second_size)[None, :]
        % length
    )
    angles = products.astype(jnp.float32) * (-2.0 * math.pi / length)
    return (jnp.cos(angles), jnp.sin(angles))


def forward_dft(signal, tables):
    cos_a, sin_a, cos_t, sin_t, cos_b, sin_b = tables
    outer_size = cos_a.shape[0]
    inner_size = cos_b.shape[0]
    blocks = signal.reshape(signal.shape[0], outer_size, inner_size)
    first_re = contract("rab,ak->rkb", blocks, cos_a)
    first_im = contract("rab,ak->rkb", blocks, sin_a)
    turned_re = first_re * cos_t - first_im * sin_t
    turned_im = first_re * sin_t + first_im * cos_t
    spec_re = contract("rkb,bq->rkq", turned_re, cos_b) - contract("rkb,bq->rkq", turned_im, sin_b)
    spec_im = contract("rkb,bq->rkq", turned_re, sin_b) + contract("rkb,bq->rkq", turned_im, cos_b)
    return (spec_re, spec_im)


def inverse_dft(spec_re, spec_im, tables):
    cos_a, sin_a, cos_t, sin_t, cos_b, sin_b = tables
    length = cos_a.shape[0] * cos_b.shape[0]
    back_re = contract("rkq,bq->rkb", spec_re, cos_b) + contract("rkq,bq->rkb", spec_im, sin_b)
    back_im = contract("rkq,bq->rkb", spec_im, cos_b) - contract("rkq,bq->rkb", spec_re, sin_b)
    untw_re = back_re * cos_t + back_im * sin_t
    untw_im = back_im * cos_t - back_re * sin_t
    result = contract("rkb,ak->rab", untw_re, cos_a) + contract("rkb,ak->rab", untw_im, sin_a)
    return result.reshape(spec_re.shape[0], length) / length


def spectral_conv(signal, kernel):
    length = signal.shape[1]
    inner_size = 128
    outer_size = length // inner_size
    cos_a, sin_a = trig_table(outer_size, outer_size, outer_size)
    cos_t, sin_t = trig_table(outer_size, inner_size, length)
    cos_b, sin_b = trig_table(inner_size, inner_size, inner_size)
    tables = (cos_a, sin_a, cos_t, sin_t, cos_b, sin_b)
    half_width = kernel.shape[0] // 2
    zero_fill = jnp.zeros((length - kernel.shape[0],), jnp.float32)
    kernel_full = jnp.concatenate((kernel[half_width:], zero_fill, kernel[:half_width]))[None, :]
    kern_re, kern_im = forward_dft(kernel_full, tables)
    spec_re, spec_im = forward_dft(signal, tables)
    prod_re = spec_re * kern_re - spec_im * kern_im
    prod_im = spec_re * kern_im + spec_im * kern_re
    return inverse_dft(prod_re, prod_im, tables)


def along_cols(field, kernel):
    pencil = lax.all_to_all(field, "cols", split_axis=0, concat_axis=1, tiled=True)
    blended = spectral_conv(pencil, kernel)
    return lax.all_to_all(blended, "cols", split_axis=1, concat_axis=0, tiled=True)


def along_rows(field, kernel):
    pencil = lax.all_to_all(field.T, "rows", split_axis=0, concat_axis=1, tiled=True)
    blended = spectral_conv(pencil, kernel)
    returned = lax.all_to_all(blended, "rows", split_axis=1, concat_axis=0, tiled=True)
    return returned.T


def body(density, value_field, potential, kern_rows, kern_cols):
    for step_index in range(STEPS):
        fields = jnp.stack((density, value_field))
        padded = extended(fields, (("rows", 1), ("cols", 2)), 1)
        dens_pad = padded[0]
        value_pad = padded[1]
        density = density_step(dens_pad, value_pad)
        spread = along_cols(density, kern_cols)
        congestion = along_rows(spread, kern_rows)
        value_field = value_step(value_pad, potential + congestion)
    return (density, value_field)


def solution(mesh):
    placed = (P("rows", "cols"), P("rows", "cols"), P("rows", "cols"), P(), P())
    return jax.shard_map(
        body,
        mesh=mesh,
        in_specs=placed,
        out_specs=(P("rows", "cols"), P("rows", "cols")),
        check_vma=False,
    )
```

profile of v0, /device:TPU:1, one launch (start us, length us, event | category | flops | bytes accessed | tf_op | source)
XLA Modules:
  0.0 351.5 jit_solution(8694442658900127121)
XLA Ops:
  1.6 3.1 collective-permute-start
  5.9 1.9 collective-permute-done.1
  8.3 5.3 %collective-permute-start.3 = (f32[2,258,1]{2,1,0:T(8,128)S(1)}, f32[2,258,1]{2,1,0:T(8,128)S(1)}, u32[]{:S(2)}, u32[]{:S(2)}) collective-permute-start(f32[2,258,1]{2,1,0:T(8,128)S(1)} %get-tuple-element.10), channel_id=1, source_target_pairs={{1,0},{2,1},{3,2},{4,3},{5,4},{6,5},{7,6},{0,7},{9,8},{10,9},{11,1... | collective-permute-start | bytes 6200 | tf_op jit(solution)/shard_map/ppermute | solution.py:24
  13.9 3.0 collective-permute-done.3
  17.0 8.3 %collective-permute-done.2 = f32[2,258,1]{2,1,0:T(8,128)S(1)} collective-permute-done((f32[2,258,1]{2,1,0:T(8,128)S(1)}, f32[2,258,1]{2,1,0:T(8,128)S(1)}, u32[]{:S(2)}, u32[]{:S(2)}) %collective-permute-start.2) | collective-permute-done | bytes 2096 | tf_op jit(solution)/shard_map/ppermute | solution.py:21
  25.2 2.5 concatenate.21
  27.8 1.8 slice_bitcast_fusion.2
  29.6 3.3 multiply_add_fusion.9
  32.9 3.8 %all-to-all-start = ((f32[8,32,1024]{2,1,0:T(8,128)}), f32[8,32,1024]{2,1,0:T(8,128)S(1)}, u32[]{:S(2)}, u32[]{:S(2)}) async-start(f32[8,32,1024]{2,1,0:T(8,128)} %bitcast.8), calls=%async_computation | async-start | bytes 2097152 | tf_op jit(solution)/shard_map/all_to_all | solution.py:138
  39.3 11.5 %all-to-all-done = f32[8,32,1024]{2,1,0:T(8,128)S(1)} async-done(((f32[8,32,1024]{2,1,0:T(8,128)}), f32[8,32,1024]{2,1,0:T(8,128)S(1)}, u32[]{:S(2)}, u32[]{:S(2)}) %all-to-all-start) | async-done | bytes 1048608 | tf_op jit(solution)/shard_map/all_to_all | solution.py:138
  57.7 1.2 convolution_subtract_fusion.7
  58.9 1.2 fusion.84
  60.2 1.7 fusion.83
  61.9 1.2 convolution_subtract_fusion.6
  63.1 1.2 convolution_add_fusion.10
  67.6 18.2 %all_to_all.128 = f32[32,8,1024]{2,0,1:T(8,128)S(1)} all-to-all(f32[32,8,1024]{2,0,1:T(8,128)S(1)} %copy.46), channel_id=1, replica_groups=mesh['rows'=32,'cols'=8] {'cols'}, dimensions={1} | all-to-all | bytes 2097152 | tf_op jit(solution)/shard_map/all_to_all | solution.py:140
  85.8 1.3 copy.47
  87.1 14.9 %all-to-all-start.2 = ((f32[32,32,256]{2,1,0:T(8,128)}), f32[32,32,256]{2,1,0:T(8,128)S(1)}, u32[]{:S(2)}, u32[]{:S(2)}) async-start(f32[32,32,256]{2,1,0:T(8,128)} %bitcast.21), calls=%async_computation.2 | async-start | bytes 2097152 | tf_op jit(solution)/shard_map/all_to_all | solution.py:144
  105.1 23.2 %all-to-all-done.2 = f32[32,32,256]{2,1,0:T(8,128)S(1)} async-done(((f32[32,32,256]{2,1,0:T(8,128)}), f32[32,32,256]{2,1,0:T(8,128)S(1)}, u32[]{:S(2)}, u32[]{:S(2)}) %all-to-all-start.2) | async-done | bytes 1048608 | tf_op jit(solution)/shard_map/all_to_all | solution.py:144
  136.3 1.2 fusion.86
  137.5 1.7 fusion.85
  139.2 1.2 convolution_subtract_fusion.4
  140.4 1.2 convolution_add_fusion.7
  145.0 32.2 %all_to_all.129 = f32[32,32,256]{2,0,1:T(8,128)S(1)} all-to-all(f32[32,32,256]{2,0,1:T(8,128)S(1)} %copy.51), channel_id=1, replica_groups=mesh['rows'=32,'cols'=8] {'rows'}, dimensions={1} | all-to-all | bytes 2097152 | tf_op jit(solution)/shard_map/all_to_all | solution.py:146
  177.6 2.6 fusion.26
  181.0 4.2 %collective-permute-start.4 = (f32[2,1,1024]{2,1,0:T(1,128)S(1)}, f32[2,1,1024]{2,1,0:T(1,128)S(1)}, u32[]{:S(2)}, u32[]{:S(2)}) collective-permute-start(f32[2,1,1024]{2,1,0:T(1,128)S(1)} %get-tuple-element.12), channel_id=1, source_target_pairs={{0,8},{8,16},{16,24},{24,32},{32,40},{40,48},{48,56},{56,64},{64,7... | collective-permute-start | bytes 24584 | tf_op jit(solution)/shard_map/ppermute | solution.py:21
  186.0 2.3 collective-permute-done.5
  188.3 1.5 pad_maximum_fusion.1
  189.9 1.8 collective-permute-start.7
  191.7 1.3 collective-permute-start.6
  193.0 6.5 %collective-permute-done.7 = f32[2,258,1]{2,1,0:T(8,128)S(1)} collective-permute-done((f32[2,258,1]{2,1,0:T(8,128)S(1)}, f32[2,258,1]{2,1,0:T(8,128)S(1)}, u32[]{:S(2)}, u32[]{:S(2)}) %collective-permute-start.7) | collective-permute-done | bytes 2096 | tf_op jit(solution)/shard_map/ppermute | solution.py:24
  199.5 6.0 %collective-permute-done.6 = f32[2,258,1]{2,1,0:T(8,128)S(1)} collective-permute-done((f32[2,258,1]{2,1,0:T(8,128)S(1)}, f32[2,258,1]{2,1,0:T(8,128)S(1)}, u32[]{:S(2)}, u32[]{:S(2)}) %collective-permute-start.6) | collective-permute-done | bytes 2096 | tf_op jit(solution)/shard_map/ppermute | solution.py:21
  205.5 2.5 concatenate.25
  208.0 1.8 slice_bitcast_fusion
  209.8 2.3 multiply_add_fusion.4
  212.1 19.2 %all_to_all.130 = f32[8,32,1024]{2,1,0:T(8,128)S(1)} all-to-all(f32[8,32,1024]{2,1,0:T(8,128)S(1)} %bitcast.240), channel_id=1, replica_groups=mesh['rows'=32,'cols'=8] {'cols'}, dimensions={0} | all-to-all | bytes 2097152 | tf_op jit(solution)/shard_map/all_to_all | solution.py:138
  239.4 1.2 fusion.88
  240.6 1.2 fusion.87
  241.9 1.2 convolution_subtract_fusion.2
  243.1 1.5 convolution_add_fusion.4
  247.8 17.6 %all_to_all.131 = f32[32,8,1024]{2,0,1:T(8,128)S(1)} all-to-all(f32[32,8,1024]{2,0,1:T(8,128)S(1)} %copy.56), channel_id=1, replica_groups=mesh['rows'=32,'cols'=8] {'cols'}, dimensions={1} | all-to-all | bytes 2097152 | tf_op jit(solution)/shard_map/all_to_all | solution.py:140
  265.8 32.7 %all_to_all.132 = f32[32,32,256]{2,1,0:T(8,128)S(1)} all-to-all(f32[32,32,256]{2,1,0:T(8,128)S(1)} %bitcast.232), channel_id=1, replica_groups=mesh['rows'=32,'cols'=8] {'rows'}, dimensions={0} | all-to-all | bytes 2097152 | tf_op jit(solution)/shard_map/all_to_all | solution.py:144
  306.5 1.2 fusion.90
  307.7 1.2 fusion.89
  309.0 1.2 convolution_subtract_fusion
  310.2 1.6 convolution_add_fusion.1
  315.2 32.2 %all_to_all.133 = f32[32,32,256]{2,0,1:T(8,128)S(1)} all-to-all(f32[32,32,256]{2,0,1:T(8,128)S(1)} %copy.61), channel_id=1, replica_groups=mesh['rows'=32,'cols'=8] {'rows'}, dimensions={1} | all-to-all | bytes 2097152 | tf_op jit(solution)/shard_map/all_to_all | solution.py:146
  347.8 3.6 %fusion.10 = f32[256,1024]{1,0:T(8,128)} fusion(f32[256,1024]{1,0:T(8,128)} %param.7, f32[1024,256]{0,1:T(8,128)S(1)} %copy.62, f32[258,1026]{1,0:T(8,128)S(1)} %get-tuple-element.4), kind=kLoop, calls=%fused_computation.41 | loop fusion | flops 7077888 | bytes 8388608 | tf_op jit(solution)/shard_map/add | solution.py:77
  (84 shorter events, 54.7 us)
Async XLA Ops:
  0.6 7.2 %copy-start = (f32[256,1024]{1,0:T(8,128)S(1)}, f32[256,1024]{1,0:T(8,128)}, u32[]{:S(2)}) copy-start(f32[256,1024]{1,0:T(8,128)} %param.6) | copy-start | bytes 3145732
  0.6 7.2 %copy-start.1 = (f32[256,1024]{1,0:T(8,128)S(1)}, f32[256,1024]{1,0:T(8,128)}, u32[]{:S(2)}) copy-start(f32[256,1024]{1,0:T(8,128)} %param.5) | copy-start | bytes 3145732
  1.6 4.3 %collective-permute-start = (f32[2,1,1024]{2,1,0:T(1,128)S(1)}, f32[2,1,1024]{2,1,0:T(1,128)S(1)}, u32[]{:S(2)}, u32[]{:S(2)}) collective-permute-start(f32[2,1,1024]{2,1,0:T(1,128)S(1)} %get-tuple-element.14), channel_id=1, source_target_pairs={{0,8},{8,16},{16,24},{24,32},{32,40},{40,48},{48,56},{56,64},{64,7... | collective-permute-start | bytes 24584 | tf_op jit(solution)/shard_map/ppermute | solution.py:21
  4.7 3.1 collective-permute-start.1
  8.3 8.7 %collective-permute-start.3 = (f32[2,258,1]{2,1,0:T(8,128)S(1)}, f32[2,258,1]{2,1,0:T(8,128)S(1)}, u32[]{:S(2)}, u32[]{:S(2)}) collective-permute-start(f32[2,258,1]{2,1,0:T(8,128)S(1)} %get-tuple-element.10), channel_id=1, source_target_pairs={{1,0},{2,1},{3,2},{4,3},{5,4},{6,5},{7,6},{0,7},{9,8},{10,9},{11,1... | collective-permute-start | bytes 6200 | tf_op jit(solution)/shard_map/ppermute | solution.py:24
  13.6 11.7 %collective-permute-start.2 = (f32[2,258,1]{2,1,0:T(8,128)S(1)}, f32[2,258,1]{2,1,0:T(8,128)S(1)}, u32[]{:S(2)}, u32[]{:S(2)}) collective-permute-start(f32[2,258,1]{2,1,0:T(8,128)S(1)} %get-tuple-element.11), channel_id=1, source_target_pairs={{0,1},{1,2},{2,3},{3,4},{4,5},{5,6},{6,7},{7,0},{8,9},{9,10},{10,1... | collective-permute-start | bytes 6200 | tf_op jit(solution)/shard_map/ppermute | solution.py:21
  32.9 18.0 %all-to-all-start = ((f32[8,32,1024]{2,1,0:T(8,128)}), f32[8,32,1024]{2,1,0:T(8,128)S(1)}, u32[]{:S(2)}, u32[]{:S(2)}) async-start(f32[8,32,1024]{2,1,0:T(8,128)} %bitcast.8), calls=%async_computation | async-start | bytes 2097152 | tf_op jit(solution)/shard_map/all_to_all | solution.py:138
  85.8 16.2 %copy-start.3 = (f32[256]{0:T(256)S(1)}, f32[256]{0:T(256)}, u32[]{:S(2)}) copy-start(f32[256]{0:T(256)} %param.8) | copy-start | bytes 3076
  87.1 41.2 %all-to-all-start.2 = ((f32[32,32,256]{2,1,0:T(8,128)}), f32[32,32,256]{2,1,0:T(8,128)S(1)}, u32[]{:S(2)}, u32[]{:S(2)}) async-start(f32[32,32,256]{2,1,0:T(8,128)} %bitcast.21), calls=%async_computation.2 | async-start | bytes 2097152 | tf_op jit(solution)/shard_map/all_to_all | solution.py:144
  181.0 5.0 %collective-permute-start.4 = (f32[2,1,1024]{2,1,0:T(1,128)S(1)}, f32[2,1,1024]{2,1,0:T(1,128)S(1)}, u32[]{:S(2)}, u32[]{:S(2)}) collective-permute-start(f32[2,1,1024]{2,1,0:T(1,128)S(1)} %get-tuple-element.12), channel_id=1, source_target_pairs={{0,8},{8,16},{16,24},{24,32},{32,40},{40,48},{48,56},{56,64},{64,7... | collective-permute-start | bytes 24584 | tf_op jit(solution)/shard_map/ppermute | solution.py:21
  185.2 3.1 collective-permute-start.5
  189.9 9.5 %collective-permute-start.7 = (f32[2,258,1]{2,1,0:T(8,128)S(1)}, f32[2,258,1]{2,1,0:T(8,128)S(1)}, u32[]{:S(2)}, u32[]{:S(2)}) collective-permute-start(f32[2,258,1]{2,1,0:T(8,128)S(1)} %get-tuple-element.8), channel_id=1, source_target_pairs={{1,0},{2,1},{3,2},{4,3},{5,4},{6,5},{7,6},{0,7},{9,8},{10,9},{11,1... | collective-permute-start | bytes 6200 | tf_op jit(solution)/shard_map/ppermute | solution.py:24
  191.7 13.8 %collective-permute-start.6 = (f32[2,258,1]{2,1,0:T(8,128)S(1)}, f32[2,258,1]{2,1,0:T(8,128)S(1)}, u32[]{:S(2)}, u32[]{:S(2)}) collective-permute-start(f32[2,258,1]{2,1,0:T(8,128)S(1)} %get-tuple-element.9), channel_id=1, source_target_pairs={{0,1},{1,2},{2,3},{3,4},{4,5},{5,6},{6,7},{7,0},{8,9},{9,10},{10,1... | collective-permute-start | bytes 6200 | tf_op jit(solution)/shard_map/ppermute | solution.py:21
  212.1 19.2 %copy-start.2 = (f32[256,1024]{1,0:T(8,128)}, f32[256,1024]{1,0:T(8,128)S(1)}, u32[]{:S(2)}) copy-start(f32[256,1024]{1,0:T(8,128)S(1)} %multiply_add_fusion.4) | copy-start | bytes 3145732
where the time goes:
time: 359 us; the launch traced here: 351 us
  blocking collectives  152 us (42%)
  matrix products  65.7 us (18%)
  waiting for transfers between devices  63.5 us (18%)
  starting transfers between devices  34.7 us (10%)
  local copies, waits for them, and re-layouts  18.3 us (5%)
  other arithmetic  15.5 us (4%)
    dot_general x60, matrix products, contract(): return jnp.einsum(form, left, right, precision=lax.Precision.HIGHEST)  65.7 us
    all_to_all x2, blocking collectives, along_rows(): lax.all_to_all(blended, 'rows', split_axis=1, concat_axis=0, tiled=True)  64.5 us
    all_to_all x2, blocking collectives, along_cols(): lax.all_to_all(blended, 'cols', split_axis=1, concat_axis=0, tiled=True)  35.9 us
    all_to_all x1, blocking collectives, along_rows(): lax.all_to_all(field.T, 'rows', split_axis=0, concat_axis=1, tiled=True)  32.7 us
    all_to_all x1, waiting for transfers between devices, along_rows(): lax.all_to_all(field.T, 'rows', split_axis=0, concat_axis=1, tiled=True)  23.2 us
    all_to_all x1, blocking collectives, along_cols(): lax.all_to_all(field, 'cols', split_axis=0, concat_axis=1, tiled=True)  19.2 us
    ppermute x4, waiting for transfers between devices, extended(): lax.ppermute(lax.slice_in_dim(block, block.shape[dim] - width, None, axis...  15.1 us
    all_to_all x1, starting transfers between devices, along_rows(): lax.all_to_all(field.T, 'rows', split_axis=0, concat_axis=1, tiled=True)  14.9 us
  transfers between devices with their start and end apart: 10, of which 9 were waited for; matrix products, arithmetic and copies ran while one was open for 2% of the time, Pallas kernels for 0%

commit v1 on v0

v1 whole, which is shorter than its diff:
```python
import functools

import jax
import jax.numpy as jnp
from jax import lax
from jax.experimental import pallas as pl
from jax.experimental.pallas import tpu as pltpu
from jax.sharding import PartitionSpec as P

STEPS = 2
NU = 0.5
DT = 0.1

ROWS = 256
COLS = 1024
KW = 256
HR = 136
HL = 128
NR = ROWS + 2 * HR
NL = COLS + 2 * HL + 128
PAD = 8
SR = NR + 2 * PAD
LAST = ROWS - HR
EDGE_C = COLS - HL
BOTTOM = NR - HR

VMEM = pl.BlockSpec(memory_space=pltpu.VMEM)
F32 = jnp.float32
BF16 = jnp.bfloat16


def call(kernel, out_shapes, scratch, flops, byte_count, *operands):
    return pl.pallas_call(
        kernel,
        out_shape=out_shapes,
        in_specs=[VMEM] * len(operands),
        out_specs=[VMEM] * len(out_shapes),
        scratch_shapes=scratch,
        compiler_params=pltpu.CompilerParams(vmem_limit_bytes=40 * 1024 * 1024),
        cost_estimate=pl.CostEstimate(
            flops=flops, bytes_accessed=byte_count, transcendentals=0
        ),
    )(*operands)


def edge_starts():
    core = lax.rem(lax.axis_index("rows"), 2)
    far = pl.multiple_of(core * LAST, 8)
    near = pl.multiple_of((1 - core) * LAST, 8)
    return far, near


def table_kernel(v_ref, w_ref, rows_hi, rows_lo, cols_hi, cols_lo):
    v = jnp.broadcast_to(v_ref[0:1, :], (KW, 2 * KW))
    table = pltpu.roll(v, 0, 1, stride=1, stride_axis=0)
    hi = table.astype(BF16)
    rows_hi[...] = hi
    rows_lo[...] = (table - hi.astype(F32)).astype(BF16)
    w = jnp.broadcast_to(w_ref[0:1, :], (2 * KW, 3 * KW))
    table = pltpu.roll(w, 0, 1, stride=1, stride_axis=0)[:, :KW]
    hi = table.astype(BF16)
    cols_hi[...] = hi
    cols_lo[...] = (table - hi.astype(F32)).astype(BF16)


def tables(kern_rows, kern_cols):
    v = jnp.concatenate([jnp.zeros((1,), F32), kern_rows[::-1], jnp.zeros((KW - 1,), F32)])
    w = jnp.concatenate([jnp.zeros((2 * KW,), F32), kern_cols])
    v = jnp.broadcast_to(v[None], (8, 2 * KW))
    w = jnp.broadcast_to(w[None], (8, 3 * KW))
    shapes = [
        jax.ShapeDtypeStruct((KW, 2 * KW), BF16),
        jax.ShapeDtypeStruct((KW, 2 * KW), BF16),
        jax.ShapeDtypeStruct((2 * KW, KW), BF16),
        jax.ShapeDtypeStruct((2 * KW, KW), BF16),
    ]
    return call(table_kernel, shapes, [], 10**7, 10**6, v, w)


def pack_kernel(count, *refs):
    arrays = refs[:count]
    far_buf, near_buf, left_buf, right_buf = refs[count:]
    far, near = edge_starts()
    base = count * ROWS
    for n, ref in enumerate(arrays):
        far_buf[n * HR : (n + 1) * HR, :] = ref[pl.ds(far, HR), :]
        near_buf[n * HR : (n + 1) * HR, :] = ref[pl.ds(near, HR), :]
        left_buf[n * ROWS : (n + 1) * ROWS, :] = ref[:, 0:HL]
        right_buf[n * ROWS : (n + 1) * ROWS, :] = ref[:, EDGE_C:COLS]
        turned = ref[:, HL : HL + 128].T
        for half in range(2):
            rows = slice(base + 8 * half + 2 * n, base + 8 * half + 2 * n + 2)
            left_buf[rows, :] = turned[0:2, half * 128 : half * 128 + 128]
        turned = ref[:, EDGE_C - 128 : EDGE_C].T
        for half in range(2):
            rows = slice(base + 8 * half + 2 * n, base + 8 * half + 2 * n + 2)
            right_buf[rows, :] = turned[126:128, half * 128 : half * 128 + 128]


def pack(*arrays):
    count = len(arrays)
    shapes = [
        jax.ShapeDtypeStruct((count * HR, COLS), F32),
        jax.ShapeDtypeStruct((count * HR, COLS), F32),
        jax.ShapeDtypeStruct((count * ROWS + 16, HL), F32),
        jax.ShapeDtypeStruct((count * ROWS + 16, HL), F32),
    ]
    return call(functools.partial(pack_kernel, count), shapes, [], 10**6, 10**6, *arrays)


def corner_kernel(count, left_halo, right_halo, far_buf, near_buf):
    base = count * ROWS
    for buf, start in zip((far_buf, near_buf), edge_starts()):
        for side, halo in enumerate((left_halo, right_halo)):
            for n in range(count):
                at = (side * count + n) * HR
                buf[at : at + HR, :] = halo[pl.ds(n * ROWS + start, HR), :]
            at = 2 * count * HR + 16 * side
            buf[at : at + 16, :] = halo[base : base + 16, :]


def corners(count, left_halo, right_halo):
    shape = jax.ShapeDtypeStruct((2 * count * HR + 32, HL), F32)
    return call(
        functools.partial(corner_kernel, count), [shape, shape], [], 10**6, 10**6, left_halo, right_halo
    )


def row_pairs(count, first):
    pairs = []
    for a in range(first, count, 2):
        b = (a + 1) % count
        pairs += [(a, b), (b, a)]
    return pairs


def exchange(*arrays):
    count = len(arrays)
    far_buf, near_buf, left_buf, right_buf = pack(*arrays)
    n_rows = lax.axis_size("rows")
    n_cols = lax.axis_size("cols")
    to_right = [(c, (c + 1) % n_cols) for c in range(n_cols)]
    to_left = [(c, (c - 1) % n_cols) for c in range(n_cols)]
    far = lax.ppermute(far_buf, "rows", row_pairs(n_rows, 1))
    left = lax.ppermute(right_buf, "cols", to_right)
    right = lax.ppermute(left_buf, "cols", to_left)
    near = lax.ppermute(near_buf, "rows", row_pairs(n_rows, 0))
    far_corner, near_corner = corners(count, left, right)
    far_corner = lax.ppermute(far_corner, "rows", row_pairs(n_rows, 1))
    near_corner = lax.ppermute(near_corner, "rows", row_pairs(n_rows, 0))
    return far, near, left, right, far_corner, near_corner


def assemble(count, own, halos, extended, turn):
    far, near, left, right, far_corner, near_corner = halos
    core = lax.rem(lax.axis_index("rows"), 2)
    far_at = pl.multiple_of(PAD + core * BOTTOM, 8)
    near_at = pl.multiple_of(PAD + (1 - core) * BOTTOM, 8)
    far_from = pl.multiple_of((1 - core) * LAST, 8)
    near_from = pl.multiple_of(core * LAST, 8)
    zeros = jnp.zeros((128, ROWS), F32)
    mid = slice(PAD + HR, PAD + HR + ROWS)
    for n in range(count):
        ext = extended[n]
        ext[mid, HL : HL + COLS] = own[n][...]
        ext[mid, 0:HL] = left[n * ROWS : (n + 1) * ROWS, :]
        ext[mid, HL + COLS : 2 * HL + COLS] = right[n * ROWS : (n + 1) * ROWS, :]
        base = count * ROWS
        turn[...] = zeros
        for half in range(2):
            lanes = slice(half * 128, half * 128 + 128)
            at = base + 8 * half + 2 * n
            turn[0:2, lanes] = right[at : at + 2, :]
            turn[126:128, lanes] = left[at : at + 2, :]
        ext[mid, 2 * HL + COLS : NL] = turn[...].T
        for rows_buf, corner, at_row, from_row in (
            (far, far_corner, far_at, far_from),
            (near, near_corner, near_at, near_from),
        ):
            ext[pl.ds(at_row, HR), HL : HL + COLS] = rows_buf[n * HR : (n + 1) * HR, :]
            ext[pl.ds(at_row, HR), 0:HL] = corner[n * HR : (n + 1) * HR, :]
            right_rows = slice((count + n) * HR, (count + n + 1) * HR)
            ext[pl.ds(at_row, HR), HL + COLS : 2 * HL + COLS] = corner[right_rows, :]
            base_t = 2 * count * HR
            for half in range(2):
                lanes = slice(half * 128, half * 128 + 128)
                at = base_t + 8 * half + 2 * n
                turn[126:128, lanes] = corner[at : at + 2, :]
                turn[0:2, lanes] = corner[at + 16 : at + 18, :]
            turned = turn[...].T
            ext[pl.ds(at_row, HR), 2 * HL + COLS : NL] = jnp.where(
                core == (0 if rows_buf is far else 1), turned[LAST:ROWS, :], turned[0:HR, :]
            )


def advance_density(dens, value, out):
    shape = (8, NL)
    sub = lax.broadcasted_iota(jnp.int32, shape, 0)
    top = sub == 0
    end = sub == 7
    c = DT * NU

    def flux(a, here, there):
        a = DT * a
        return here * jnp.maximum(a + c, c) + there * jnp.minimum(a - c, -c)

    def step(i, carry):
        flux_before, m, u = carry
        r = pl.multiple_of(8 * i, 8)
        m_next = dens[pl.ds(r + 8, 8), :]
        u_next = value[pl.ds(r + 8, 8), :]
        m_down = pltpu.roll(jnp.where(top, m_next, m), 7, 0)
        u_down = pltpu.roll(jnp.where(top, u_next, u), 7, 0)
        flux_x = flux(u - u_down, m, m_down)
        flux_up = pltpu.roll(jnp.where(end, flux_before, flux_x), 1, 0)
        m_right = pltpu.roll(m, NL - 1, 1)
        u_right = pltpu.roll(u, NL - 1, 1)
        flux_y = flux(u - u_right, m, m_right)
        flux_left = pltpu.roll(flux_y, 1, 1)

        @pl.when(i > 0)
        def _():
            out[pl.ds(pl.multiple_of(r - 8, 8), 8), :] = m - (
                (flux_x - flux_up) + (flux_y - flux_left)
            )

        return flux_x, m_next, u_next

    start = (jnp.zeros(shape, F32), dens[0:8, :], value[0:8, :])
    lax.fori_loop(0, NR // 8 + 1, step, start)


def split(x):
    hi = x.astype(BF16)
    return hi, (x - hi.astype(F32)).astype(BF16)


def dot(a, b):
    return jnp.dot(a, b, preferred_element_type=F32)


def convolve(dens, rows_hi, rows_lo, cols_hi, cols_lo, mix_hi, mix_lo, out):
    for b in range((COLS + 2 * HL) // 256):
        lanes = slice(256 * b, 256 * b + 256)
        hi, lo = split(dens[HR - 128 : HR - 128 + 2 * KW, lanes])
        mixed = dot(rows_hi[...], hi) + dot(rows_hi[...], lo) + dot(rows_lo[...], hi)
        hi, lo = split(mixed)
        mix_hi[:, lanes] = hi
        mix_lo[:, lanes] = lo
    for b in range(COLS // 256):
        lanes = slice(256 * b, 256 * b + 2 * KW)
        hi = mix_hi[:, lanes]
        lo = mix_lo[:, lanes]
        out[:, 256 * b : 256 * b + 256] = (
            dot(hi, cols_hi[...]) + dot(lo, cols_hi[...]) + dot(hi, cols_lo[...])
        )


def advance_value(value, potential, cong, out):
    width = COLS + 2 * HL
    shape = (8, width)
    sub = lax.broadcasted_iota(jnp.int32, shape, 0)
    top = sub == 0
    end = sub == 7
    own = slice(HL, HL + COLS)

    def step(i, carry):
        before, u = carry
        r = pl.multiple_of(PAD + HR + 8 * i, 8)
        u_next = value[pl.ds(r + 8, 8), 0:width]
        down = pltpu.roll(jnp.where(top, u_next, u), 7, 0) - u
        up = pltpu.roll(jnp.where(end, before, down), 1, 0)
        right = pltpu.roll(u, width - 1, 1) - u
        left = pltpu.roll(right, 1, 1)
        down_o, up_o, right_o, left_o = down[:, own], up[:, own], right[:, own], left[:, own]
        grad_sq = (
            jnp.square(jnp.maximum(up_o, 0.0))
            + jnp.square(jnp.minimum(down_o, 0.0))
            + jnp.square(jnp.maximum(left_o, 0.0))
            + jnp.square(jnp.minimum(right_o, 0.0))
        )
        lap = (down_o - up_o) + (right_o - left_o)
        rows = pl.ds(pl.multiple_of(8 * i, 8), 8)
        cost = potential[rows, :] + cong[rows, :]
        out[rows, :] = u[:, own] + DT * (NU * lap - 0.5 * grad_sq + cost)
        return down, u_next

    first = PAD + HR
    u_before = value[first - 8 : first, 0:width]
    u_first = value[first : first + 8, 0:width]
    before = pltpu.roll(jnp.where(top, u_first, u_before), 7, 0) - u_before
    lax.fori_loop(0, ROWS // 8, step, (before, u_first))


def first_kernel(*refs):
    dens, value, potential = refs[:3]
    table = refs[3:7]
    halos = refs[7:13]
    dens_ext, value_out = refs[13:15]
    dens_pad, value_pad, mix_hi, mix_lo, cong, turn = refs[15:]
    assemble(2, (dens, value), halos, (dens_pad, value_pad), turn)
    advance_density(dens_pad, value_pad, dens_ext.at[PAD : PAD + NR])
    dens_ext[0:PAD, :] = jnp.zeros((PAD, NL), F32)
    dens_ext[PAD + NR : SR, :] = jnp.zeros((PAD, NL), F32)
    convolve(dens_ext.at[PAD : PAD + NR], *table, mix_hi, mix_lo, cong)
    advance_value(value_pad, potential, cong, value_out)


def second_kernel(*refs):
    dens_ext, value, potential = refs[:3]
    table = refs[3:7]
    halos = refs[7:13]
    dens_out, value_out = refs[13:15]
    dens_new, value_pad, mix_hi, mix_lo, cong, turn = refs[15:]
    assemble(1, (value,), halos, (value_pad,), turn)
    advance_density(dens_ext, value_pad, dens_new)
    dens_out[...] = dens_new[HR : HR + ROWS, HL : HL + COLS]
    convolve(dens_new, *table, mix_hi, mix_lo, cong)
    advance_value(value_pad, potential, cong, value_out)


def body(density, value_field, potential, kern_rows, kern_cols):
    block = jax.ShapeDtypeStruct((ROWS, COLS), F32)
    mix = [
        pltpu.VMEM((ROWS, COLS + 2 * HL), BF16),
        pltpu.VMEM((ROWS, COLS + 2 * HL), BF16),
        pltpu.VMEM((ROWS, COLS), F32),
        pltpu.VMEM((128, ROWS), F32),
    ]
    table = tables(kern_rows, kern_cols)
    halos = exchange(density, value_field)
    dens_ext, value = call(
        first_kernel,
        [jax.ShapeDtypeStruct((SR, NL), F32), block],
        [pltpu.VMEM((SR, NL), F32), pltpu.VMEM((SR, NL), F32)] + mix,
        2 * 10**9,
        10**7,
        density,
        value_field,
        potential,
        *table,
        *halos,
    )
    halos = exchange(value)
    return tuple(
        call(
            second_kernel,
            [block, block],
            [pltpu.VMEM((NR, NL), F32), pltpu.VMEM((SR, NL), F32)] + mix,
            2 * 10**9,
            10**7,
            dens_ext,
            value,
            potential,
            *table,
            *halos,
        )
    )


def solution(mesh):
    placed = (P("rows", "cols"), P("rows", "cols"), P("rows", "cols"), P(), P())
    return jax.shard_map(
        body,
        mesh=mesh,
        in_specs=placed,
        out_specs=(P("rows", "cols"), P("rows", "cols")),
        check_vma=False,
    )
```

time: 359 us -> 117 us (0.33); the launches traced: 351 us -> 116 us
  blocking collectives: 152 us -> 0 us
  matrix products: 65.7 us -> 0 us
  Pallas kernels: 0 us -> 43.9 us
  waiting for transfers between devices: 63.5 us -> 36 us
  other arithmetic: 15.5 us -> 0.08 us
  local copies, waits for them, and re-layouts: 18.3 us -> 5.45 us
  starting transfers between devices: 34.7 us -> 29.4 us
    all_to_all x6 -> x0, blocking collectives: 152 us -> none  [the longest x2 64.5 us: along_rows(): lax.all_to_all(blended, 'rows', split_axis=1, concat_axis=0, tiled=True)]
    dot_general x60 -> x0, matrix products: 65.7 us -> none  [contract(): return jnp.einsum(form, left, right, precision=lax.Precision.HIGHEST)]
    pallas_call x0 -> x7, Pallas kernels: none -> 43.9 us  [call(): pl.pallas_call(kernel, out_shape=out_shapes, in_specs=[VMEM] * len(operan...]
    all_to_all x2 -> x0, waiting for transfers between devices: 34.8 us -> none  [the longest x1 23.2 us: along_rows(): lax.all_to_all(field.T, 'rows', split_axis=0, concat_axis=1, tiled=True)]
    all_to_all x2 -> x0, starting transfers between devices: 18.7 us -> none  [the longest x1 14.9 us: along_rows(): lax.all_to_all(field.T, 'rows', split_axis=0, concat_axis=1, tiled=True)]
    ppermute x8 -> x12, starting transfers between devices: 16 us -> 29.4 us  [the longest x2 10 us: exchange(): near = lax.ppermute(near_buf, 'rows', row_pairs(n_rows, 0))]
    add x3 -> x0, other arithmetic: 9.23 us -> none  [the longest x2 5.63 us: density_step(): here_cell + time_step * (diffusion * laplace - (flux_down - flux_up) - (f...]
    ppermute x8 -> x12, waiting for transfers between devices: 28.7 us -> 36 us  [the longest x2 25.8 us: exchange(): left = lax.ppermute(right_buf, 'cols', to_right)]
  transfers between devices with their start and end apart: 10 -> 12, of which waited for: 9 -> 6; matrix products, arithmetic and copies ran while one was open for 2% -> 0% of each run, Pallas kernels for 0% -> 1%
where the time goes in v1:
time: 117 us; the launch traced here: 116 us
  Pallas kernels  43.9 us (38%)
  waiting for transfers between devices  36 us (31%)
  starting transfers between devices  29.4 us (25%)
  local copies, waits for them, and re-layouts  5.45 us (5%)
    pallas_call x7, Pallas kernels, call(): pl.pallas_call(kernel, out_shape=out_shapes, in_specs=[VMEM] * len(operan...  43.9 us
    ppermute x2, waiting for transfers between devices, exchange(): left = lax.ppermute(right_buf, 'cols', to_right)  25.8 us
    ppermute x2, starting transfers between devices, exchange(): near = lax.ppermute(near_buf, 'rows', row_pairs(n_rows, 0))  10 us
    ppermute x2, starting transfers between devices, exchange(): near_corner = lax.ppermute(near_corner, 'rows', row_pairs(n_rows, 0))  5.98 us
    unnamed x18, local copies, waits for them, and re-layouts  5.34 us
    ppermute x2, starting transfers between devices, exchange(): right = lax.ppermute(left_buf, 'cols', to_left)  5.26 us
    ppermute x2, waiting for transfers between devices, exchange(): right = lax.ppermute(left_buf, 'cols', to_left)  5.23 us
    ppermute x2, waiting for transfers between devices, exchange(): far_corner = lax.ppermute(far_corner, 'rows', row_pairs(n_rows, 1))  4.96 us
  transfers between devices with their start and end apart: 12, of which 6 were waited for; matrix products, arithmetic and copies ran while one was open for 0% of the time, Pallas kernels for 1%

profile of v1, /device:TPU:1, one launch (start us, length us, event | category | flops | bytes accessed | tf_op | source)
XLA Modules:
  0.0 115.5 jit_solution(14829421782902726006)
XLA Ops:
  0.6 0.0 copy-start.1
  0.6 1.2 %copy-done.1 = f32[256,1024]{1,0:T(8,128)S(1)} copy-done((f32[256,1024]{1,0:T(8,128)S(1)}, f32[256,1024]{1,0:T(8,128)}, u32[]{:S(2)}) %copy-start.1) | copy-done | bytes 1048600
  1.9 0.0 copy-start.3
  1.9 1.2 %copy-done.3 = f32[256,1024]{1,0:T(8,128)S(1)} copy-done((f32[256,1024]{1,0:T(8,128)S(1)}, f32[256,1024]{1,0:T(8,128)}, u32[]{:S(2)}) %copy-start.3) | copy-done | bytes 1048600
  3.1 0.0 copy-start.7
  3.1 0.0 copy-start.8
  3.1 0.0 copy-start
  3.1 0.0 copy-start.2
  3.1 1.6 %shard_map.69 = (f32[272,1024]{1,0:T(8,128)}, f32[272,1024]{1,0:T(8,128)}, f32[528,128]{1,0:T(8,128)S(1)}, f32[528,128]{1,0:T(8,128)S(1)}) custom-call(f32[256,1024]{1,0:T(8,128)S(1)} %copy-done.1, f32[256,1024]{1,0:T(8,128)S(1)} %copy-done.3), custom_call_target="tpu_custom_call" | custom-call | flops 1000000 | bytes 1000000 | tf_op jit(solution)/shard_map/pallas_call | solution.py:33
  4.7 3.0 %collective-permute-start = (f32[272,1024]{1,0:T(8,128)}, f32[272,1024]{1,0:T(8,128)S(1)}, u32[]{:S(2)}, u32[]{:S(2)}) collective-permute-start(f32[272,1024]{1,0:T(8,128)} %get-tuple-element.24), channel_id=1, source_target_pairs={{8,16},{16,8},{24,32},{32,24},{40,48},{48,40},{56,64},{64,56},{72,... | collective-permute-start | bytes 3342344 | tf_op jit(solution)/shard_map/ppermute | solution.py:144
  7.7 4.7 %collective-permute-start.1 = (f32[272,1024]{1,0:T(8,128)}, f32[272,1024]{1,0:T(8,128)}, u32[]{:S(2)}, u32[]{:S(2)}) collective-permute-start(f32[272,1024]{1,0:T(8,128)} %get-tuple-element.25), channel_id=1, source_target_pairs={{0,8},{8,0},{16,24},{24,16},{32,40},{40,32},{48,56},{56,48},{64,72... | collective-permute-start | bytes 3342344 | tf_op jit(solution)/shard_map/ppermute | solution.py:147
  12.4 2.5 %collective-permute-start.2 = (f32[528,128]{1,0:T(8,128)S(1)}, f32[528,128]{1,0:T(8,128)S(1)}, u32[]{:S(2)}, u32[]{:S(2)}) collective-permute-start(f32[528,128]{1,0:T(8,128)S(1)} %get-tuple-element.26), channel_id=1, source_target_pairs={{0,1},{1,2},{2,3},{3,4},{4,5},{5,6},{6,7},{7,0},{8,9},{9,10},{10,1... | collective-permute-start | bytes 811016 | tf_op jit(solution)/shard_map/ppermute | solution.py:145
  14.8 2.6 %collective-permute-start.3 = (f32[528,128]{1,0:T(8,128)S(1)}, f32[528,128]{1,0:T(8,128)S(1)}, u32[]{:S(2)}, u32[]{:S(2)}) collective-permute-start(f32[528,128]{1,0:T(8,128)S(1)} %get-tuple-element.27), channel_id=1, source_target_pairs={{0,7},{1,0},{2,1},{3,2},{4,3},{5,4},{6,5},{7,6},{8,15},{9,8},{10,9... | collective-permute-start | bytes 811016 | tf_op jit(solution)/shard_map/ppermute | solution.py:146
  17.5 17.6 %collective-permute-done.2.left_halo.refs_9_ = f32[528,128]{1,0:T(8,128)S(1)} collective-permute-done((f32[528,128]{1,0:T(8,128)S(1)}, f32[528,128]{1,0:T(8,128)S(1)}, u32[]{:S(2)}, u32[]{:S(2)}) %collective-permute-start.2) | collective-permute-done | bytes 270368 | tf_op jit(solution)/shard_map/ppermute | solution.py:145
  35.1 3.3 %collective-permute-done.3.right_halo.refs_10_ = f32[528,128]{1,0:T(8,128)S(1)} collective-permute-done((f32[528,128]{1,0:T(8,128)S(1)}, f32[528,128]{1,0:T(8,128)S(1)}, u32[]{:S(2)}, u32[]{:S(2)}) %collective-permute-start.3) | collective-permute-done | bytes 270368 | tf_op jit(solution)/shard_map/ppermute | solution.py:146
  38.5 0.8 shard_map.70
  39.3 0.7 copy-done.5
  40.0 0.0 collective-permute-start.4
  40.0 3.5 %collective-permute-start.5 = (f32[576,128]{1,0:T(8,128)}, f32[576,128]{1,0:T(8,128)}, u32[]{:S(2)}, u32[]{:S(2)}) collective-permute-start(f32[576,128]{1,0:T(8,128)} %get-tuple-element.29), channel_id=1, source_target_pairs={{0,8},{8,0},{16,24},{24,16},{32,40},{40,32},{48,56},{56,48},{64,72... | collective-permute-start | bytes 884744 | tf_op jit(solution)/shard_map/ppermute | solution.py:150
  43.5 0.0 copy-done.7
  43.5 0.1 rev.3
  43.6 0.0 copy-done.8
  43.7 0.1 pad_maximum_fusion
  43.7 0.2 shard_map.68
  44.0 2.8 %collective-permute-done.4.refs_11_ = f32[576,128]{1,0:T(8,128)} collective-permute-done((f32[576,128]{1,0:T(8,128)}, f32[576,128]{1,0:T(8,128)}, u32[]{:S(2)}, u32[]{:S(2)}) %collective-permute-start.4) | collective-permute-done | bytes 294944 | tf_op jit(solution)/shard_map/ppermute | solution.py:149
  46.8 0.0 collective-permute-done.5.refs_12_
  46.8 0.0 collective-permute-done.refs_7_
  46.8 0.0 collective-permute-done.1.refs_8_
  46.8 0.0 copy-done
  46.8 0.0 copy-done.2
  46.8 0.0 copy-start.4
  46.8 1.2 %copy-done.4 = f32[256,1024]{1,0:T(8,128)S(1)} copy-done((f32[256,1024]{1,0:T(8,128)S(1)}, f32[256,1024]{1,0:T(8,128)}, u32[]{:S(2)}) %copy-start.4) | copy-done | bytes 1048600
  48.0 1.0 copy-done.6
  49.0 20.7 %shard_map.71 = (f32[544,1408]{1,0:T(8,128)S(1)}, f32[256,1024]{1,0:T(8,128)S(1)}) custom-call(f32[256,1024]{1,0:T(8,128)S(1)} %copy-done.2, f32[256,1024]{1,0:T(8,128)S(1)} %copy-done.4, f32[256,1024]{1,0:T(8,128)S(1)} %copy-done, bf16[256,512]{1,0:T(8,128)(2,1)S(1)} %get-tuple-element.20.refs_3_, bf16[256,512]{1,0:T(8,128)(2,1)S(1)} %get-tuple-element.21.refs_4_, ...), custom_call_target="tpu_custom_call" | custom-call | flops 2000000000 | bytes 10000000 | tf_op jit(solution)/shard_map/pallas_call | solution.py:33
  69.7 0.1 shard_map.72
  69.8 0.1 collective-permute-start.6
  69.9 5.3 %collective-permute-start.7 = (f32[136,1024]{1,0:T(8,128)S(1)}, f32[136,1024]{1,0:T(8,128)S(1)}, u32[]{:S(2)}, u32[]{:S(2)}) collective-permute-start(f32[136,1024]{1,0:T(8,128)S(1)} %get-tuple-element.33), channel_id=1, source_target_pairs={{0,8},{8,0},{16,24},{24,16},{32,40},{40,32},{48,56},{56,48},{64,72... | collective-permute-start | bytes 1671176 | tf_op jit(solution)/shard_map/ppermute | solution.py:147
  75.2 2.4 %collective-permute-start.8 = (f32[272,128]{1,0:T(8,128)S(1)}, f32[272,128]{1,0:T(8,128)S(1)}, u32[]{:S(2)}, u32[]{:S(2)}) collective-permute-start(f32[272,128]{1,0:T(8,128)S(1)} %get-tuple-element.34), channel_id=1, source_target_pairs={{0,1},{1,2},{2,3},{3,4},{4,5},{5,6},{6,7},{7,0},{8,9},{9,10},{10,1... | collective-permute-start | bytes 417800 | tf_op jit(solution)/shard_map/ppermute | solution.py:145
  77.7 2.6 %collective-permute-start.9 = (f32[272,128]{1,0:T(8,128)S(1)}, f32[272,128]{1,0:T(8,128)S(1)}, u32[]{:S(2)}, u32[]{:S(2)}) collective-permute-start(f32[272,128]{1,0:T(8,128)S(1)} %get-tuple-element.35), channel_id=1, source_target_pairs={{0,7},{1,0},{2,1},{3,2},{4,3},{5,4},{6,5},{7,6},{8,15},{9,8},{10,9... | collective-permute-start | bytes 417800 | tf_op jit(solution)/shard_map/ppermute | solution.py:146
  80.3 8.1 %collective-permute-done.8.left_halo.refs_9_ = f32[272,128]{1,0:T(8,128)S(1)} collective-permute-done((f32[272,128]{1,0:T(8,128)S(1)}, f32[272,128]{1,0:T(8,128)S(1)}, u32[]{:S(2)}, u32[]{:S(2)}) %collective-permute-start.8) | collective-permute-done | bytes 139296 | tf_op jit(solution)/shard_map/ppermute | solution.py:145
  88.4 1.9 %collective-permute-done.9.right_halo.refs_10_ = f32[272,128]{1,0:T(8,128)S(1)} collective-permute-done((f32[272,128]{1,0:T(8,128)S(1)}, f32[272,128]{1,0:T(8,128)S(1)}, u32[]{:S(2)}, u32[]{:S(2)}) %collective-permute-start.9) | collective-permute-done | bytes 139296 | tf_op jit(solution)/shard_map/ppermute | solution.py:146
  90.4 0.1 collective-permute-start.10
  90.5 2.5 %collective-permute-start.11 = (f32[304,128]{1,0:T(8,128)S(1)}, f32[304,128]{1,0:T(8,128)S(1)}, u32[]{:S(2)}, u32[]{:S(2)}) collective-permute-start(f32[304,128]{1,0:T(8,128)S(1)} %get-tuple-element.37), channel_id=1, source_target_pairs={{0,8},{8,0},{16,24},{24,16},{32,40},{40,32},{48,56},{56,48},{64,72... | collective-permute-start | bytes 466952 | tf_op jit(solution)/shard_map/ppermute | solution.py:150
  92.9 2.2 %collective-permute-done.10.refs_11_ = f32[304,128]{1,0:T(8,128)S(1)} collective-permute-done((f32[304,128]{1,0:T(8,128)S(1)}, f32[304,128]{1,0:T(8,128)S(1)}, u32[]{:S(2)}, u32[]{:S(2)}) %collective-permute-start.10) | collective-permute-done | bytes 155680 | tf_op jit(solution)/shard_map/ppermute | solution.py:149
  95.1 0.0 collective-permute-done.11.refs_12_
  95.1 0.0 collective-permute-done.6.refs_7_
  95.1 0.0 collective-permute-done.7.refs_8_
  95.1 20.4 %shard_map.74 = (f32[256,1024]{1,0:T(8,128)}, f32[256,1024]{1,0:T(8,128)}) custom-call(f32[544,1408]{1,0:T(8,128)S(1)} %get-tuple-element.30.refs_0_, f32[256,1024]{1,0:T(8,128)S(1)} %get-tuple-element.31.refs_0_.refs_1_, f32[256,1024]{1,0:T(8,128)S(1)} %copy-done, bf16[256,512]{1,0:T(8,128)(2,1)S(1)} %get-tuple-element.20.refs_3_, ...), custom_call_target="tpu_custom_call" | custom-call | flops 2000000000 | bytes 10000000 | tf_op jit(solution)/shard_map/pallas_call | solution.py:33
  (7 shorter events, 0.0 us)
Async XLA Ops:
  0.6 1.2 %copy-start.1 = (f32[256,1024]{1,0:T(8,128)S(1)}, f32[256,1024]{1,0:T(8,128)}, u32[]{:S(2)}) copy-start(f32[256,1024]{1,0:T(8,128)} %refs_0_.3) | copy-start | bytes 3145732
  1.9 1.2 %copy-start.3 = (f32[256,1024]{1,0:T(8,128)S(1)}, f32[256,1024]{1,0:T(8,128)}, u32[]{:S(2)}) copy-start(f32[256,1024]{1,0:T(8,128)} %refs_1_.3) | copy-start | bytes 3145732
  3.1 40.5 %copy-start.7 = (f32[256]{0:T(256)S(1)}, f32[256]{0:T(256)}, u32[]{:S(2)}) copy-start(f32[256]{0:T(256)} %param.8) | copy-start | bytes 3076
  3.1 40.6 %copy-start.8 = (f32[256]{0:T(256)S(1)}, f32[256]{0:T(256)}, u32[]{:S(2)}) copy-start(f32[256]{0:T(256)} %param.9) | copy-start | bytes 3076
  3.1 43.7 %copy-start = (f32[256,1024]{1,0:T(8,128)S(1)}, f32[256,1024]{1,0:T(8,128)}, u32[]{:S(2)}) copy-start(f32[256,1024]{1,0:T(8,128)} %refs_2_.3) | copy-start | bytes 3145732
  3.1 43.7 %copy-start.2 = (f32[256,1024]{1,0:T(8,128)S(1)}, f32[256,1024]{1,0:T(8,128)}, u32[]{:S(2)}) copy-start(f32[256,1024]{1,0:T(8,128)} %refs_0_.3) | copy-start | bytes 3145732
  4.7 42.1 %collective-permute-start = (f32[272,1024]{1,0:T(8,128)}, f32[272,1024]{1,0:T(8,128)S(1)}, u32[]{:S(2)}, u32[]{:S(2)}) collective-permute-start(f32[272,1024]{1,0:T(8,128)} %get-tuple-element.24), channel_id=1, source_target_pairs={{8,16},{16,8},{24,32},{32,24},{40,48},{48,40},{56,64},{64,56},{72,... | collective-permute-start | bytes 3342344 | tf_op jit(solution)/shard_map/ppermute | solution.py:144
  7.7 39.1 %collective-permute-start.1 = (f32[272,1024]{1,0:T(8,128)}, f32[272,1024]{1,0:T(8,128)}, u32[]{:S(2)}, u32[]{:S(2)}) collective-permute-start(f32[272,1024]{1,0:T(8,128)} %get-tuple-element.25), channel_id=1, source_target_pairs={{0,8},{8,0},{16,24},{24,16},{32,40},{40,32},{48,56},{56,48},{64,72... | collective-permute-start | bytes 3342344 | tf_op jit(solution)/shard_map/ppermute | solution.py:147
  12.4 22.7 %collective-permute-start.2 = (f32[528,128]{1,0:T(8,128)S(1)}, f32[528,128]{1,0:T(8,128)S(1)}, u32[]{:S(2)}, u32[]{:S(2)}) collective-permute-start(f32[528,128]{1,0:T(8,128)S(1)} %get-tuple-element.26), channel_id=1, source_target_pairs={{0,1},{1,2},{2,3},{3,4},{4,5},{5,6},{6,7},{7,0},{8,9},{9,10},{10,1... | collective-permute-start | bytes 811016 | tf_op jit(solution)/shard_map/ppermute | solution.py:145
  14.8 23.6 %collective-permute-start.3 = (f32[528,128]{1,0:T(8,128)S(1)}, f32[528,128]{1,0:T(8,128)S(1)}, u32[]{:S(2)}, u32[]{:S(2)}) collective-permute-start(f32[528,128]{1,0:T(8,128)S(1)} %get-tuple-element.27), channel_id=1, source_target_pairs={{0,7},{1,0},{2,1},{3,2},{4,3},{5,4},{6,5},{7,6},{8,15},{9,8},{10,9... | collective-permute-start | bytes 811016 | tf_op jit(solution)/shard_map/ppermute | solution.py:146
  39.3 0.7 copy-start.5
  40.0 6.8 %collective-permute-start.4 = (f32[576,128]{1,0:T(8,128)}, f32[576,128]{1,0:T(8,128)}, u32[]{:S(2)}, u32[]{:S(2)}) collective-permute-start(f32[576,128]{1,0:T(8,128)} %get-tuple-element.28), channel_id=1, source_target_pairs={{8,16},{16,8},{24,32},{32,24},{40,48},{48,40},{56,64},{64,56},{72,... | collective-permute-start | bytes 884744 | tf_op jit(solution)/shard_map/ppermute | solution.py:149
  40.0 6.8 %collective-permute-start.5 = (f32[576,128]{1,0:T(8,128)}, f32[576,128]{1,0:T(8,128)}, u32[]{:S(2)}, u32[]{:S(2)}) collective-permute-start(f32[576,128]{1,0:T(8,128)} %get-tuple-element.29), channel_id=1, source_target_pairs={{0,8},{8,0},{16,24},{24,16},{32,40},{40,32},{48,56},{56,48},{64,72... | collective-permute-start | bytes 884744 | tf_op jit(solution)/shard_map/ppermute | solution.py:150
  46.8 1.2 %copy-start.4 = (f32[256,1024]{1,0:T(8,128)S(1)}, f32[256,1024]{1,0:T(8,128)}, u32[]{:S(2)}) copy-start(f32[256,1024]{1,0:T(8,128)} %refs_1_.3) | copy-start | bytes 3145732
  48.0 1.0 copy-start.6
  69.8 25.3 %collective-permute-start.6 = (f32[136,1024]{1,0:T(8,128)S(1)}, f32[136,1024]{1,0:T(8,128)S(1)}, u32[]{:S(2)}, u32[]{:S(2)}) collective-permute-start(f32[136,1024]{1,0:T(8,128)S(1)} %get-tuple-element.32), channel_id=1, source_target_pairs={{8,16},{16,8},{24,32},{32,24},{40,48},{48,40},{56,64},{64,56},{72,... | collective-permute-start | bytes 1671176 | tf_op jit(solution)/shard_map/ppermute | solution.py:144
  69.9 25.2 %collective-permute-start.7 = (f32[136,1024]{1,0:T(8,128)S(1)}, f32[136,1024]{1,0:T(8,128)S(1)}, u32[]{:S(2)}, u32[]{:S(2)}) collective-permute-start(f32[136,1024]{1,0:T(8,128)S(1)} %get-tuple-element.33), channel_id=1, source_target_pairs={{0,8},{8,0},{16,24},{24,16},{32,40},{40,32},{48,56},{56,48},{64,72... | collective-permute-start | bytes 1671176 | tf_op jit(solution)/shard_map/ppermute | solution.py:147
  75.2 13.2 %collective-permute-start.8 = (f32[272,128]{1,0:T(8,128)S(1)}, f32[272,128]{1,0:T(8,128)S(1)}, u32[]{:S(2)}, u32[]{:S(2)}) collective-permute-start(f32[272,128]{1,0:T(8,128)S(1)} %get-tuple-element.34), channel_id=1, source_target_pairs={{0,1},{1,2},{2,3},{3,4},{4,5},{5,6},{6,7},{7,0},{8,9},{9,10},{10,1... | collective-permute-start | bytes 417800 | tf_op jit(solution)/shard_map/ppermute | solution.py:145
  77.7 12.7 %collective-permute-start.9 = (f32[272,128]{1,0:T(8,128)S(1)}, f32[272,128]{1,0:T(8,128)S(1)}, u32[]{:S(2)}, u32[]{:S(2)}) collective-permute-start(f32[272,128]{1,0:T(8,128)S(1)} %get-tuple-element.35), channel_id=1, source_target_pairs={{0,7},{1,0},{2,1},{3,2},{4,3},{5,4},{6,5},{7,6},{8,15},{9,8},{10,9... | collective-permute-start | bytes 417800 | tf_op jit(solution)/shard_map/ppermute | solution.py:146
  90.4 4.7 %collective-permute-start.10 = (f32[304,128]{1,0:T(8,128)S(1)}, f32[304,128]{1,0:T(8,128)S(1)}, u32[]{:S(2)}, u32[]{:S(2)}) collective-permute-start(f32[304,128]{1,0:T(8,128)S(1)} %get-tuple-element.36), channel_id=1, source_target_pairs={{8,16},{16,8},{24,32},{32,24},{40,48},{48,40},{56,64},{64,56},{72,... | collective-permute-start | bytes 466952 | tf_op jit(solution)/shard_map/ppermute | solution.py:149
  90.5 4.6 %collective-permute-start.11 = (f32[304,128]{1,0:T(8,128)S(1)}, f32[304,128]{1,0:T(8,128)S(1)}, u32[]{:S(2)}, u32[]{:S(2)}) collective-permute-start(f32[304,128]{1,0:T(8,128)S(1)} %get-tuple-element.37), channel_id=1, source_target_pairs={{0,8},{8,0},{16,24},{24,16},{32,40},{40,32},{48,56},{56,48},{64,72... | collective-permute-start | bytes 466952 | tf_op jit(solution)/shard_map/ppermute | solution.py:150

commit v2 on v0

v2 whole, which is shorter than its diff:
```python
import functools

import jax
import jax.numpy as jnp
from jax import lax
from jax.experimental import pallas as pl
from jax.experimental.pallas import tpu as pltpu
from jax.sharding import PartitionSpec as P

STEPS = 2
NU = 0.5
DT = 0.1

ROWS = 256
COLS = 1024
KW = 256
HALF = KW // 2
EDGE = 128
MID = COLS - 2 * EDGE
FROM_R = COLS - EDGE
RAW_AT = HALF
TURNED_AT = RAW_AT + 16
FIRST_ROWS = TURNED_AT + 8
TALL = 3 * ROWS
SEGMENTS = TALL // EDGE
COL_ROWS = ROWS + 4 * SEGMENTS

VMEM = pl.BlockSpec(memory_space=pltpu.VMEM)
F32 = jnp.float32
BF16 = jnp.bfloat16


def shape(*dims, kind=F32):
    return jax.ShapeDtypeStruct(dims, kind)


def call(kernel, out_shapes, scratch, micros, *operands):
    return pl.pallas_call(
        kernel,
        out_shape=out_shapes,
        in_specs=[VMEM] * len(operands),
        out_specs=[VMEM] * len(out_shapes),
        scratch_shapes=scratch,
        compiler_params=pltpu.CompilerParams(vmem_limit_bytes=32 * 1024 * 1024),
        cost_estimate=pl.CostEstimate(
            flops=int(micros * 10**9), bytes_accessed=int(micros * 3 * 10**6), transcendentals=0
        ),
    )(*operands)


def core_index():
    return lax.rem(lax.axis_index("rows"), 2)


def split(x):
    hi = x.astype(BF16)
    return hi, (x - hi.astype(F32)).astype(BF16)


def product(left, right):
    dot = functools.partial(jnp.dot, preferred_element_type=F32)
    return dot(left[0], right[0]) + (dot(left[1], right[0]) + dot(left[0], right[1]))


def put_split(refs, x):
    refs[0][...], refs[1][...] = split(x)


def table_kernel(v_ref, w_ref, rows_hi, rows_lo, turned_hi, turned_lo, cols_hi, cols_lo):
    v = jnp.broadcast_to(v_ref[0:1, :], (KW, 2 * KW))
    put_split((rows_hi, rows_lo), pltpu.roll(v, 0, 1, stride=1, stride_axis=0))
    for n, refs in enumerate(((turned_hi, turned_lo), (cols_hi, cols_lo))):
        w = jnp.broadcast_to(w_ref[n : n + 1, :], (2 * KW, 3 * KW))
        put_split(refs, pltpu.roll(w, 0, 1, stride=1, stride_axis=0)[:, :KW])


def tables(kern_rows, kern_cols):
    v = jnp.concatenate([jnp.zeros((1,), F32), kern_rows[::-1], jnp.zeros((KW - 1,), F32)])
    w = jnp.pad(jnp.stack([kern_rows, kern_cols]), ((0, 6), (2 * KW, 0)))
    v = jnp.broadcast_to(v[None], (8, 2 * KW))
    shapes = [shape(KW, 2 * KW, kind=BF16)] * 2 + [shape(2 * KW, KW, kind=BF16)] * 4
    out = call(table_kernel, shapes, [], 0.3, v, w)
    return out[0:2], out[2:4], out[4:6]


def flux(a, here, there):
    c = DT * NU
    a = DT * a
    return here * jnp.maximum(a + c, c) + there * jnp.minimum(a - c, -c)


def eight_rows(m, u):
    width = m.shape[1]
    flux_x = flux(u - pltpu.roll(u, 7, 0), m, pltpu.roll(m, 7, 0))
    flux_y = flux(u - pltpu.roll(u, width - 1, 1), m, pltpu.roll(m, width - 1, 1))
    return m - ((flux_x - pltpu.roll(flux_x, 1, 0)) + (flux_y - pltpu.roll(flux_y, 1, 1)))


def inner_density(dens, value, out):
    dims = (8, COLS)
    sub = lax.broadcasted_iota(jnp.int32, dims, 0)
    top = sub == 0
    end = sub == 7

    def step(i, flux_before):
        rows = pl.ds(pl.multiple_of(8 * i, 8), 8)
        after = pl.ds(pl.multiple_of(jnp.minimum(8 * i + 8, ROWS - 8), 8), 8)
        m = dens[rows, :]
        u = value[rows, :]
        m_down = pltpu.roll(jnp.where(top, dens[after, :], m), 7, 0)
        u_down = pltpu.roll(jnp.where(top, value[after, :], u), 7, 0)
        flux_x = flux(u - u_down, m, m_down)
        flux_up = pltpu.roll(jnp.where(end, flux_before, flux_x), 1, 0)
        flux_y = flux(u - pltpu.roll(u, COLS - 1, 1), m, pltpu.roll(m, COLS - 1, 1))
        out[rows, :] = m - ((flux_x - flux_up) + (flux_y - pltpu.roll(flux_y, 1, 1)))
        return flux_x

    lax.fori_loop(0, ROWS // 8, step, jnp.zeros(dims, F32), unroll=4)


def inner_value(value, potential, around, out):
    dims = (8, COLS)
    sub = lax.broadcasted_iota(jnp.int32, dims, 0)
    top = sub == 0
    end = sub == 7
    below = jnp.broadcast_to(around[6:7, :], dims)
    above = jnp.broadcast_to(around[1:2, :], dims)
    first = value[0:8, :] - above

    def step(i, before):
        rows = pl.ds(pl.multiple_of(8 * i, 8), 8)
        after = pl.ds(pl.multiple_of(jnp.minimum(8 * i + 8, ROWS - 8), 8), 8)
        u = value[rows, :]
        u_next = jnp.where(i == ROWS // 8 - 1, below, value[after, :])
        down = pltpu.roll(jnp.where(top, u_next, u), 7, 0) - u
        up = pltpu.roll(jnp.where(end, before, down), 1, 0)
        right = pltpu.roll(u, COLS - 1, 1) - u
        left = pltpu.roll(right, 1, 1)
        out[rows, :] = value_formula(u, down, up, right, left, potential[rows, :])
        return down

    start = jnp.broadcast_to(first[0:1, :], dims)
    lax.fori_loop(0, ROWS // 8, step, start, unroll=4)


def value_formula(u, down, up, right, left, cost):
    grad_sq = (
        jnp.square(jnp.maximum(up, 0.0))
        + jnp.square(jnp.minimum(down, 0.0))
        + jnp.square(jnp.maximum(left, 0.0))
        + jnp.square(jnp.minimum(right, 0.0))
    )
    lap = (down - up) + (right - left)
    return u + DT * (NU * lap - 0.5 * grad_sq + cost)


def prepare(dens, value, new, own_t, far_1, near_1, far_2, near_2):
    core = core_index()
    inner_density(dens, value, new)
    own_t[0:2, :] = dens[:, 0:EDGE].T[0:2, :]
    own_t[2:4, :] = dens[:, FROM_R:COLS].T[EDGE - 2 : EDGE, :]
    own_t[4:6, :] = value[:, 0:EDGE].T[0:2, :]
    own_t[6:8, :] = value[:, FROM_R:COLS].T[EDGE - 2 : EDGE, :]
    for one, two, bottom in ((far_1, far_2, core), (near_1, near_2, 1 - core)):
        rows = pl.ds(pl.multiple_of(bottom * HALF, 8), HALF)
        one[0:HALF, 0:EDGE] = new[rows, 0:EDGE]
        one[0:HALF, EDGE : 2 * EDGE] = new[rows, FROM_R:COLS]
        two[...] = new[rows, EDGE:FROM_R]
        tile = pl.ds(pl.multiple_of(bottom * (ROWS - 8), 8), 8)
        for n, ref in enumerate((dens, value)):
            eight = ref[tile, :]
            pair = jnp.where(bottom == 1, eight[6:8, :], eight[0:2, :])
            for q in range(COLS // 256):
                at = RAW_AT + 4 * q + 2 * n
                one[at : at + 2, :] = pair[:, 256 * q : 256 * q + 256]
        one[TURNED_AT:FIRST_ROWS, :] = own_t[...]


MESSAGES = [
    shape(ROWS, COLS),
    shape(8, ROWS),
    shape(FIRST_ROWS, 2 * EDGE),
    shape(FIRST_ROWS, 2 * EDGE),
    shape(HALF, MID),
    shape(HALF, MID),
]


def halo_rows(ext, far, near):
    core = core_index()
    ext[pl.ds(pl.multiple_of(core * (HALF + ROWS), 8), HALF), :] = far
    ext[pl.ds(pl.multiple_of((1 - core) * (HALF + ROWS), 8), HALF), :] = near


def edge_kernel(
    dens, value, new, own_t, far, near, rows_hi, rows_lo,
    to_left, to_right, seams, around, tall, mixed, dens_8, ext,
):
    core = core_index()
    for ref, own, n in ((dens_8, dens, 0), (around, value, 1)):
        for q in range(COLS // 256):
            lanes = slice(256 * q, 256 * q + 256)
            at = RAW_AT + 4 * q + 2 * n
            f = far[at : at + 2, :]
            g = near[at : at + 2, :]
            ref[0:2, lanes] = jnp.where(core == 0, f, g)
            ref[6:8, lanes] = jnp.where(core == 0, g, f)
        ref[2:4, :] = own[0:2, :]
        ref[4:6, :] = own[ROWS - 2 : ROWS, :]
    seam = eight_rows(dens_8[...], around[...])
    seams[...] = seam
    f = far[TURNED_AT:FIRST_ROWS, :]
    g = near[TURNED_AT:FIRST_ROWS, :]
    tall[:, 0:ROWS] = jnp.where(core == 0, f, g)
    tall[:, ROWS : 2 * ROWS] = own_t[...]
    tall[:, 2 * ROWS : TALL] = jnp.where(core == 0, g, f)

    halo_rows(ext, far[0:HALF, :], near[0:HALF, :])
    ext[HALF : HALF + ROWS, 0:EDGE] = new[:, 0:EDGE]
    ext[HALF : HALF + ROWS, EDGE : 2 * EDGE] = new[:, FROM_R:COLS]
    put_seams(ext, seams, ((slice(0, EDGE), slice(0, EDGE)), (slice(EDGE, 2 * EDGE), slice(FROM_R, COLS))))
    result = product((rows_hi[...], rows_lo[...]), split(ext[...]))
    mixed[...] = result
    for ref, lanes, at in ((to_left, slice(0, EDGE), 0), (to_right, slice(EDGE, 2 * EDGE), 2)):
        ref[0:ROWS, :] = result[:, lanes]
        for q in range(SEGMENTS):
            segment = slice(EDGE * q, EDGE * q + EDGE)
            ref[ROWS + 4 * q : ROWS + 4 * q + 2, :] = tall[at : at + 2, segment]
            ref[ROWS + 4 * q + 2 : ROWS + 4 * q + 4, :] = tall[at + 4 : at + 6, segment]


def put_seams(ext, seams, lane_pairs):
    for to, source in lane_pairs:
        ext[HALF - 1 : HALF, to] = seams[1:2, source]
        ext[HALF : HALF + 1, to] = seams[2:3, source]
        ext[HALF + ROWS - 1 : HALF + ROWS, to] = seams[5:6, source]
        ext[HALF + ROWS : HALF + ROWS + 1, to] = seams[6:7, source]


def middle_kernel(
    new, value, potential, seams, around, far, near, rows_hi, rows_lo, cols_hi, cols_lo,
    cong, inner, ext, mix_hi, mix_lo,
):
    halo_rows(ext, far[...], near[...])
    ext[HALF : HALF + ROWS, :] = new[:, EDGE:FROM_R]
    put_seams(ext, seams, ((slice(0, MID), slice(EDGE, FROM_R)),))
    rows = (rows_hi[...], rows_lo[...])
    for b in range(MID // 256):
        lanes = slice(256 * b, 256 * b + 256)
        mix_hi[:, lanes], mix_lo[:, lanes] = split(product(rows, split(ext[:, lanes])))
    before = (cols_hi[0:KW, :], cols_lo[0:KW, :])
    after = (cols_hi[KW : 2 * KW, :], cols_lo[KW : 2 * KW, :])
    for b in range(COLS // 256):
        total = None
        for block, table in ((b - 1, before), (b, after)):
            if 0 <= block < MID // 256:
                lanes = slice(256 * block, 256 * block + 256)
                part = product((mix_hi[:, lanes], mix_lo[:, lanes]), table)
                total = part if total is None else total + part
        cong[:, 256 * b : 256 * b + 256] = total
    inner_value(value, potential, around, inner)


def finish(
    potential, new, seams, tall, left, right, mixed, cong, inner, turned_table, cols_hi, cols_lo,
    dens_out, value_out, dens_t, value_t, turn,
):
    for ref, n in ((dens_t, 0), (value_t, 1)):
        for q in range(SEGMENTS):
            lanes = slice(EDGE * q, EDGE * q + EDGE)
            at = ROWS + 4 * q + 2 * n
            ref[0:2, lanes] = left[at : at + 2, :]
            ref[6:8, lanes] = right[at : at + 2, :]
        ref[2:6, :] = tall[4 * n : 4 * n + 4, :]
    u = value_t[...]
    new_t = eight_rows(dens_t[...], u)
    window = new_t[:, HALF : HALF + 2 * KW]
    window = jnp.concatenate([window, window], axis=0)
    turn[0:8, :] = product(split(window), (turned_table[0][...], turned_table[1][...]))[0:8, :]
    own = slice(ROWS, 2 * ROWS)
    turn[8:16, :] = new_t[:, own]
    right_t = pltpu.roll(u, 7, 0) - u
    left_t = u - pltpu.roll(u, 1, 0)
    down_t = pltpu.roll(u, TALL - 1, 1) - u
    up_t = u - pltpu.roll(u, 1, 1)
    turn[24:26, :] = potential[:, 0:EDGE].T[0:2, :]
    turn[26:28, :] = potential[:, FROM_R:COLS].T[EDGE - 2 : EDGE, :]
    cost_t = jnp.concatenate([turn[24:26, :], turn[24:28, :], turn[26:28, :]], axis=0)
    turn[16:24, :] = value_formula(
        u[:, own], down_t[:, own], up_t[:, own], right_t[:, own], left_t[:, own], cost_t
    )
    columns = turn[...].T

    def column(n):
        return columns[:, n : n + 1]

    lane = lax.broadcasted_iota(jnp.int32, (ROWS, 2 * EDGE), 1)
    before = (cols_hi[0:KW, :], cols_lo[0:KW, :])
    after = (cols_hi[KW : 2 * KW, :], cols_lo[KW : 2 * KW, :])
    low = jnp.concatenate([left[0:ROWS, :], mixed[:, 0:EDGE]], axis=1)
    low = jnp.where(lane == EDGE - 1, column(1), jnp.where(lane == EDGE, column(2), low))
    low = cong[:, 0:256] + product(split(low), before)
    high = jnp.concatenate([mixed[:, EDGE : 2 * EDGE], right[0:ROWS, :]], axis=1)
    high = jnp.where(lane == EDGE - 1, column(5), jnp.where(lane == EDGE, column(6), high))
    high = cong[:, COLS - 256 : COLS] + product(split(high), after)

    lane = lax.broadcasted_iota(jnp.int32, (ROWS, EDGE), 1)
    inside = slice(256, COLS - 256)
    value_out[:, inside] = inner[:, inside] + DT * cong[:, inside]
    value_out[:, EDGE:256] = inner[:, EDGE:256] + DT * low[:, EDGE:256]
    value_out[:, COLS - 256 : FROM_R] = inner[:, COLS - 256 : FROM_R] + DT * high[:, 0:EDGE]
    value_out[:, 0:EDGE] = jnp.where(lane == 0, column(18), inner[:, 0:EDGE]) + DT * low[:, 0:EDGE]
    value_out[:, FROM_R:COLS] = (
        jnp.where(lane == EDGE - 1, column(21), inner[:, FROM_R:COLS]) + DT * high[:, EDGE:256]
    )
    dens_out[:, EDGE:FROM_R] = new[:, EDGE:FROM_R]
    dens_out[0:1, EDGE:FROM_R] = seams[2:3, EDGE:FROM_R]
    dens_out[ROWS - 1 : ROWS, EDGE:FROM_R] = seams[5:6, EDGE:FROM_R]
    row = lax.broadcasted_iota(jnp.int32, (ROWS, EDGE), 0)
    for lanes, at, n in ((slice(0, EDGE), 0, 10), (slice(FROM_R, COLS), EDGE - 1, 13)):
        block = jnp.where(row == 0, seams[2:3, lanes], new[:, lanes])
        block = jnp.where(row == ROWS - 1, seams[5:6, lanes], block)
        dens_out[:, lanes] = jnp.where(lane == at, column(n), block)


FINISH_SCRATCH = [
    pltpu.VMEM((8, TALL), F32),
    pltpu.VMEM((8, TALL), F32),
    pltpu.VMEM((128, ROWS), F32),
]


def finish_kernel(*refs):
    finish(*refs[:9], refs[9:11], *refs[11:])


def finish_prepare_kernel(*refs):
    outs = refs[13:21]
    finish(*refs[:9], refs[9:11], *refs[11:13], *outs[:2], *refs[21:])
    prepare(*outs)


def row_pairs(count, first):
    pairs = []
    for a in range(first, count, 2):
        b = (a + 1) % count
        pairs += [(a, b), (b, a)]
    return pairs


def body(density, value_field, potential, kern_rows, kern_cols):
    n_rows = lax.axis_size("rows")
    n_cols = lax.axis_size("cols")
    far_pairs = row_pairs(n_rows, 1)
    near_pairs = row_pairs(n_rows, 0)
    to_right = [(c, (c + 1) % n_cols) for c in range(n_cols)]
    to_left = [(c, (c - 1) % n_cols) for c in range(n_cols)]
    block = shape(ROWS, COLS)
    rows_table, turned_table, cols_table = tables(kern_rows, kern_cols)
    dens, value = density, value_field
    messages = call(prepare, MESSAGES, [], 2, dens, value)
    for step_index in range(STEPS):
        new, own_t, far_1, near_1, far_2, near_2 = messages
        far_1 = lax.ppermute(far_1, "rows", far_pairs)
        near_1 = lax.ppermute(near_1, "rows", near_pairs)
        far_2 = lax.ppermute(far_2, "rows", far_pairs)
        near_2 = lax.ppermute(near_2, "rows", near_pairs)
        left, right, seams, around, tall, mixed = call(
            edge_kernel,
            [shape(COL_ROWS, EDGE), shape(COL_ROWS, EDGE), shape(8, COLS), shape(8, COLS), shape(8, TALL), shape(ROWS, 2 * EDGE)],
            [pltpu.VMEM((8, COLS), F32), pltpu.VMEM((2 * KW, 2 * EDGE), F32)],
            1,
            dens, value, new, own_t, far_1, near_1, *rows_table,
        )
        right_in = lax.ppermute(left, "cols", to_left)
        left_in = lax.ppermute(right, "cols", to_right)
        cong, inner = call(
            middle_kernel,
            [block, block],
            [pltpu.VMEM((2 * KW, MID), F32), pltpu.VMEM((ROWS, MID), BF16), pltpu.VMEM((ROWS, MID), BF16)],
            3,
            new, value, potential, seams, around, far_2, near_2, *rows_table, *cols_table,
        )
        operands = (potential, new, seams, tall, left_in, right_in, mixed, cong, inner, *turned_table, *cols_table)
        if step_index < STEPS - 1:
            dens, value, *messages = call(
                finish_prepare_kernel, [block, block] + MESSAGES, FINISH_SCRATCH, 4, *operands
            )
        else:
            dens, value = call(finish_kernel, [block, block], FINISH_SCRATCH, 2, *operands)
    return dens, value


def solution(mesh):
    placed = (P("rows", "cols"), P("rows", "cols"), P("rows", "cols"), P(), P())
    return jax.shard_map(
        body,
        mesh=mesh,
        in_specs=placed,
        out_specs=(P("rows", "cols"), P("rows", "cols")),
        check_vma=False,
    )
```

time: 359 us -> 57.2 us (0.16)
  the two profiles are of different devices: /device:TPU:1 before, /device:TPU:8 now
where the time goes in v2:
time: 57.2 us; the launch traced here: 57 us
  starting transfers between devices  21.2 us (37%)
  Pallas kernels  17.4 us (30%)
  waiting for transfers between devices  15 us (26%)
  local copies, waits for them, and re-layouts  2.57 us (4%)
  between operations  0.73 us (1%)
    pallas_call x8, Pallas kernels, call(): pl.pallas_call(kernel, out_shape=out_shapes, in_specs=[VMEM] * len(operan...  17.4 us
    ppermute x2, waiting for transfers between devices, body(): far_1 = lax.ppermute(far_1, 'rows', far_pairs)  12.3 us
    ppermute x2, starting transfers between devices, body(): far_2 = lax.ppermute(far_2, 'rows', far_pairs)  10.6 us
    ppermute x2, starting transfers between devices, body(): left_in = lax.ppermute(right, 'cols', to_right)  5.62 us
    ppermute x2, starting transfers between devices, body(): right_in = lax.ppermute(left, 'cols', to_left)  3.4 us
    unnamed x14, local copies, waits for them, and re-layouts  2.47 us
    ppermute x2, waiting for transfers between devices, body(): right_in = lax.ppermute(left, 'cols', to_left)  2.46 us
    ppermute x2, starting transfers between devices, body(): far_1 = lax.ppermute(far_1, 'rows', far_pairs)  1.32 us
  transfers between devices with their start and end apart: 12, of which 5 were waited for; matrix products, arithmetic and copies ran while one was open for 0% of the time, Pallas kernels for 16%

profile of v2, /device:TPU:8, one launch (start us, length us, event | category | flops | bytes accessed | tf_op | source)
XLA Modules:
  0.0 57.0 jit_solution(1881403108021432910)
XLA Ops:
  0.6 0.0 copy-start
  0.6 1.2 %copy-done = f32[256,1024]{1,0:T(8,128)S(1)} copy-done((f32[256,1024]{1,0:T(8,128)S(1)}, f32[256,1024]{1,0:T(8,128)}, u32[]{:S(2)}) %copy-start) | copy-done | bytes 1048600
  1.9 0.0 copy-start.2
  1.9 1.2 %copy-done.2 = f32[256,1024]{1,0:T(8,128)S(1)} copy-done((f32[256,1024]{1,0:T(8,128)S(1)}, f32[256,1024]{1,0:T(8,128)}, u32[]{:S(2)}) %copy-start.2) | copy-done | bytes 1048600
  3.1 0.0 copy-start.5
  3.1 0.0 copy-start.6
  3.1 0.0 copy-start.3
  3.1 2.9 %shard_map.68 = (f32[256,1024]{1,0:T(8,128)S(1)}, f32[8,256]{1,0:T(8,128)S(1)}, f32[152,256]{1,0:T(8,128)}, f32[152,256]{1,0:T(8,128)}, f32[128,768]{1,0:T(8,128)}, /*index=5*/f32[128,768]{1,0:T(8,128)}) custom-call(f32[256,1024]{1,0:T(8,128)S(1)} %copy-done, f32[256,1024]{1,0:T(8,128)S(1)} %copy-done.2), custom_call_target="tpu_custom_call" | custom-call | flops 2000000000 | bytes 6000000 | tf_op jit(solution)/shard_map/pallas_call | solution.py:38
  6.0 0.0 copy-start.1
  6.0 6.2 %collective-permute-start.4 = (f32[128,768]{1,0:T(8,128)}, f32[128,768]{1,0:T(8,128)}, u32[]{:S(2)}, u32[]{:S(2)}) collective-permute-start(f32[128,768]{1,0:T(8,128)} %get-tuple-element.50), channel_id=1, source_target_pairs={{8,16},{16,8},{24,32},{32,24},{40,48},{48,40},{56,64},{64,56},{72,... | collective-permute-start | bytes 1179656 | tf_op jit(solution)/shard_map/ppermute | solution.py:366
  12.3 0.0 collective-permute-start.5
  12.3 1.1 %collective-permute-start = (f32[152,256]{1,0:T(8,128)}, f32[152,256]{1,0:T(8,128)S(1)}, u32[]{:S(2)}, u32[]{:S(2)}) collective-permute-start(f32[152,256]{1,0:T(8,128)} %get-tuple-element.40), channel_id=1, source_target_pairs={{8,16},{16,8},{24,32},{32,24},{40,48},{48,40},{56,64},{64,56},{72,... | collective-permute-start | bytes 466952 | tf_op jit(solution)/shard_map/ppermute | solution.py:364
  13.4 0.0 collective-permute-start.1
  13.4 0.0 copy-done.5
  13.4 0.1 rev.3
  13.5 0.1 pad_maximum_fusion
  13.6 0.0 copy-done.6
  13.6 0.3 shard_map.69
  13.9 5.7 %collective-permute-done.far = f32[152,256]{1,0:T(8,128)S(1)} collective-permute-done((f32[152,256]{1,0:T(8,128)}, f32[152,256]{1,0:T(8,128)S(1)}, u32[]{:S(2)}, u32[]{:S(2)}) %collective-permute-start) | collective-permute-done | bytes 155680 | tf_op jit(solution)/shard_map/ppermute | solution.py:364
  19.6 0.0 collective-permute-done.1.near
  19.6 0.0 copy-done.3
  19.6 0.0 copy-done.1
  19.6 0.0 copy-start.4
  19.6 0.6 shard_map.70
  20.2 2.8 %collective-permute-start.2 = (f32[280,128]{1,0:T(8,128)S(1)}, f32[280,128]{1,0:T(8,128)S(1)}, u32[]{:S(2)}, u32[]{:S(2)}) collective-permute-start(f32[280,128]{1,0:T(8,128)S(1)} %get-tuple-element.46), channel_id=1, source_target_pairs={{0,1},{1,2},{2,3},{3,4},{4,5},{5,6},{6,7},{7,0},{8,9},{9,10},{10,1... | collective-permute-start | bytes 430088 | tf_op jit(solution)/shard_map/ppermute | solution.py:376
  23.0 1.7 %collective-permute-start.3 = (f32[280,128]{1,0:T(8,128)S(1)}, f32[280,128]{1,0:T(8,128)S(1)}, u32[]{:S(2)}, u32[]{:S(2)}) collective-permute-start(f32[280,128]{1,0:T(8,128)S(1)} %get-tuple-element.47), channel_id=1, source_target_pairs={{0,7},{1,0},{2,1},{3,2},{4,3},{5,4},{6,5},{7,6},{8,15},{9,8},{10,9... | collective-permute-start | bytes 430088 | tf_op jit(solution)/shard_map/ppermute | solution.py:375
  24.7 0.0 collective-permute-done.4.far
  24.7 0.0 collective-permute-done.5.near
  24.7 0.0 copy-done.4
  24.7 4.3 %shard_map.71 = (f32[256,1024]{1,0:T(8,128)S(1)}, f32[256,1024]{1,0:T(8,128)S(1)}) custom-call(f32[256,1024]{1,0:T(8,128)S(1)} %get-tuple-element.38.new.refs_1_, f32[256,1024]{1,0:T(8,128)S(1)} %copy-done.3, f32[256,1024]{1,0:T(8,128)S(1)} %copy-done.4, f32[8,1024]{1,0:T(8,128)S(1)} %get-tuple-element.44.seams.refs_2_, ...), custom_call_target="tpu_custom_call" | custom-call | flops 3000000000 | bytes 9000000 | tf_op jit(solution)/shard_map/pallas_call | solution.py:38
  29.1 0.0 collective-permute-done.2.refs_4_
  29.1 0.9 %collective-permute-done.3.refs_5_ = f32[280,128]{1,0:T(8,128)S(1)} collective-permute-done((f32[280,128]{1,0:T(8,128)S(1)}, f32[280,128]{1,0:T(8,128)S(1)}, u32[]{:S(2)}, u32[]{:S(2)}) %collective-permute-start.3) | collective-permute-done | bytes 143392 | tf_op jit(solution)/shard_map/ppermute | solution.py:375
  30.0 3.1 %shard_map.72 = (f32[256,1024]{1,0:T(8,128)S(1)}, f32[256,1024]{1,0:T(8,128)S(1)}, f32[256,1024]{1,0:T(8,128)S(1)}, f32[8,256]{1,0:T(8,128)S(1)}, f32[152,256]{1...) custom-call(f32[256,1024]{1,0:T(8,128)S(1)} %copy-done.4, ...), custom_call_target="tpu_custom_call" | custom-call | flops 4000000000 | bytes 12000000 | tf_op jit(solution)/shard_map/pallas_call | solution.py:38
  33.1 4.3 %collective-permute-start.10 = (f32[128,768]{1,0:T(8,128)S(1)}, f32[128,768]{1,0:T(8,128)S(1)}, u32[]{:S(2)}, u32[]{:S(2)}) collective-permute-start(f32[128,768]{1,0:T(8,128)S(1)} %get-tuple-element.70), channel_id=1, source_target_pairs={{8,16},{16,8},{24,32},{32,24},{40,48},{48,40},{56,64},{64,56},{72,... | collective-permute-start | bytes 1179656 | tf_op jit(solution)/shard_map/ppermute | solution.py:366
  37.4 0.0 collective-permute-start.11
  37.4 0.2 collective-permute-start.6
  37.6 0.3 collective-permute-start.7
  37.9 6.6 %collective-permute-done.6.far = f32[152,256]{1,0:T(8,128)S(1)} collective-permute-done((f32[152,256]{1,0:T(8,128)S(1)}, f32[152,256]{1,0:T(8,128)S(1)}, u32[]{:S(2)}, u32[]{:S(2)}) %collective-permute-start.6) | collective-permute-done | bytes 155680 | tf_op jit(solution)/shard_map/ppermute | solution.py:364
  44.5 0.0 collective-permute-done.7.near
  44.5 0.6 shard_map.73
  45.1 2.8 %collective-permute-start.8 = (f32[280,128]{1,0:T(8,128)S(1)}, f32[280,128]{1,0:T(8,128)S(1)}, u32[]{:S(2)}, u32[]{:S(2)}) collective-permute-start(f32[280,128]{1,0:T(8,128)S(1)} %get-tuple-element.66), channel_id=1, source_target_pairs={{0,1},{1,2},{2,3},{3,4},{4,5},{5,6},{6,7},{7,0},{8,9},{9,10},{10,1... | collective-permute-start | bytes 430088 | tf_op jit(solution)/shard_map/ppermute | solution.py:376
  47.9 1.7 %collective-permute-start.9 = (f32[280,128]{1,0:T(8,128)S(1)}, f32[280,128]{1,0:T(8,128)S(1)}, u32[]{:S(2)}, u32[]{:S(2)}) collective-permute-start(f32[280,128]{1,0:T(8,128)S(1)} %get-tuple-element.67), channel_id=1, source_target_pairs={{0,7},{1,0},{2,1},{3,2},{4,3},{5,4},{6,5},{7,6},{8,15},{9,8},{10,9... | collective-permute-start | bytes 430088 | tf_op jit(solution)/shard_map/ppermute | solution.py:375
  49.6 0.0 collective-permute-done.10.far
  49.6 0.0 collective-permute-done.11.near
  49.6 3.2 %shard_map.74 = (f32[256,1024]{1,0:T(8,128)S(1)}, f32[256,1024]{1,0:T(8,128)S(1)}) custom-call(f32[256,1024]{1,0:T(8,128)S(1)} %get-tuple-element.58.new.refs_1_, f32[256,1024]{1,0:T(8,128)S(1)} %get-tuple-element.60.value, f32[256,1024]{1,0:T(8,128)S(1)} %copy-done.4, f32[8,1024]{1,0:T(8,128)S(1)} %get-tuple-element.64.seams.refs_2_, ...), custom_call_target="tpu_custom_call" | custom-call | flops 3000000000 | bytes 9000000 | tf_op jit(solution)/shard_map/pallas_call | solution.py:38
  52.9 0.3 collective-permute-done.8.refs_4_
  53.1 1.5 %collective-permute-done.9.refs_5_ = f32[280,128]{1,0:T(8,128)S(1)} collective-permute-done((f32[280,128]{1,0:T(8,128)S(1)}, f32[280,128]{1,0:T(8,128)S(1)}, u32[]{:S(2)}, u32[]{:S(2)}) %collective-permute-start.9) | collective-permute-done | bytes 143392 | tf_op jit(solution)/shard_map/ppermute | solution.py:375
  54.7 2.3 %shard_map.75 = (f32[256,1024]{1,0:T(8,128)}, f32[256,1024]{1,0:T(8,128)}) custom-call(f32[256,1024]{1,0:T(8,128)S(1)} %copy-done.4, f32[256,1024]{1,0:T(8,128)S(1)} %get-tuple-element.58.new.refs_1_, f32[8,1024]{1,0:T(8,128)S(1)} %get-tuple-element.64.seams.refs_2_, f32[8,768]{1,0:T(8,128)S(1)} %get-tuple-element.65.refs_3_, ...), custom_call_target="tpu_custom_call" | custom-call | flops 2000000000 | bytes 6000000 | tf_op jit(solution)/shard_map/pallas_call | solution.py:38
  (3 shorter events, 0.0 us)
Async XLA Ops:
  0.6 1.2 %copy-start = (f32[256,1024]{1,0:T(8,128)S(1)}, f32[256,1024]{1,0:T(8,128)}, u32[]{:S(2)}) copy-start(f32[256,1024]{1,0:T(8,128)} %dens.3) | copy-start | bytes 3145732
  1.9 1.2 %copy-start.2 = (f32[256,1024]{1,0:T(8,128)S(1)}, f32[256,1024]{1,0:T(8,128)}, u32[]{:S(2)}) copy-start(f32[256,1024]{1,0:T(8,128)} %value.5) | copy-start | bytes 3145732
  3.1 10.3 %copy-start.5 = (f32[256]{0:T(256)S(1)}, f32[256]{0:T(256)}, u32[]{:S(2)}) copy-start(f32[256]{0:T(256)} %param.8) | copy-start | bytes 3076
  3.1 10.5 %copy-start.6 = (f32[256]{0:T(256)S(1)}, f32[256]{0:T(256)}, u32[]{:S(2)}) copy-start(f32[256]{0:T(256)} %param.9) | copy-start | bytes 3076
  3.1 16.5 %copy-start.3 = (f32[256,1024]{1,0:T(8,128)S(1)}, f32[256,1024]{1,0:T(8,128)}, u32[]{:S(2)}) copy-start(f32[256,1024]{1,0:T(8,128)} %value.5) | copy-start | bytes 3145732
  6.0 13.6 %copy-start.1 = (f32[256,1024]{1,0:T(8,128)S(1)}, f32[256,1024]{1,0:T(8,128)}, u32[]{:S(2)}) copy-start(f32[256,1024]{1,0:T(8,128)} %dens.3) | copy-start | bytes 3145732
  6.0 18.7 %collective-permute-start.4 = (f32[128,768]{1,0:T(8,128)}, f32[128,768]{1,0:T(8,128)}, u32[]{:S(2)}, u32[]{:S(2)}) collective-permute-start(f32[128,768]{1,0:T(8,128)} %get-tuple-element.50), channel_id=1, source_target_pairs={{8,16},{16,8},{24,32},{32,24},{40,48},{48,40},{56,64},{64,56},{72,... | collective-permute-start | bytes 1179656 | tf_op jit(solution)/shard_map/ppermute | solution.py:366
  12.3 12.4 %collective-permute-start.5 = (f32[128,768]{1,0:T(8,128)}, f32[128,768]{1,0:T(8,128)}, u32[]{:S(2)}, u32[]{:S(2)}) collective-permute-start(f32[128,768]{1,0:T(8,128)} %get-tuple-element.51), channel_id=1, source_target_pairs={{0,8},{8,0},{16,24},{24,16},{32,40},{40,32},{48,56},{56,48},{64,72... | collective-permute-start | bytes 1179656 | tf_op jit(solution)/shard_map/ppermute | solution.py:367
  12.3 7.3 %collective-permute-start = (f32[152,256]{1,0:T(8,128)}, f32[152,256]{1,0:T(8,128)S(1)}, u32[]{:S(2)}, u32[]{:S(2)}) collective-permute-start(f32[152,256]{1,0:T(8,128)} %get-tuple-element.40), channel_id=1, source_target_pairs={{8,16},{16,8},{24,32},{32,24},{40,48},{48,40},{56,64},{64,56},{72,... | collective-permute-start | bytes 466952 | tf_op jit(solution)/shard_map/ppermute | solution.py:364
  13.4 6.2 %collective-permute-start.1 = (f32[152,256]{1,0:T(8,128)}, f32[152,256]{1,0:T(8,128)S(1)}, u32[]{:S(2)}, u32[]{:S(2)}) collective-permute-start(f32[152,256]{1,0:T(8,128)} %get-tuple-element.41), channel_id=1, source_target_pairs={{0,8},{8,0},{16,24},{24,16},{32,40},{40,32},{48,56},{56,48},{64,72... | collective-permute-start | bytes 466952 | tf_op jit(solution)/shard_map/ppermute | solution.py:365
  19.6 5.1 %copy-start.4 = (f32[256,1024]{1,0:T(8,128)S(1)}, f32[256,1024]{1,0:T(8,128)}, u32[]{:S(2)}) copy-start(f32[256,1024]{1,0:T(8,128)} %refs_0_.3) | copy-start | bytes 3145732
  20.2 8.9 %collective-permute-start.2 = (f32[280,128]{1,0:T(8,128)S(1)}, f32[280,128]{1,0:T(8,128)S(1)}, u32[]{:S(2)}, u32[]{:S(2)}) collective-permute-start(f32[280,128]{1,0:T(8,128)S(1)} %get-tuple-element.46), channel_id=1, source_target_pairs={{0,1},{1,2},{2,3},{3,4},{4,5},{5,6},{6,7},{7,0},{8,9},{9,10},{10,1... | collective-permute-start | bytes 430088 | tf_op jit(solution)/shard_map/ppermute | solution.py:376
  23.0 7.0 %collective-permute-start.3 = (f32[280,128]{1,0:T(8,128)S(1)}, f32[280,128]{1,0:T(8,128)S(1)}, u32[]{:S(2)}, u32[]{:S(2)}) collective-permute-start(f32[280,128]{1,0:T(8,128)S(1)} %get-tuple-element.47), channel_id=1, source_target_pairs={{0,7},{1,0},{2,1},{3,2},{4,3},{5,4},{6,5},{7,6},{8,15},{9,8},{10,9... | collective-permute-start | bytes 430088 | tf_op jit(solution)/shard_map/ppermute | solution.py:375
  33.1 16.6 %collective-permute-start.10 = (f32[128,768]{1,0:T(8,128)S(1)}, f32[128,768]{1,0:T(8,128)S(1)}, u32[]{:S(2)}, u32[]{:S(2)}) collective-permute-start(f32[128,768]{1,0:T(8,128)S(1)} %get-tuple-element.70), channel_id=1, source_target_pairs={{8,16},{16,8},{24,32},{32,24},{40,48},{48,40},{56,64},{64,56},{72,... | collective-permute-start | bytes 1179656 | tf_op jit(solution)/shard_map/ppermute | solution.py:366
  37.4 12.2 %collective-permute-start.11 = (f32[128,768]{1,0:T(8,128)S(1)}, f32[128,768]{1,0:T(8,128)S(1)}, u32[]{:S(2)}, u32[]{:S(2)}) collective-permute-start(f32[128,768]{1,0:T(8,128)S(1)} %get-tuple-element.71), channel_id=1, source_target_pairs={{0,8},{8,0},{16,24},{24,16},{32,40},{40,32},{48,56},{56,48},{64,72... | collective-permute-start | bytes 1179656 | tf_op jit(solution)/shard_map/ppermute | solution.py:367
  37.4 7.1 %collective-permute-start.6 = (f32[152,256]{1,0:T(8,128)S(1)}, f32[152,256]{1,0:T(8,128)S(1)}, u32[]{:S(2)}, u32[]{:S(2)}) collective-permute-start(f32[152,256]{1,0:T(8,128)S(1)} %get-tuple-element.62), channel_id=1, source_target_pairs={{8,16},{16,8},{24,32},{32,24},{40,48},{48,40},{56,64},{64,56},{72,... | collective-permute-start | bytes 466952 | tf_op jit(solution)/shard_map/ppermute | solution.py:364
  37.6 6.9 %collective-permute-start.7 = (f32[152,256]{1,0:T(8,128)S(1)}, f32[152,256]{1,0:T(8,128)S(1)}, u32[]{:S(2)}, u32[]{:S(2)}) collective-permute-start(f32[152,256]{1,0:T(8,128)S(1)} %get-tuple-element.63), channel_id=1, source_target_pairs={{0,8},{8,0},{16,24},{24,16},{32,40},{40,32},{48,56},{56,48},{64,72... | collective-permute-start | bytes 466952 | tf_op jit(solution)/shard_map/ppermute | solution.py:365
  45.1 8.0 %collective-permute-start.8 = (f32[280,128]{1,0:T(8,128)S(1)}, f32[280,128]{1,0:T(8,128)S(1)}, u32[]{:S(2)}, u32[]{:S(2)}) collective-permute-start(f32[280,128]{1,0:T(8,128)S(1)} %get-tuple-element.66), channel_id=1, source_target_pairs={{0,1},{1,2},{2,3},{3,4},{4,5},{5,6},{6,7},{7,0},{8,9},{9,10},{10,1... | collective-permute-start | bytes 430088 | tf_op jit(solution)/shard_map/ppermute | solution.py:376
  47.9 6.8 %collective-permute-start.9 = (f32[280,128]{1,0:T(8,128)S(1)}, f32[280,128]{1,0:T(8,128)S(1)}, u32[]{:S(2)}, u32[]{:S(2)}) collective-permute-start(f32[280,128]{1,0:T(8,128)S(1)} %get-tuple-element.67), channel_id=1, source_target_pairs={{0,7},{1,0},{2,1},{3,2},{4,3},{5,4},{6,5},{7,6},{8,15},{9,8},{10,9... | collective-permute-start | bytes 430088 | tf_op jit(solution)/shard_map/ppermute | solution.py:375

commit v3 on v2

v3 whole, which is shorter than its diff:
```python
import functools

import jax
import jax.numpy as jnp
from jax import lax
from jax.experimental import pallas as pl
from jax.experimental.pallas import tpu as pltpu
from jax.sharding import PartitionSpec as P

STEPS = 2
EDGE_COST = 6
FIRST_MIB = 51
NU = 0.5
DT = 0.1

ROWS = 256
COLS = 1024
KW = 256
HALF = KW // 2
EDGE = 128
MID = COLS - 2 * EDGE
FROM_R = COLS - EDGE
RAW_AT = HALF
TURNED_AT = RAW_AT + 16
FIRST_ROWS = TURNED_AT + 8
TALL = 3 * ROWS
SEGMENTS = TALL // EDGE
COL_ROWS = ROWS + 4 * SEGMENTS

VMEM = pl.BlockSpec(memory_space=pltpu.VMEM)
HBM = pl.BlockSpec(memory_space=pltpu.HBM)
F32 = jnp.float32
BF16 = jnp.bfloat16


def shape(*dims, kind=F32):
    return jax.ShapeDtypeStruct(dims, kind)


def call(kernel, out_shapes, scratch, micros, *operands, hbm_in=(), hbm_out=(), aliases=None, mib=24):
    return pl.pallas_call(
        kernel,
        out_shape=out_shapes,
        in_specs=[HBM if n in hbm_in else VMEM for n in range(len(operands))],
        out_specs=[HBM if n in hbm_out else VMEM for n in range(len(out_shapes))],
        scratch_shapes=scratch,
        input_output_aliases=aliases or {},
        compiler_params=pltpu.CompilerParams(vmem_limit_bytes=mib * 1024 * 1024),
        cost_estimate=pl.CostEstimate(
            flops=int(micros * 10**9), bytes_accessed=int(micros * 3 * 10**6), transcendentals=0
        ),
    )(*operands)


def core_index():
    return lax.rem(lax.axis_index("rows"), 2)


def split(x):
    hi = x.astype(BF16)
    return hi, (x - hi.astype(F32)).astype(BF16)


def product(left, right):
    dot = functools.partial(jnp.dot, preferred_element_type=F32)
    return dot(left[0], right[0]) + (dot(left[1], right[0]) + dot(left[0], right[1]))


def put_split(refs, x):
    refs[0][...], refs[1][...] = split(x)


def band_tables(kern_rows, kern_cols, rows_hi, rows_lo, turned_hi, turned_lo, cols_hi, cols_lo):
    for kern, refs in ((kern_rows, (turned_hi, turned_lo)), (kern_cols, (cols_hi, cols_lo))):
        row = jnp.concatenate([jnp.zeros((1, 2 * KW), F32), kern[...]], axis=1)
        full = jnp.broadcast_to(row, (2 * KW, 3 * KW))
        table = pltpu.roll(full, 0, 1, stride=1, stride_axis=0)[:, :KW]
        put_split(refs, table)
        if kern is kern_rows:
            put_split((rows_hi, rows_lo), table.T)


TABLES = [shape(KW, 2 * KW, kind=BF16)] * 2 + [shape(2 * KW, KW, kind=BF16)] * 4


def flux(a, here, there):
    c = DT * NU
    a = DT * a
    return here * jnp.maximum(a + c, c) + there * jnp.minimum(a - c, -c)


def eight_rows(m, u):
    width = m.shape[1]
    flux_x = flux(u - pltpu.roll(u, 7, 0), m, pltpu.roll(m, 7, 0))
    flux_y = flux(u - pltpu.roll(u, width - 1, 1), m, pltpu.roll(m, width - 1, 1))
    return m - ((flux_x - pltpu.roll(flux_x, 1, 0)) + (flux_y - pltpu.roll(flux_y, 1, 1)))


def middle_density(dens, value, out):
    dims = (8, MID)
    sub = lax.broadcasted_iota(jnp.int32, dims, 0)
    top = sub == 0
    end = sub == 7
    own = slice(EDGE, FROM_R)

    def step(i, flux_before):
        rows = pl.ds(pl.multiple_of(8 * i, 8), 8)
        after = pl.ds(pl.multiple_of(jnp.minimum(8 * i + 8, ROWS - 8), 8), 8)
        m_all = dens[rows, :]
        u_all = value[rows, :]
        m = m_all[:, own]
        u = u_all[:, own]
        m_down = pltpu.roll(jnp.where(top, dens[after, own], m), 7, 0)
        u_down = pltpu.roll(jnp.where(top, value[after, own], u), 7, 0)
        flux_x = flux(u - u_down, m, m_down)
        flux_up = pltpu.roll(jnp.where(end, flux_before, flux_x), 1, 0)
        u_right = pltpu.roll(u_all, COLS - 1, 1)[:, 0:FROM_R]
        m_right = pltpu.roll(m_all, COLS - 1, 1)[:, 0:FROM_R]
        flux_y = flux(u_all[:, 0:FROM_R] - u_right, m_all[:, 0:FROM_R], m_right)
        flux_left = pltpu.roll(flux_y, 1, 1)[:, own]
        out[rows, :] = m - ((flux_x - flux_up) + (flux_y[:, own] - flux_left))
        return flux_x

    lax.fori_loop(0, ROWS // 8, step, jnp.zeros(dims, F32), unroll=4)


def inner_value(value, potential, out):
    dims = (8, COLS)
    sub = lax.broadcasted_iota(jnp.int32, dims, 0)
    top = sub == 0
    end = sub == 7

    def step(i, before):
        rows = pl.ds(pl.multiple_of(8 * i, 8), 8)
        after = pl.ds(pl.multiple_of(jnp.minimum(8 * i + 8, ROWS - 8), 8), 8)
        u = value[rows, :]
        down = pltpu.roll(jnp.where(top, value[after, :], u), 7, 0) - u
        up = pltpu.roll(jnp.where(end, before, down), 1, 0)
        right = pltpu.roll(u, COLS - 1, 1) - u
        left = pltpu.roll(right, 1, 1)
        out[rows, :] = value_formula(u, down, up, right, left, potential[rows, :])
        return down

    lax.fori_loop(0, ROWS // 8, step, jnp.zeros(dims, F32), unroll=4)


def end_rows(value, potential, around, out):
    sub = lax.broadcasted_iota(jnp.int32, (8, COLS), 0)
    for rows, at, halo in ((slice(0, 8), 0, 1), (slice(ROWS - 8, ROWS), 7, 6)):
        u = value[rows, :]
        there = around[halo : halo + 1, :]
        down = pltpu.roll(u, 7, 0)
        up = pltpu.roll(u, 1, 0)
        if at == 0:
            up = jnp.where(sub == 0, there, up)
        else:
            down = jnp.where(sub == 7, there, down)
        right = pltpu.roll(u, COLS - 1, 1) - u
        result = value_formula(u, down - u, u - up, right, pltpu.roll(right, 1, 1), potential[rows, :])
        out[rows.start + at : rows.start + at + 1, :] = result[at : at + 1, :]


def value_formula(u, down, up, right, left, cost):
    grad_sq = (
        jnp.square(jnp.maximum(up, 0.0))
        + jnp.square(jnp.minimum(down, 0.0))
        + jnp.square(jnp.maximum(left, 0.0))
        + jnp.square(jnp.minimum(right, 0.0))
    )
    lap = (down - up) + (right - left)
    return u + DT * (NU * lap - 0.5 * grad_sq + cost)


def side_density(dens, value, out):
    dims = (8, EDGE)
    sub = lax.broadcasted_iota(jnp.int32, dims, 0)
    lane = lax.broadcasted_iota(jnp.int32, dims, 1)
    top = sub == 0
    end = sub == 7
    blocks = [slice(at, at + EDGE) for at in (0, EDGE, FROM_R - EDGE, FROM_R)]

    def right(here, there):
        return jnp.where(lane == EDGE - 1, pltpu.roll(there, EDGE - 1, 1), pltpu.roll(here, EDGE - 1, 1))

    def left(here, there):
        return jnp.where(lane == 0, pltpu.roll(there, 1, 1), pltpu.roll(here, 1, 1))

    def step(i, carry):
        rows = pl.ds(pl.multiple_of(8 * i, 8), 8)
        after = pl.ds(pl.multiple_of(jnp.minimum(8 * i + 8, ROWS - 8), 8), 8)
        result = []
        for n, flux_before in zip((0, 3), carry):
            m = dens[rows, blocks[n]]
            u = value[rows, blocks[n]]
            m_down = pltpu.roll(jnp.where(top, dens[after, blocks[n]], m), 7, 0)
            u_down = pltpu.roll(jnp.where(top, value[after, blocks[n]], u), 7, 0)
            flux_x = flux(u - u_down, m, m_down)
            flux_up = pltpu.roll(jnp.where(end, flux_before, flux_x), 1, 0)
            if n == 0:
                flux_right = flux(u - right(u, value[rows, blocks[1]]), m, right(m, dens[rows, blocks[1]]))
                flux_left = pltpu.roll(flux_right, 1, 1)
            else:
                m_left = left(m, dens[rows, blocks[2]])
                flux_left = flux(left(u, value[rows, blocks[2]]) - u, m_left, m)
                flux_right = pltpu.roll(flux_left, EDGE - 1, 1)
            at = slice(0, EDGE) if n == 0 else slice(EDGE, 2 * EDGE)
            out[rows, at] = m - ((flux_x - flux_up) + (flux_right - flux_left))
            result.append(flux_x)
        return tuple(result)

    zeros = jnp.zeros(dims, F32)
    lax.fori_loop(0, ROWS // 8, step, (zeros, zeros), unroll=8)


def prepare_sides(dens, value, side, own_t, far, near):
    core = core_index()
    side_density(dens, value, side)
    for n, ref in enumerate((dens, value)):
        own_t[4 * n : 4 * n + 2, :] = ref[:, 0:EDGE].T[0:2, :]
        own_t[4 * n + 2 : 4 * n + 4, :] = ref[:, FROM_R:COLS].T[EDGE - 2 : EDGE, :]
    for one, bottom in ((far, core), (near, 1 - core)):
        one[0:HALF, :] = side[pl.ds(pl.multiple_of(bottom * HALF, 8), HALF), :]
        for n, ref in enumerate((dens, value)):
            eight = ref[pl.ds(pl.multiple_of(bottom * (ROWS - 8), 8), 8), :]
            pair = jnp.where(bottom == 1, eight[6:8, :], eight[0:2, :])
            for q in range(COLS // 256):
                at = RAW_AT + 4 * q + 2 * n
                one[at : at + 2, :] = pair[:, 256 * q : 256 * q + 256]
        one[TURNED_AT:FIRST_ROWS, :] = own_t[...]


def rest_kernel(dens, value, new, far, near):
    core = core_index()
    middle_density(dens, value, new)
    for two, bottom in ((far, core), (near, 1 - core)):
        two[...] = new[pl.ds(pl.multiple_of(bottom * HALF, 8), HALF), :]


FIRST = [
    shape(ROWS, 2 * EDGE),
    shape(8, ROWS),
    shape(FIRST_ROWS, 2 * EDGE),
    shape(FIRST_ROWS, 2 * EDGE),
]
SECOND = [shape(ROWS, MID), shape(HALF, MID), shape(HALF, MID)]
BLOCK = shape(ROWS, COLS)


def first_sides_kernel(dens_in, value_in, dens, value, side, own_t, far, near, semaphores):
    outer = []
    inner = []
    quarter = 2 * EDGE
    for q in (0, 3, 1, 2):
        lanes = slice(quarter * q, quarter * q + quarter)
        for source, target in ((dens_in, dens), (value_in, value)):
            copies = outer if q in (0, 3) else inner
            n = len(outer) + len(inner)
            copies.append(pltpu.make_async_copy(source.at[:, lanes], target.at[:, lanes], semaphores.at[n]))
    for copy in outer + inner:
        copy.start()
    for copy in outer + inner:
        copy.wait()
    prepare_sides(dens, value, side, own_t, far, near)


def turned_cost(potential, cost_t):
    cost_t[0:2, :] = potential[:, 0:EDGE].T[0:2, :]
    cost_t[2:4, :] = potential[:, FROM_R:COLS].T[EDGE - 2 : EDGE, :]


def first_rest_kernel(dens, value, kern_rows, kern_cols, new, far, near, *refs):
    copies = [
        pltpu.make_async_copy(source, target, refs[8].at[n])
        for n, (source, target) in enumerate(((kern_rows, refs[6]), (kern_cols, refs[7])))
    ]
    for copy in copies:
        copy.start()
    rest_kernel(dens, value, new, far, near)
    for copy in copies:
        copy.wait()
    band_tables(refs[6], refs[7], *refs[:6])


def halo_rows(ext, far, near):
    core = core_index()
    ext[pl.ds(pl.multiple_of(core * (HALF + ROWS), 8), HALF), :] = far
    ext[pl.ds(pl.multiple_of((1 - core) * (HALF + ROWS), 8), HALF), :] = near


def edge_kernel(
    dens, value, side, own_t, far, near, rows_hi, rows_lo,
    to_left, to_right, seams, around, tall, mixed, dens_8, ext,
):
    core = core_index()
    for ref, own, n in ((dens_8, dens, 0), (around, value, 1)):
        for q in range(COLS // 256):
            lanes = slice(256 * q, 256 * q + 256)
            at = RAW_AT + 4 * q + 2 * n
            f = far[at : at + 2, :]
            g = near[at : at + 2, :]
            ref[0:2, lanes] = jnp.where(core == 0, f, g)
            ref[6:8, lanes] = jnp.where(core == 0, g, f)
        ref[2:4, :] = own[0:2, :]
        ref[4:6, :] = own[ROWS - 2 : ROWS, :]
    seam = eight_rows(dens_8[...], around[...])
    seams[...] = seam
    f = far[TURNED_AT:FIRST_ROWS, :]
    g = near[TURNED_AT:FIRST_ROWS, :]
    tall[:, 0:ROWS] = jnp.where(core == 0, f, g)
    tall[:, ROWS : 2 * ROWS] = own_t[...]
    tall[:, 2 * ROWS : TALL] = jnp.where(core == 0, g, f)

    halo_rows(ext, far[0:HALF, :], near[0:HALF, :])
    ext[HALF : HALF + ROWS, :] = side[...]
    put_seams(ext, seams, ((slice(0, EDGE), slice(0, EDGE)), (slice(EDGE, 2 * EDGE), slice(FROM_R, COLS))))
    result = product((rows_hi[...], rows_lo[...]), split(ext[...]))
    mixed[...] = result
    for ref, lanes, at in ((to_left, slice(0, EDGE), 0), (to_right, slice(EDGE, 2 * EDGE), 2)):
        ref[0:ROWS, :] = result[:, lanes]
        for q in range(SEGMENTS):
            segment = slice(EDGE * q, EDGE * q + EDGE)
            ref[ROWS + 4 * q : ROWS + 4 * q + 2, :] = tall[at : at + 2, segment]
            ref[ROWS + 4 * q + 2 : ROWS + 4 * q + 4, :] = tall[at + 4 : at + 6, segment]


def put_seams(ext, seams, lane_pairs):
    for to, source in lane_pairs:
        ext[HALF - 1 : HALF, to] = seams[1:2, source]
        ext[HALF : HALF + 1, to] = seams[2:3, source]
        ext[HALF + ROWS - 1 : HALF + ROWS, to] = seams[5:6, source]
        ext[HALF + ROWS : HALF + ROWS + 1, to] = seams[6:7, source]


def middle_mix(
    new, seams, far, near, rows_hi, rows_lo, cols_hi, cols_lo, cong_s, cong_m, ext, mix_hi, mix_lo
):
    rows = (rows_hi[...], rows_lo[...])
    for b in range(MID // 256):
        lanes = slice(256 * b, 256 * b + 256)
        mix_hi[:, lanes], mix_lo[:, lanes] = split(product(rows, split(ext[:, lanes])))
    before = (cols_hi[0:KW, :], cols_lo[0:KW, :])
    after = (cols_hi[KW : 2 * KW, :], cols_lo[KW : 2 * KW, :])
    for b in range(COLS // 256):
        total = None
        for block, table in ((b - 1, before), (b, after)):
            if 0 <= block < MID // 256:
                lanes = slice(256 * block, 256 * block + 256)
                part = product((mix_hi[:, lanes], mix_lo[:, lanes]), table)
                total = part if total is None else total + part
        if b == 0:
            cong_s[:, 0:256] = total
        elif b == COLS // 256 - 1:
            cong_s[:, 256:512] = total
        else:
            cong_m[:, 256 * (b - 1) : 256 * b] = total


INSIDE = slice(2 * EDGE, COLS - 2 * EDGE)
INSIDE_N = COLS - 4 * EDGE


def middle_ext(new, seams, far, near, ext):
    halo_rows(ext, far[...], near[...])
    ext[HALF : HALF + ROWS, :] = new[...]
    put_seams(ext, seams, ((slice(0, MID), slice(EDGE, FROM_R)),))


def middle_kernel(*refs):
    new, seams, far, near = refs[:4]
    value, potential, around = refs[8:11]
    cong_s, inner, cost_t, dens_out, value_out, ext, mix_hi, mix_lo, cong_m = refs[11:]
    middle_ext(new, seams, far, near, ext)
    middle_mix(*refs[:8], cong_s, cong_m, ext, mix_hi, mix_lo)
    turned_cost(potential, cost_t)
    inner_value(value, potential, inner)
    end_rows(value, potential, around, inner)
    dens_out[:, EDGE:FROM_R] = ext[HALF : HALF + ROWS, :]
    value_out[:, INSIDE] = inner[:, INSIDE] + DT * cong_m[...]


def last_middle_kernel(*refs):
    new, seams, far, near = refs[:4]
    value, potential, around = refs[8:11]
    cong_s, inner, cost_t, dens_out, value_out, ext, mix_hi, mix_lo, cong_m, value_mid, semaphores = refs[11:]
    middle_ext(new, seams, far, near, ext)
    dens_copy = pltpu.make_async_copy(
        ext.at[HALF : HALF + ROWS, :], dens_out.at[:, EDGE:FROM_R], semaphores.at[0]
    )
    dens_copy.start()
    middle_mix(*refs[:8], cong_s, cong_m, ext, mix_hi, mix_lo)
    turned_cost(potential, cost_t)
    inner_value(value, potential, inner)
    end_rows(value, potential, around, inner)
    value_mid[...] = inner[:, INSIDE] + DT * cong_m[...]
    value_copy = pltpu.make_async_copy(value_mid, value_out.at[:, INSIDE], semaphores.at[1])
    value_copy.start()
    dens_copy.wait()
    value_copy.wait()


def finish(
    cost_t, side, seams, tall, left, right, mixed, cong, inner, turned_hi, turned_lo, cols_hi, cols_lo,
    put_dens, put_value, dens_t, value_t, turn,
):
    for ref, n in ((dens_t, 0), (value_t, 1)):
        for q in range(SEGMENTS):
            lanes = slice(EDGE * q, EDGE * q + EDGE)
            at = ROWS + 4 * q + 2 * n
            ref[0:2, lanes] = left[at : at + 2, :]
            ref[6:8, lanes] = right[at : at + 2, :]
        ref[2:6, :] = tall[4 * n : 4 * n + 4, :]
    u = value_t[...]
    new_t = eight_rows(dens_t[...], u)
    window = new_t[:, HALF : HALF + 2 * KW]
    window = jnp.concatenate([window, window], axis=0)
    turn[0:8, :] = product(split(window), (turned_hi[...], turned_lo[...]))[0:8, :]
    own = slice(ROWS, 2 * ROWS)
    turn[8:16, :] = new_t[:, own]
    right_t = pltpu.roll(u, 7, 0) - u
    left_t = u - pltpu.roll(u, 1, 0)
    down_t = pltpu.roll(u, TALL - 1, 1) - u
    up_t = u - pltpu.roll(u, 1, 1)
    cost = jnp.concatenate([cost_t[0:2, :], cost_t[0:4, :], cost_t[2:4, :]], axis=0)
    turn[16:24, :] = value_formula(
        u[:, own], down_t[:, own], up_t[:, own], right_t[:, own], left_t[:, own], cost
    )
    columns = turn[...].T

    def column(n):
        return columns[:, n : n + 1]

    lane = lax.broadcasted_iota(jnp.int32, (ROWS, 2 * EDGE), 1)
    before = (cols_hi[0:KW, :], cols_lo[0:KW, :])
    after = (cols_hi[KW : 2 * KW, :], cols_lo[KW : 2 * KW, :])
    low = jnp.concatenate([left[0:ROWS, :], mixed[:, 0:EDGE]], axis=1)
    low = jnp.where(lane == EDGE - 1, column(1), jnp.where(lane == EDGE, column(2), low))
    low = cong[:, 0:256] + product(split(low), before)
    high = jnp.concatenate([mixed[:, EDGE : 2 * EDGE], right[0:ROWS, :]], axis=1)
    high = jnp.where(lane == EDGE - 1, column(5), jnp.where(lane == EDGE, column(6), high))
    high = cong[:, 256:512] + product(split(high), after)

    lane = lax.broadcasted_iota(jnp.int32, (ROWS, EDGE), 1)
    row = lax.broadcasted_iota(jnp.int32, (ROWS, EDGE), 0)
    put_value(1, inner[:, EDGE : 2 * EDGE] + DT * low[:, EDGE : 2 * EDGE])
    put_value(2, inner[:, FROM_R - EDGE : FROM_R] + DT * high[:, 0:EDGE])
    put_value(0, jnp.where(lane == 0, column(18), inner[:, 0:EDGE]) + DT * low[:, 0:EDGE])
    put_value(
        3, jnp.where(lane == EDGE - 1, column(21), inner[:, FROM_R:COLS]) + DT * high[:, EDGE : 2 * EDGE]
    )
    for block, lanes, from_side, at, n in (
        (0, slice(0, EDGE), slice(0, EDGE), 0, 10),
        (3, slice(FROM_R, COLS), slice(EDGE, 2 * EDGE), EDGE - 1, 13),
    ):
        x = jnp.where(row == 0, seams[2:3, lanes], side[:, from_side])
        x = jnp.where(row == ROWS - 1, seams[5:6, lanes], x)
        put_dens(block, jnp.where(lane == at, column(n), x))


FINISH_SCRATCH = [
    pltpu.VMEM((8, TALL), F32),
    pltpu.VMEM((8, TALL), F32),
    pltpu.VMEM((128, ROWS), F32),
]


def next_sides_kernel(*refs):
    dens, value = refs[15:17]
    starts = (0, EDGE, FROM_R - EDGE, FROM_R)

    def put(ref):
        def store(block, x):
            ref[:, starts[block] : starts[block] + EDGE] = x

        return store

    finish(*refs[:13], put(dens), put(value), *refs[21:])
    prepare_sides(dens, value, *refs[17:21])


def last_sides_kernel(*refs):
    dens_out, value_out = refs[15:17]
    dens_s, value_s, dens_t, value_t, turn, semaphores = refs[17:]
    starts = (0, EDGE, FROM_R - EDGE, FROM_R)
    copies = []

    def put(sides, out):
        def store(block, x):
            lanes = slice(EDGE * block, EDGE * block + EDGE)
            sides[:, lanes] = x
            target = out.at[:, starts[block] : starts[block] + EDGE]
            copy = pltpu.make_async_copy(sides.at[:, lanes], target, semaphores.at[len(copies)])
            copy.start()
            copies.append(copy)

        return store

    finish(*refs[:13], put(dens_s, dens_out), put(value_s, value_out), dens_t, value_t, turn)
    for copy in copies:
        copy.wait()


def row_pairs(count, first):
    pairs = []
    for a in range(first, count, 2):
        b = (a + 1) % count
        pairs += [(a, b), (b, a)]
    return pairs


def body(density, value_field, potential, kern_rows, kern_cols):
    n_rows = lax.axis_size("rows")
    n_cols = lax.axis_size("cols")
    far_pairs = row_pairs(n_rows, 1)
    near_pairs = row_pairs(n_rows, 0)
    to_right = [(c, (c + 1) % n_cols) for c in range(n_cols)]
    to_left = [(c, (c - 1) % n_cols) for c in range(n_cols)]
    dens, value, side, own_t, far_1, near_1 = call(
        first_sides_kernel,
        [BLOCK, BLOCK] + FIRST,
        [pltpu.SemaphoreType.DMA((8,))],
        1,
        density, value_field,
        hbm_in=(0, 1),
        mib=FIRST_MIB,
    )
    for step_index in range(STEPS):
        last = step_index == STEPS - 1
        if step_index == 0:
            new, far_2, near_2, *table = call(
                first_rest_kernel,
                SECOND + TABLES,
                [pltpu.VMEM((1, KW), F32), pltpu.VMEM((1, KW), F32), pltpu.SemaphoreType.DMA((2,))],
                1,
                dens, value, kern_rows[None], kern_cols[None],
                hbm_in=(2, 3),
            )
            rows_table, turned_table, cols_table = table[0:2], table[2:4], table[4:6]
        else:
            new, far_2, near_2 = call(rest_kernel, SECOND, [], 1, dens, value)
        far_1 = lax.ppermute(far_1, "rows", far_pairs)
        near_1 = lax.ppermute(near_1, "rows", near_pairs)
        far_2 = lax.ppermute(far_2, "rows", far_pairs)
        near_2 = lax.ppermute(near_2, "rows", near_pairs)
        left, right, seams, around, tall, mixed = call(
            edge_kernel,
            [shape(COL_ROWS, EDGE), shape(COL_ROWS, EDGE), shape(8, COLS), shape(8, COLS), shape(8, TALL), shape(ROWS, 2 * EDGE)],
            [pltpu.VMEM((8, COLS), F32), pltpu.VMEM((2 * KW, 2 * EDGE), F32)],
            EDGE_COST,
            dens, value, side, own_t, far_1, near_1, *rows_table,
        )
        right_in = lax.ppermute(left, "cols", to_left)
        left_in = lax.ppermute(right, "cols", to_right)
        scratch = [
            pltpu.VMEM((2 * KW, MID), F32),
            pltpu.VMEM((ROWS, MID), BF16),
            pltpu.VMEM((ROWS, MID), BF16),
            pltpu.VMEM((ROWS, INSIDE_N), F32),
        ]
        if last:
            scratch += [pltpu.VMEM((ROWS, INSIDE_N), F32), pltpu.SemaphoreType.DMA((2,))]
        cong, inner, cost_t, *results = call(
            last_middle_kernel if last else middle_kernel,
            [shape(ROWS, 4 * EDGE), BLOCK, shape(8, ROWS), BLOCK, BLOCK],
            scratch,
            3,
            new, seams, far_2, near_2, *rows_table, *cols_table, value, potential, around,
            hbm_out=(3, 4) if last else (),
        )
        operands = (cost_t, side, seams, tall, left_in, right_in, mixed, cong, inner, *turned_table, *cols_table, *results)
        if last:
            scratch = [pltpu.VMEM((ROWS, 4 * EDGE), F32), pltpu.VMEM((ROWS, 4 * EDGE), F32)]
            return tuple(
                call(
                    last_sides_kernel,
                    [BLOCK, BLOCK],
                    scratch + FINISH_SCRATCH + [pltpu.SemaphoreType.DMA((6,))],
                    1,
                    *operands,
                    hbm_in=(13, 14),
                    hbm_out=(0, 1),
                    aliases={13: 0, 14: 1},
                )
            )
        dens, value, side, own_t, far_1, near_1 = call(
            next_sides_kernel, [BLOCK, BLOCK] + FIRST, FINISH_SCRATCH, 1, *operands, aliases={13: 0, 14: 1}
        )


def solution(mesh):
    placed = (P("rows", "cols"), P("rows", "cols"), P("rows", "cols"), P(), P())
    return jax.shard_map(
        body,
        mesh=mesh,
        in_specs=placed,
        out_specs=(P("rows", "cols"), P("rows", "cols")),
        check_vma=False,
    )
```

time: 57.2 us -> 54.4 us (0.951)
  the two profiles are of different devices: /device:TPU:8 before, /device:TPU:1 now
where the time goes in v3:
time: 54.4 us; the launch traced here: 54.3 us
  starting transfers between devices  23.8 us (44%)
  Pallas kernels  19.4 us (36%)
  waiting for transfers between devices  9.58 us (18%)
  between operations  0.89 us (2%)
  local copies, waits for them, and re-layouts  0.68 us (1%)
    pallas_call x9, Pallas kernels, call(): pl.pallas_call(kernel, out_shape=out_shapes, in_specs=[HBM if n in hbm_in...  19.4 us
    ppermute x2, starting transfers between devices, body(): right_in = lax.ppermute(left, 'cols', to_left)  6.47 us
    ppermute x2, starting transfers between devices, body(): near_1 = lax.ppermute(near_1, 'rows', near_pairs)  5.84 us
    ppermute x2, waiting for transfers between devices, body(): left_in = lax.ppermute(right, 'cols', to_right)  5.4 us
    ppermute x2, starting transfers between devices, body(): left_in = lax.ppermute(right, 'cols', to_right)  3.84 us
    ppermute x2, starting transfers between devices, body(): near_2 = lax.ppermute(near_2, 'rows', near_pairs)  3.66 us
    ppermute x2, waiting for transfers between devices, body(): right_in = lax.ppermute(left, 'cols', to_left)  3.53 us
    ppermute x2, starting transfers between devices, body(): far_1 = lax.ppermute(far_1, 'rows', far_pairs)  3.21 us
  transfers between devices with their start and end apart: 12, of which 5 were waited for; matrix products, arithmetic and copies ran while one was open for 0% of the time, Pallas kernels for 24%

profile of v3, /device:TPU:1, one launch (start us, length us, event | category | flops | bytes accessed | tf_op | source)
XLA Modules:
  0.0 54.3 jit_solution(18338245220860076645)
XLA Ops:
  0.6 0.0 copy-start.2
  0.6 2.6 %shard_map.68 = (f32[256,1024]{1,0:T(8,128)S(1)}, f32[256,1024]{1,0:T(8,128)S(1)}, f32[256,256]{1,0:T(8,128)S(1)}, f32[8,256]{1,0:T(8,128)S(1)}, f32[152,256]{1,0:T(8,128)S(1)}, /*index=5*/f32[152,256]{1,0:T(8,128)S(1)}) custom-call(f32[256,1024]{1,0:T(8,128)} %dens_in.1, f32[256,1024]{1,0:T(8,128)} %value_in.1), custom_call_target="tpu_custom_call" | custom-call | flops 1000000000 | bytes 3000000 | tf_op jit(solution)/shard_map/pallas_call | solution.py:41
  3.3 3.1 %collective-permute-start = (f32[152,256]{1,0:T(8,128)S(1)}, f32[152,256]{1,0:T(8,128)S(1)}, u32[]{:S(2)}, u32[]{:S(2)}) collective-permute-start(f32[152,256]{1,0:T(8,128)S(1)} %get-tuple-element.53), channel_id=1, source_target_pairs={{8,16},{16,8},{24,32},{32,24},{40,48},{48,40},{56,64},{64,56},{72,... | collective-permute-start | bytes 466952 | tf_op jit(solution)/shard_map/ppermute | solution.py:540
  6.4 4.7 %collective-permute-start.1 = (f32[152,256]{1,0:T(8,128)S(1)}, f32[152,256]{1,0:T(8,128)S(1)}, u32[]{:S(2)}, u32[]{:S(2)}) collective-permute-start(f32[152,256]{1,0:T(8,128)S(1)} %get-tuple-element.54), channel_id=1, source_target_pairs={{0,8},{8,0},{16,24},{24,16},{32,40},{40,32},{48,56},{56,48},{64,72... | collective-permute-start | bytes 466952 | tf_op jit(solution)/shard_map/ppermute | solution.py:541
  11.1 0.0 copy-start.1
  11.1 0.0 copy-done.2
  11.1 0.7 %copy-done.1 = f32[256]{0:T(256)S(1)} copy-done((f32[256]{0:T(256)S(1)}, f32[256]{0:T(256)}, u32[]{:S(2)}) %copy-start.1) | copy-done | bytes 1048
  11.8 2.1 %shard_map.69 = (f32[256,768]{1,0:T(8,128)S(1)}, f32[128,768]{1,0:T(8,128)S(1)}, f32[128,768]{1,0:T(8,128)S(1)}, bf16[256,512]{1,0:T(8,128)(2,1)S(1)}, bf16[256,...) custom-call(f32[256,1024]{1,0:T(8,128)S(1)} %get-tuple-element.48.de, ...), custom_call_target="tpu_custom_call" | custom-call | flops 1000000000 | bytes 3000000 | tf_op jit(solution)/shard_map/pallas_call | solution.py:41
  13.9 0.1 collective-permute-start.2
  14.0 1.1 %collective-permute-start.3 = (f32[128,768]{1,0:T(8,128)S(1)}, f32[128,768]{1,0:T(8,128)S(1)}, u32[]{:S(2)}, u32[]{:S(2)}) collective-permute-start(f32[128,768]{1,0:T(8,128)S(1)} %get-tuple-element.59), channel_id=1, source_target_pairs={{0,8},{8,0},{16,24},{24,16},{32,40},{40,32},{48,56},{56,48},{64,72... | collective-permute-start | bytes 1179656 | tf_op jit(solution)/shard_map/ppermute | solution.py:543
  15.1 0.0 collective-permute-done.far
  15.1 0.0 collective-permute-done.1.near
  15.1 0.0 copy-start
  15.1 0.6 %shard_map.70 = (f32[280,128]{1,0:T(8,128)S(1)}, f32[280,128]{1,0:T(8,128)S(1)}, f32[8,1024]{1,0:T(8,128)S(1)}, f32[8,1024]{1,0:T(8,128)S(1)}, f32[8,768]{1,0:T(8,128)S(1)}, /*index=5*/f32[256,256]{1,0:T(8,128)S(1)}) custom-call(f32[256,1024]{1,0:T(8,128)S(1)} %get-tuple-element.48.dens, f32[256,1024]{1,0:T(8,128)S(1)} %get-tuple-element.49.value.refs_8_, ...), custom_call_target="tpu_custom_call" | custom-call | flops 6000000000 | bytes 18000000 | tf_op jit(solution)/shard_map/pallas_call | solution.py:41
  15.7 2.5 %collective-permute-start.4 = (f32[280,128]{1,0:T(8,128)S(1)}, f32[280,128]{1,0:T(8,128)S(1)}, u32[]{:S(2)}, u32[]{:S(2)}) collective-permute-start(f32[280,128]{1,0:T(8,128)S(1)} %get-tuple-element.65), channel_id=1, source_target_pairs={{0,1},{1,2},{2,3},{3,4},{4,5},{5,6},{6,7},{7,0},{8,9},{9,10},{10,1... | collective-permute-start | bytes 430088 | tf_op jit(solution)/shard_map/ppermute | solution.py:552
  18.2 2.6 %collective-permute-start.5 = (f32[280,128]{1,0:T(8,128)S(1)}, f32[280,128]{1,0:T(8,128)S(1)}, u32[]{:S(2)}, u32[]{:S(2)}) collective-permute-start(f32[280,128]{1,0:T(8,128)S(1)} %get-tuple-element.66), channel_id=1, source_target_pairs={{0,7},{1,0},{2,1},{3,2},{4,3},{5,4},{6,5},{7,6},{8,15},{9,8},{10,9... | collective-permute-start | bytes 430088 | tf_op jit(solution)/shard_map/ppermute | solution.py:551
  20.8 0.6 %collective-permute-done.2.refs_2_ = f32[128,768]{1,0:T(8,128)S(1)} collective-permute-done((f32[128,768]{1,0:T(8,128)S(1)}, f32[128,768]{1,0:T(8,128)S(1)}, u32[]{:S(2)}, u32[]{:S(2)}) %collective-permute-start.2) | collective-permute-done | bytes 393248 | tf_op jit(solution)/shard_map/ppermute | solution.py:542
  21.4 0.0 collective-permute-done.3.refs_3_
  21.5 0.0 copy-done
  21.5 3.5 %shard_map.71 = (f32[256,512]{1,0:T(8,128)S(1)}, f32[256,1024]{1,0:T(8,128)S(1)}, f32[8,256]{1,0:T(8,128)S(1)}, f32[256,1024]{1,0:T(8,128)S(1)}, f32[256,1024]{1,0:T(8,128)S(1)}) custom-call(f32[256,768]{1,0:T(8,128)S(1)} %get-tuple-element.50.refs_0_, f32[8,1024]{1,0:T(8,128)S(1)} %get-tuple-element.57.refs_1_.refs_2_, ...), custom_call_target="tpu_custom_call" | custom-call | flops 3000000000 | bytes 9000000 | tf_op jit(solution)/shard_map/pallas_call | solution.py:41
  25.0 4.0 %collective-permute-done.4.refs_4_ = f32[280,128]{1,0:T(8,128)S(1)} collective-permute-done((f32[280,128]{1,0:T(8,128)S(1)}, f32[280,128]{1,0:T(8,128)S(1)}, u32[]{:S(2)}, u32[]{:S(2)}) %collective-permute-start.4) | collective-permute-done | bytes 143392 | tf_op jit(solution)/shard_map/ppermute | solution.py:552
  29.0 1.6 %collective-permute-done.5.refs_5_ = f32[280,128]{1,0:T(8,128)S(1)} collective-permute-done((f32[280,128]{1,0:T(8,128)S(1)}, f32[280,128]{1,0:T(8,128)S(1)}, u32[]{:S(2)}, u32[]{:S(2)}) %collective-permute-start.5) | collective-permute-done | bytes 143392 | tf_op jit(solution)/shard_map/ppermute | solution.py:551
  30.5 2.0 %shard_map.72 = (f32[256,1024]{1,0:T(8,128)S(1)}, f32[256,1024]{1,0:T(8,128)S(1)}, f32[256,256]{1,0:T(8,128)S(1)}, f32[8,256]{1,0:T(8,128)S(1)}, f32[152,256]{1,0:T(8,128)S(1)}, /*index=5*/f32[152,256]{1,0:T(8,128)S(1)}) custom-call(f32[8,256]{1,0:T(8,128)S(1)} %get-tuple-element.63.refs_0_, ...), custom_call_target="tpu_custom_call", output_to_operand_aliasing={{0}: (13, {}), {1}: (14, {})} | custom-call | flops 1000000000 | bytes 3000000 | tf_op jit(solution)/shard_map/pallas_call | solution.py:41
  32.5 0.1 collective-permute-start.6
  32.6 1.1 %collective-permute-start.7 = (f32[152,256]{1,0:T(8,128)S(1)}, f32[152,256]{1,0:T(8,128)S(1)}, u32[]{:S(2)}, u32[]{:S(2)}) collective-permute-start(f32[152,256]{1,0:T(8,128)S(1)} %get-tuple-element.80), channel_id=1, source_target_pairs={{0,8},{8,0},{16,24},{24,16},{32,40},{40,32},{48,56},{56,48},{64,72... | collective-permute-start | bytes 466952 | tf_op jit(solution)/shard_map/ppermute | solution.py:541
  33.8 1.8 %shard_map.73 = (f32[256,768]{1,0:T(8,128)S(1)}, f32[128,768]{1,0:T(8,128)S(1)}, f32[128,768]{1,0:T(8,128)S(1)}) custom-call(f32[256,1024]{1,0:T(8,128)S(1)} %get-tuple-element.74.dens, f32[256,1024]{1,0:T(8,128)S(1)} %get-tuple-element.75.value.refs_8_), custom_call_target="tpu_custom_call" | custom-call | flops 1000000000 | bytes 3000000 | tf_op jit(solution)/shard_map/pallas_call | solution.py:41
  35.6 0.7 %collective-permute-start.8 = (f32[128,768]{1,0:T(8,128)S(1)}, f32[128,768]{1,0:T(8,128)S(1)}, u32[]{:S(2)}, u32[]{:S(2)}) collective-permute-start(f32[128,768]{1,0:T(8,128)S(1)} %get-tuple-element.82), channel_id=1, source_target_pairs={{8,16},{16,8},{24,32},{32,24},{40,48},{48,40},{56,64},{64,56},{72,... | collective-permute-start | bytes 1179656 | tf_op jit(solution)/shard_map/ppermute | solution.py:542
  36.3 2.5 %collective-permute-start.9 = (f32[128,768]{1,0:T(8,128)S(1)}, f32[128,768]{1,0:T(8,128)S(1)}, u32[]{:S(2)}, u32[]{:S(2)}) collective-permute-start(f32[128,768]{1,0:T(8,128)S(1)} %get-tuple-element.83), channel_id=1, source_target_pairs={{0,8},{8,0},{16,24},{24,16},{32,40},{40,32},{48,56},{56,48},{64,72... | collective-permute-start | bytes 1179656 | tf_op jit(solution)/shard_map/ppermute | solution.py:543
  38.8 0.0 collective-permute-done.6.far
  38.8 0.0 collective-permute-done.7.near
  38.8 0.6 %shard_map.74 = (f32[280,128]{1,0:T(8,128)S(1)}, f32[280,128]{1,0:T(8,128)S(1)}, f32[8,1024]{1,0:T(8,128)S(1)}, f32[8,1024]{1,0:T(8,128)S(1)}, f32[8,768]{1,0:T(8,128)S(1)}, /*index=5*/f32[256,256]{1,0:T(8,128)S(1)}) custom-call(f32[256,1024]{1,0:T(8,128)S(1)} %get-tuple-element.74.dens, f32[256,1024]{1,0:T(8,128)S(1)} %get-tuple-element.75.value.refs_8_, ...), custom_call_target="tpu_custom_call" | custom-call | flops 6000000000 | bytes 18000000 | tf_op jit(solution)/shard_map/pallas_call | solution.py:41
  39.4 1.3 %collective-permute-start.10 = (f32[280,128]{1,0:T(8,128)S(1)}, f32[280,128]{1,0:T(8,128)S(1)}, u32[]{:S(2)}, u32[]{:S(2)}) collective-permute-start(f32[280,128]{1,0:T(8,128)S(1)} %get-tuple-element.87), channel_id=1, source_target_pairs={{0,1},{1,2},{2,3},{3,4},{4,5},{5,6},{6,7},{7,0},{8,9},{9,10},{10,1... | collective-permute-start | bytes 430088 | tf_op jit(solution)/shard_map/ppermute | solution.py:552
  40.7 3.8 %collective-permute-start.11 = (f32[280,128]{1,0:T(8,128)S(1)}, f32[280,128]{1,0:T(8,128)S(1)}, u32[]{:S(2)}, u32[]{:S(2)}) collective-permute-start(f32[280,128]{1,0:T(8,128)S(1)} %get-tuple-element.88), channel_id=1, source_target_pairs={{0,7},{1,0},{2,1},{3,2},{4,3},{5,4},{6,5},{7,6},{8,15},{9,8},{10,9... | collective-permute-start | bytes 430088 | tf_op jit(solution)/shard_map/ppermute | solution.py:551
  44.6 0.0 collective-permute-done.8.refs_2_
  44.6 0.0 collective-permute-done.9.refs_3_
  44.6 4.3 %shard_map.75 = (f32[256,512]{1,0:T(8,128)S(1)}, f32[256,1024]{1,0:T(8,128)S(1)}, f32[8,256]{1,0:T(8,128)S(1)}, f32[256,1024]{1,0:T(8,128)}, f32[256,1024]{1,0:T(8,128)}) custom-call(f32[256,768]{1,0:T(8,128)S(1)} %get-tuple-element.76.refs_0_, f32[8,1024]{1,0:T(8,128)S(1)} %get-tuple-element.81.refs_1_.refs_2_, ...), custom_call_target="tpu_custom_call" | custom-call | flops 3000000000 | bytes 9000000 | tf_op jit(solution)/shard_map/pallas_call | solution.py:41
  48.9 1.4 %collective-permute-done.10.refs_4_ = f32[280,128]{1,0:T(8,128)S(1)} collective-permute-done((f32[280,128]{1,0:T(8,128)S(1)}, f32[280,128]{1,0:T(8,128)S(1)}, u32[]{:S(2)}, u32[]{:S(2)}) %collective-permute-start.10) | collective-permute-done | bytes 143392 | tf_op jit(solution)/shard_map/ppermute | solution.py:552
  50.3 2.0 %collective-permute-done.11.refs_5_ = f32[280,128]{1,0:T(8,128)S(1)} collective-permute-done((f32[280,128]{1,0:T(8,128)S(1)}, f32[280,128]{1,0:T(8,128)S(1)}, u32[]{:S(2)}, u32[]{:S(2)}) %collective-permute-start.11) | collective-permute-done | bytes 143392 | tf_op jit(solution)/shard_map/ppermute | solution.py:551
  52.2 1.9 %shard_map.76 = (f32[256,1024]{1,0:T(8,128)}, f32[256,1024]{1,0:T(8,128)}) custom-call(f32[8,256]{1,0:T(8,128)S(1)} %get-tuple-element.85.refs_0_, f32[256,256]{1,0:T(8,128)S(1)} %get-tuple-element.77.side.refs_1_, f32[8,1024]{1,0:T(8,128)S(1)} %get-tuple-element.81.refs_1_.refs_2_, ...), custom_call_target="tpu_custom_call", output_to_operand_aliasing={{0}: (13, {}), {1}: (14, {})} | custom-call | flops 1000000000 | bytes 3000000 | tf_op jit(solution)/shard_map/pallas_call | solution.py:41
Async XLA Ops:
  0.6 10.5 %copy-start.2 = (f32[256]{0:T(256)S(1)}, f32[256]{0:T(256)}, u32[]{:S(2)}) copy-start(f32[256]{0:T(256)} %param.9) | copy-start | bytes 3076
  3.3 11.8 %collective-permute-start = (f32[152,256]{1,0:T(8,128)S(1)}, f32[152,256]{1,0:T(8,128)S(1)}, u32[]{:S(2)}, u32[]{:S(2)}) collective-permute-start(f32[152,256]{1,0:T(8,128)S(1)} %get-tuple-element.53), channel_id=1, source_target_pairs={{8,16},{16,8},{24,32},{32,24},{40,48},{48,40},{56,64},{64,56},{72,... | collective-permute-start | bytes 466952 | tf_op jit(solution)/shard_map/ppermute | solution.py:540
  6.4 8.7 %collective-permute-start.1 = (f32[152,256]{1,0:T(8,128)S(1)}, f32[152,256]{1,0:T(8,128)S(1)}, u32[]{:S(2)}, u32[]{:S(2)}) collective-permute-start(f32[152,256]{1,0:T(8,128)S(1)} %get-tuple-element.54), channel_id=1, source_target_pairs={{0,8},{8,0},{16,24},{24,16},{32,40},{40,32},{48,56},{56,48},{64,72... | collective-permute-start | bytes 466952 | tf_op jit(solution)/shard_map/ppermute | solution.py:541
  11.1 0.7 %copy-start.1 = (f32[256]{0:T(256)S(1)}, f32[256]{0:T(256)}, u32[]{:S(2)}) copy-start(f32[256]{0:T(256)} %param.8) | copy-start | bytes 3076
  13.9 7.6 %collective-permute-start.2 = (f32[128,768]{1,0:T(8,128)S(1)}, f32[128,768]{1,0:T(8,128)S(1)}, u32[]{:S(2)}, u32[]{:S(2)}) collective-permute-start(f32[128,768]{1,0:T(8,128)S(1)} %get-tuple-element.58), channel_id=1, source_target_pairs={{8,16},{16,8},{24,32},{32,24},{40,48},{48,40},{56,64},{64,56},{72,... | collective-permute-start | bytes 1179656 | tf_op jit(solution)/shard_map/ppermute | solution.py:542
  14.0 7.5 %collective-permute-start.3 = (f32[128,768]{1,0:T(8,128)S(1)}, f32[128,768]{1,0:T(8,128)S(1)}, u32[]{:S(2)}, u32[]{:S(2)}) collective-permute-start(f32[128,768]{1,0:T(8,128)S(1)} %get-tuple-element.59), channel_id=1, source_target_pairs={{0,8},{8,0},{16,24},{24,16},{32,40},{40,32},{48,56},{56,48},{64,72... | collective-permute-start | bytes 1179656 | tf_op jit(solution)/shard_map/ppermute | solution.py:543
  15.1 6.4 %copy-start = (f32[256,1024]{1,0:T(8,128)S(1)}, f32[256,1024]{1,0:T(8,128)}, u32[]{:S(2)}) copy-start(f32[256,1024]{1,0:T(8,128)} %refs_9_.3) | copy-start | bytes 3145732
  15.7 13.3 %collective-permute-start.4 = (f32[280,128]{1,0:T(8,128)S(1)}, f32[280,128]{1,0:T(8,128)S(1)}, u32[]{:S(2)}, u32[]{:S(2)}) collective-permute-start(f32[280,128]{1,0:T(8,128)S(1)} %get-tuple-element.65), channel_id=1, source_target_pairs={{0,1},{1,2},{2,3},{3,4},{4,5},{5,6},{6,7},{7,0},{8,9},{9,10},{10,1... | collective-permute-start | bytes 430088 | tf_op jit(solution)/shard_map/ppermute | solution.py:552
  18.2 12.3 %collective-permute-start.5 = (f32[280,128]{1,0:T(8,128)S(1)}, f32[280,128]{1,0:T(8,128)S(1)}, u32[]{:S(2)}, u32[]{:S(2)}) collective-permute-start(f32[280,128]{1,0:T(8,128)S(1)} %get-tuple-element.66), channel_id=1, source_target_pairs={{0,7},{1,0},{2,1},{3,2},{4,3},{5,4},{6,5},{7,6},{8,15},{9,8},{10,9... | collective-permute-start | bytes 430088 | tf_op jit(solution)/shard_map/ppermute | solution.py:551
  32.5 6.3 %collective-permute-start.6 = (f32[152,256]{1,0:T(8,128)S(1)}, f32[152,256]{1,0:T(8,128)S(1)}, u32[]{:S(2)}, u32[]{:S(2)}) collective-permute-start(f32[152,256]{1,0:T(8,128)S(1)} %get-tuple-element.79), channel_id=1, source_target_pairs={{8,16},{16,8},{24,32},{32,24},{40,48},{48,40},{56,64},{64,56},{72,... | collective-permute-start | bytes 466952 | tf_op jit(solution)/shard_map/ppermute | solution.py:540
  32.6 6.2 %collective-permute-start.7 = (f32[152,256]{1,0:T(8,128)S(1)}, f32[152,256]{1,0:T(8,128)S(1)}, u32[]{:S(2)}, u32[]{:S(2)}) collective-permute-start(f32[152,256]{1,0:T(8,128)S(1)} %get-tuple-element.80), channel_id=1, source_target_pairs={{0,8},{8,0},{16,24},{24,16},{32,40},{40,32},{48,56},{56,48},{64,72... | collective-permute-start | bytes 466952 | tf_op jit(solution)/shard_map/ppermute | solution.py:541
  35.6 9.0 %collective-permute-start.8 = (f32[128,768]{1,0:T(8,128)S(1)}, f32[128,768]{1,0:T(8,128)S(1)}, u32[]{:S(2)}, u32[]{:S(2)}) collective-permute-start(f32[128,768]{1,0:T(8,128)S(1)} %get-tuple-element.82), channel_id=1, source_target_pairs={{8,16},{16,8},{24,32},{32,24},{40,48},{48,40},{56,64},{64,56},{72,... | collective-permute-start | bytes 1179656 | tf_op jit(solution)/shard_map/ppermute | solution.py:542
  36.3 8.3 %collective-permute-start.9 = (f32[128,768]{1,0:T(8,128)S(1)}, f32[128,768]{1,0:T(8,128)S(1)}, u32[]{:S(2)}, u32[]{:S(2)}) collective-permute-start(f32[128,768]{1,0:T(8,128)S(1)} %get-tuple-element.83), channel_id=1, source_target_pairs={{0,8},{8,0},{16,24},{24,16},{32,40},{40,32},{48,56},{56,48},{64,72... | collective-permute-start | bytes 1179656 | tf_op jit(solution)/shard_map/ppermute | solution.py:543
  39.4 10.9 %collective-permute-start.10 = (f32[280,128]{1,0:T(8,128)S(1)}, f32[280,128]{1,0:T(8,128)S(1)}, u32[]{:S(2)}, u32[]{:S(2)}) collective-permute-start(f32[280,128]{1,0:T(8,128)S(1)} %get-tuple-element.87), channel_id=1, source_target_pairs={{0,1},{1,2},{2,3},{3,4},{4,5},{5,6},{6,7},{7,0},{8,9},{9,10},{10,1... | collective-permute-start | bytes 430088 | tf_op jit(solution)/shard_map/ppermute | solution.py:552
  40.7 11.5 %collective-permute-start.11 = (f32[280,128]{1,0:T(8,128)S(1)}, f32[280,128]{1,0:T(8,128)S(1)}, u32[]{:S(2)}, u32[]{:S(2)}) collective-permute-start(f32[280,128]{1,0:T(8,128)S(1)} %get-tuple-element.88), channel_id=1, source_target_pairs={{0,7},{1,0},{2,1},{3,2},{4,3},{5,4},{6,5},{7,6},{8,15},{9,8},{10,9... | collective-permute-start | bytes 430088 | tf_op jit(solution)/shard_map/ppermute | solution.py:551

commit v4 on v3

--- a/solution.py
+++ b/solution.py
@@ -97,51 +97,45 @@
 
 
 def middle_density(dens, value, out):
-    dims = (8, MID)
-    sub = lax.broadcasted_iota(jnp.int32, dims, 0)
-    top = sub == 0
-    end = sub == 7
     own = slice(EDGE, FROM_R)
+    tall = 64
 
     def step(i, flux_before):
-        rows = pl.ds(pl.multiple_of(8 * i, 8), 8)
-        after = pl.ds(pl.multiple_of(jnp.minimum(8 * i + 8, ROWS - 8), 8), 8)
+        rows = pl.ds(pl.multiple_of(tall * i, tall), tall)
+        after = pl.ds(pl.multiple_of(jnp.minimum(tall * i + tall, ROWS - 8), 8), 8)
         m_all = dens[rows, :]
         u_all = value[rows, :]
         m = m_all[:, own]
         u = u_all[:, own]
-        m_down = pltpu.roll(jnp.where(top, dens[after, own], m), 7, 0)
-        u_down = pltpu.roll(jnp.where(top, value[after, own], u), 7, 0)
+        m_down = jnp.concatenate([m[1:], dens[after, own][0:1]], axis=0)
+        u_down = jnp.concatenate([u[1:], value[after, own][0:1]], axis=0)
         flux_x = flux(u - u_down, m, m_down)
-        flux_up = pltpu.roll(jnp.where(end, flux_before, flux_x), 1, 0)
+        flux_up = jnp.concatenate([flux_before, flux_x[:-1]], axis=0)
         u_right = pltpu.roll(u_all, COLS - 1, 1)[:, 0:FROM_R]
         m_right = pltpu.roll(m_all, COLS - 1, 1)[:, 0:FROM_R]
         flux_y = flux(u_all[:, 0:FROM_R] - u_right, m_all[:, 0:FROM_R], m_right)
         flux_left = pltpu.roll(flux_y, 1, 1)[:, own]
         out[rows, :] = m - ((flux_x - flux_up) + (flux_y[:, own] - flux_left))
-        return flux_x
-
-    lax.fori_loop(0, ROWS // 8, step, jnp.zeros(dims, F32), unroll=4)
+        return flux_x[-1:]
+
+    lax.fori_loop(0, ROWS // tall, step, jnp.zeros((1, MID), F32))
 
 
 def inner_value(value, potential, out):
-    dims = (8, COLS)
-    sub = lax.broadcasted_iota(jnp.int32, dims, 0)
-    top = sub == 0
-    end = sub == 7
+    tall = 32
 
     def step(i, before):
-        rows = pl.ds(pl.multiple_of(8 * i, 8), 8)
-        after = pl.ds(pl.multiple_of(jnp.minimum(8 * i + 8, ROWS - 8), 8), 8)
+        rows = pl.ds(pl.multiple_of(tall * i, tall), tall)
+        after = pl.ds(pl.multiple_of(jnp.minimum(tall * i + tall, ROWS - 8), 8), 8)
         u = value[rows, :]
-        down = pltpu.roll(jnp.where(top, value[after, :], u), 7, 0) - u
-        up = pltpu.roll(jnp.where(end, before, down), 1, 0)
+        down = jnp.concatenate([u[1:], value[after, :][0:1]], axis=0) - u
+        up = jnp.concatenate([before, down[:-1]], axis=0)
         right = pltpu.roll(u, COLS - 1, 1) - u
         left = pltpu.roll(right, 1, 1)
         out[rows, :] = value_formula(u, down, up, right, left, potential[rows, :])
-        return down
-
-    lax.fori_loop(0, ROWS // 8, step, jnp.zeros(dims, F32), unroll=4)
+        return down[-1:]
+
+    lax.fori_loop(0, ROWS // tall, step, jnp.zeros((1, COLS), F32), unroll=4)
 
 
 def end_rows(value, potential, around, out):
@@ -172,49 +166,37 @@
 
 
 def side_density(dens, value, out):
-    dims = (8, EDGE)
-    sub = lax.broadcasted_iota(jnp.int32, dims, 0)
-    lane = lax.broadcasted_iota(jnp.int32, dims, 1)
-    top = sub == 0
-    end = sub == 7
+    lane = lax.broadcasted_iota(jnp.int32, (ROWS, EDGE), 1)
     blocks = [slice(at, at + EDGE) for at in (0, EDGE, FROM_R - EDGE, FROM_R)]
 
-    def right(here, there):
-        return jnp.where(lane == EDGE - 1, pltpu.roll(there, EDGE - 1, 1), pltpu.roll(here, EDGE - 1, 1))
-
-    def left(here, there):
-        return jnp.where(lane == 0, pltpu.roll(there, 1, 1), pltpu.roll(here, 1, 1))
-
-    def step(i, carry):
-        rows = pl.ds(pl.multiple_of(8 * i, 8), 8)
-        after = pl.ds(pl.multiple_of(jnp.minimum(8 * i + 8, ROWS - 8), 8), 8)
-        result = []
-        for n, flux_before in zip((0, 3), carry):
-            m = dens[rows, blocks[n]]
-            u = value[rows, blocks[n]]
-            m_down = pltpu.roll(jnp.where(top, dens[after, blocks[n]], m), 7, 0)
-            u_down = pltpu.roll(jnp.where(top, value[after, blocks[n]], u), 7, 0)
-            flux_x = flux(u - u_down, m, m_down)
-            flux_up = pltpu.roll(jnp.where(end, flux_before, flux_x), 1, 0)
-            if n == 0:
-                flux_right = flux(u - right(u, value[rows, blocks[1]]), m, right(m, dens[rows, blocks[1]]))
-                flux_left = pltpu.roll(flux_right, 1, 1)
-            else:
-                m_left = left(m, dens[rows, blocks[2]])
-                flux_left = flux(left(u, value[rows, blocks[2]]) - u, m_left, m)
-                flux_right = pltpu.roll(flux_left, EDGE - 1, 1)
-            at = slice(0, EDGE) if n == 0 else slice(EDGE, 2 * EDGE)
-            out[rows, at] = m - ((flux_x - flux_up) + (flux_right - flux_left))
-            result.append(flux_x)
-        return tuple(result)
-
-    zeros = jnp.zeros(dims, F32)
-    lax.fori_loop(0, ROWS // 8, step, (zeros, zeros), unroll=8)
-
-
-def prepare_sides(dens, value, side, own_t, far, near):
+    def right(ref, here):
+        there = pltpu.roll(ref[:, blocks[1]], EDGE - 1, 1)
+        return jnp.where(lane == EDGE - 1, there, pltpu.roll(here, EDGE - 1, 1))
+
+    def left(ref, here):
+        there = pltpu.roll(ref[:, blocks[2]], 1, 1)
+        return jnp.where(lane == 0, there, pltpu.roll(here, 1, 1))
+
+    for n in (0, 3):
+        m = dens[:, blocks[n]]
+        u = value[:, blocks[n]]
+        flux_x = flux(u - pltpu.roll(u, ROWS - 1, 0), m, pltpu.roll(m, ROWS - 1, 0))
+        flux_up = pltpu.roll(flux_x, 1, 0)
+        if n == 0:
+            flux_right = flux(u - right(value, u), m, right(dens, m))
+            flux_left = pltpu.roll(flux_right, 1, 1)
+        else:
+            flux_left = flux(left(value, u) - u, left(dens, m), m)
+            flux_right = pltpu.roll(flux_left, EDGE - 1, 1)
+        at = slice(0, EDGE) if n == 0 else slice(EDGE, 2 * EDGE)
+        out[:, at] = m - ((flux_x - flux_up) + (flux_right - flux_left))
+
+
+def prepare_sides(dens, value, side, own_t, far, near, wait_middle=None):
     core = core_index()
     side_density(dens, value, side)
+    if wait_middle is not None:
+        wait_middle()
     for n, ref in enumerate((dens, value)):
         own_t[4 * n : 4 * n + 2, :] = ref[:, 0:EDGE].T[0:2, :]
         own_t[4 * n + 2 : 4 * n + 4, :] = ref[:, FROM_R:COLS].T[EDGE - 2 : EDGE, :]
@@ -258,9 +240,14 @@
             copies.append(pltpu.make_async_copy(source.at[:, lanes], target.at[:, lanes], semaphores.at[n]))
     for copy in outer + inner:
         copy.start()
-    for copy in outer + inner:
+    for copy in outer:
         copy.wait()
-    prepare_sides(dens, value, side, own_t, far, near)
+
+    def wait_middle():
+        for copy in inner:
+            copy.wait()
+
+    prepare_sides(dens, value, side, own_t, far, near, wait_middle)
 
 
 def turned_cost(potential, cost_t):

time: 54.4 us -> 51.9 us (0.954)
  Pallas kernels: 19.4 us -> 16.6 us
    pallas_call x9, Pallas kernels: 19.4 us -> 16.6 us  [call(): pl.pallas_call(kernel, out_shape=out_shapes, in_specs=[HBM if n in hbm_in...]
  transfers between devices with their start and end apart: 12 -> 12, of which waited for: 5 -> 5; matrix products, arithmetic and copies ran while one was open for 0% -> 0% of each run, Pallas kernels for 24% -> 21%
where the time goes in v4:
time: 51.9 us; the launch traced here: 51.8 us
  starting transfers between devices  24 us (46%)
  Pallas kernels  16.6 us (32%)
  waiting for transfers between devices  9.69 us (19%)
  between operations  0.89 us (2%)
  local copies, waits for them, and re-layouts  0.68 us (1%)
    pallas_call x9, Pallas kernels, call(): pl.pallas_call(kernel, out_shape=out_shapes, in_specs=[HBM if n in hbm_in...  16.6 us
    ppermute x2, starting transfers between devices, body(): right_in = lax.ppermute(left, 'cols', to_left)  6.47 us
    ppermute x2, starting transfers between devices, body(): near_1 = lax.ppermute(near_1, 'rows', near_pairs)  5.89 us
    ppermute x2, waiting for transfers between devices, body(): left_in = lax.ppermute(right, 'cols', to_right)  5.51 us
    ppermute x2, starting transfers between devices, body(): left_in = lax.ppermute(right, 'cols', to_right)  4.02 us
    ppermute x2, starting transfers between devices, body(): near_2 = lax.ppermute(near_2, 'rows', near_pairs)  3.65 us
    ppermute x2, waiting for transfers between devices, body(): right_in = lax.ppermute(left, 'cols', to_left)  3.53 us
    ppermute x2, starting transfers between devices, body(): far_1 = lax.ppermute(far_1, 'rows', far_pairs)  3.21 us
  transfers between devices with their start and end apart: 12, of which 5 were waited for; matrix products, arithmetic and copies ran while one was open for 0% of the time, Pallas kernels for 21%

profile of v4, /device:TPU:1, one launch (start us, length us, event | category | flops | bytes accessed | tf_op | source)
XLA Modules:
  0.0 51.8 jit_solution(8963728245447610827)
XLA Ops:
  0.6 0.0 copy-start.2
  0.6 2.0 %shard_map.68 = (f32[256,1024]{1,0:T(8,128)S(1)}, f32[256,1024]{1,0:T(8,128)S(1)}, f32[256,256]{1,0:T(8,128)S(1)}, f32[8,256]{1,0:T(8,128)S(1)}, f32[152,256]{1,0:T(8,128)S(1)}, /*index=5*/f32[152,256]{1,0:T(8,128)S(1)}) custom-call(f32[256,1024]{1,0:T(8,128)} %dens_in.1, f32[256,1024]{1,0:T(8,128)} %value_in.1), custom_call_target="tpu_custom_call" | custom-call | flops 1000000000 | bytes 3000000 | tf_op jit(solution)/shard_map/pallas_call | solution.py:41
  2.7 3.1 %collective-permute-start = (f32[152,256]{1,0:T(8,128)S(1)}, f32[152,256]{1,0:T(8,128)S(1)}, u32[]{:S(2)}, u32[]{:S(2)}) collective-permute-start(f32[152,256]{1,0:T(8,128)S(1)} %get-tuple-element.53), channel_id=1, source_target_pairs={{8,16},{16,8},{24,32},{32,24},{40,48},{48,40},{56,64},{64,56},{72,... | collective-permute-start | bytes 466952 | tf_op jit(solution)/shard_map/ppermute | solution.py:527
  5.8 4.7 %collective-permute-start.1 = (f32[152,256]{1,0:T(8,128)S(1)}, f32[152,256]{1,0:T(8,128)S(1)}, u32[]{:S(2)}, u32[]{:S(2)}) collective-permute-start(f32[152,256]{1,0:T(8,128)S(1)} %get-tuple-element.54), channel_id=1, source_target_pairs={{0,8},{8,0},{16,24},{24,16},{32,40},{40,32},{48,56},{56,48},{64,72... | collective-permute-start | bytes 466952 | tf_op jit(solution)/shard_map/ppermute | solution.py:528
  10.5 0.0 copy-start.1
  10.5 0.0 copy-done.2
  10.5 0.7 %copy-done.1 = f32[256]{0:T(256)S(1)} copy-done((f32[256]{0:T(256)S(1)}, f32[256]{0:T(256)}, u32[]{:S(2)}) %copy-start.1) | copy-done | bytes 1048
  11.2 1.5 %shard_map.69 = (f32[256,768]{1,0:T(8,128)S(1)}, f32[128,768]{1,0:T(8,128)S(1)}, f32[128,768]{1,0:T(8,128)S(1)}, bf16[256,512]{1,0:T(8,128)(2,1)S(1)}, bf16[256,...) custom-call(f32[256,1024]{1,0:T(8,128)S(1)} %get-tuple-element.48.de, ...), custom_call_target="tpu_custom_call" | custom-call | flops 1000000000 | bytes 3000000 | tf_op jit(solution)/shard_map/pallas_call | solution.py:41
  12.7 0.1 collective-permute-start.2
  12.8 1.1 %collective-permute-start.3 = (f32[128,768]{1,0:T(8,128)S(1)}, f32[128,768]{1,0:T(8,128)S(1)}, u32[]{:S(2)}, u32[]{:S(2)}) collective-permute-start(f32[128,768]{1,0:T(8,128)S(1)} %get-tuple-element.59), channel_id=1, source_target_pairs={{0,8},{8,0},{16,24},{24,16},{32,40},{40,32},{48,56},{56,48},{64,72... | collective-permute-start | bytes 1179656 | tf_op jit(solution)/shard_map/ppermute | solution.py:530
  13.9 0.0 collective-permute-done.far
  13.9 0.0 collective-permute-done.1.near
  13.9 0.0 copy-start
  13.9 0.6 %shard_map.70 = (f32[280,128]{1,0:T(8,128)S(1)}, f32[280,128]{1,0:T(8,128)S(1)}, f32[8,1024]{1,0:T(8,128)S(1)}, f32[8,1024]{1,0:T(8,128)S(1)}, f32[8,768]{1,0:T(8,128)S(1)}, /*index=5*/f32[256,256]{1,0:T(8,128)S(1)}) custom-call(f32[256,1024]{1,0:T(8,128)S(1)} %get-tuple-element.48.dens, f32[256,1024]{1,0:T(8,128)S(1)} %get-tuple-element.49.value.refs_8_, ...), custom_call_target="tpu_custom_call" | custom-call | flops 6000000000 | bytes 18000000 | tf_op jit(solution)/shard_map/pallas_call | solution.py:41
  14.5 2.5 %collective-permute-start.4 = (f32[280,128]{1,0:T(8,128)S(1)}, f32[280,128]{1,0:T(8,128)S(1)}, u32[]{:S(2)}, u32[]{:S(2)}) collective-permute-start(f32[280,128]{1,0:T(8,128)S(1)} %get-tuple-element.65), channel_id=1, source_target_pairs={{0,1},{1,2},{2,3},{3,4},{4,5},{5,6},{6,7},{7,0},{8,9},{9,10},{10,1... | collective-permute-start | bytes 430088 | tf_op jit(solution)/shard_map/ppermute | solution.py:539
  17.0 2.6 %collective-permute-start.5 = (f32[280,128]{1,0:T(8,128)S(1)}, f32[280,128]{1,0:T(8,128)S(1)}, u32[]{:S(2)}, u32[]{:S(2)}) collective-permute-start(f32[280,128]{1,0:T(8,128)S(1)} %get-tuple-element.66), channel_id=1, source_target_pairs={{0,7},{1,0},{2,1},{3,2},{4,3},{5,4},{6,5},{7,6},{8,15},{9,8},{10,9... | collective-permute-start | bytes 430088 | tf_op jit(solution)/shard_map/ppermute | solution.py:538
  19.7 0.6 %collective-permute-done.2.refs_2_ = f32[128,768]{1,0:T(8,128)S(1)} collective-permute-done((f32[128,768]{1,0:T(8,128)S(1)}, f32[128,768]{1,0:T(8,128)S(1)}, u32[]{:S(2)}, u32[]{:S(2)}) %collective-permute-start.2) | collective-permute-done | bytes 393248 | tf_op jit(solution)/shard_map/ppermute | solution.py:529
  20.3 0.0 collective-permute-done.3.refs_3_
  20.3 0.0 copy-done
  20.3 3.1 %shard_map.71 = (f32[256,512]{1,0:T(8,128)S(1)}, f32[256,1024]{1,0:T(8,128)S(1)}, f32[8,256]{1,0:T(8,128)S(1)}, f32[256,1024]{1,0:T(8,128)S(1)}, f32[256,1024]{1,0:T(8,128)S(1)}) custom-call(f32[256,768]{1,0:T(8,128)S(1)} %get-tuple-element.50.refs_0_, f32[8,1024]{1,0:T(8,128)S(1)} %get-tuple-element.57.refs_1_.refs_2_, ...), custom_call_target="tpu_custom_call" | custom-call | flops 3000000000 | bytes 9000000 | tf_op jit(solution)/shard_map/pallas_call | solution.py:41
  23.4 4.4 %collective-permute-done.4.refs_4_ = f32[280,128]{1,0:T(8,128)S(1)} collective-permute-done((f32[280,128]{1,0:T(8,128)S(1)}, f32[280,128]{1,0:T(8,128)S(1)}, u32[]{:S(2)}, u32[]{:S(2)}) %collective-permute-start.4) | collective-permute-done | bytes 143392 | tf_op jit(solution)/shard_map/ppermute | solution.py:539
  27.8 1.6 %collective-permute-done.5.refs_5_ = f32[280,128]{1,0:T(8,128)S(1)} collective-permute-done((f32[280,128]{1,0:T(8,128)S(1)}, f32[280,128]{1,0:T(8,128)S(1)}, u32[]{:S(2)}, u32[]{:S(2)}) %collective-permute-start.5) | collective-permute-done | bytes 143392 | tf_op jit(solution)/shard_map/ppermute | solution.py:538
  29.4 1.7 %shard_map.72 = (f32[256,1024]{1,0:T(8,128)S(1)}, f32[256,1024]{1,0:T(8,128)S(1)}, f32[256,256]{1,0:T(8,128)S(1)}, f32[8,256]{1,0:T(8,128)S(1)}, f32[152,256]{1,0:T(8,128)S(1)}, /*index=5*/f32[152,256]{1,0:T(8,128)S(1)}) custom-call(f32[8,256]{1,0:T(8,128)S(1)} %get-tuple-element.63.refs_0_, ...), custom_call_target="tpu_custom_call", output_to_operand_aliasing={{0}: (13, {}), {1}: (14, {})} | custom-call | flops 1000000000 | bytes 3000000 | tf_op jit(solution)/shard_map/pallas_call | solution.py:41
  31.0 0.1 collective-permute-start.6
  31.1 1.2 %collective-permute-start.7 = (f32[152,256]{1,0:T(8,128)S(1)}, f32[152,256]{1,0:T(8,128)S(1)}, u32[]{:S(2)}, u32[]{:S(2)}) collective-permute-start(f32[152,256]{1,0:T(8,128)S(1)} %get-tuple-element.80), channel_id=1, source_target_pairs={{0,8},{8,0},{16,24},{24,16},{32,40},{40,32},{48,56},{56,48},{64,72... | collective-permute-start | bytes 466952 | tf_op jit(solution)/shard_map/ppermute | solution.py:528
  32.3 1.3 %shard_map.73 = (f32[256,768]{1,0:T(8,128)S(1)}, f32[128,768]{1,0:T(8,128)S(1)}, f32[128,768]{1,0:T(8,128)S(1)}) custom-call(f32[256,1024]{1,0:T(8,128)S(1)} %get-tuple-element.74.dens, f32[256,1024]{1,0:T(8,128)S(1)} %get-tuple-element.75.value.refs_8_), custom_call_target="tpu_custom_call" | custom-call | flops 1000000000 | bytes 3000000 | tf_op jit(solution)/shard_map/pallas_call | solution.py:41
  33.7 0.6 %collective-permute-start.8 = (f32[128,768]{1,0:T(8,128)S(1)}, f32[128,768]{1,0:T(8,128)S(1)}, u32[]{:S(2)}, u32[]{:S(2)}) collective-permute-start(f32[128,768]{1,0:T(8,128)S(1)} %get-tuple-element.82), channel_id=1, source_target_pairs={{8,16},{16,8},{24,32},{32,24},{40,48},{48,40},{56,64},{64,56},{72,... | collective-permute-start | bytes 1179656 | tf_op jit(solution)/shard_map/ppermute | solution.py:529
  34.3 2.5 %collective-permute-start.9 = (f32[128,768]{1,0:T(8,128)S(1)}, f32[128,768]{1,0:T(8,128)S(1)}, u32[]{:S(2)}, u32[]{:S(2)}) collective-permute-start(f32[128,768]{1,0:T(8,128)S(1)} %get-tuple-element.83), channel_id=1, source_target_pairs={{0,8},{8,0},{16,24},{24,16},{32,40},{40,32},{48,56},{56,48},{64,72... | collective-permute-start | bytes 1179656 | tf_op jit(solution)/shard_map/ppermute | solution.py:530
  36.8 0.0 collective-permute-done.6.far
  36.8 0.0 collective-permute-done.7.near
  36.8 0.6 %shard_map.74 = (f32[280,128]{1,0:T(8,128)S(1)}, f32[280,128]{1,0:T(8,128)S(1)}, f32[8,1024]{1,0:T(8,128)S(1)}, f32[8,1024]{1,0:T(8,128)S(1)}, f32[8,768]{1,0:T(8,128)S(1)}, /*index=5*/f32[256,256]{1,0:T(8,128)S(1)}) custom-call(f32[256,1024]{1,0:T(8,128)S(1)} %get-tuple-element.74.dens, f32[256,1024]{1,0:T(8,128)S(1)} %get-tuple-element.75.value.refs_8_, ...), custom_call_target="tpu_custom_call" | custom-call | flops 6000000000 | bytes 18000000 | tf_op jit(solution)/shard_map/pallas_call | solution.py:41
  37.4 1.5 %collective-permute-start.10 = (f32[280,128]{1,0:T(8,128)S(1)}, f32[280,128]{1,0:T(8,128)S(1)}, u32[]{:S(2)}, u32[]{:S(2)}) collective-permute-start(f32[280,128]{1,0:T(8,128)S(1)} %get-tuple-element.87), channel_id=1, source_target_pairs={{0,1},{1,2},{2,3},{3,4},{4,5},{5,6},{6,7},{7,0},{8,9},{9,10},{10,1... | collective-permute-start | bytes 430088 | tf_op jit(solution)/shard_map/ppermute | solution.py:539
  38.9 3.8 %collective-permute-start.11 = (f32[280,128]{1,0:T(8,128)S(1)}, f32[280,128]{1,0:T(8,128)S(1)}, u32[]{:S(2)}, u32[]{:S(2)}) collective-permute-start(f32[280,128]{1,0:T(8,128)S(1)} %get-tuple-element.88), channel_id=1, source_target_pairs={{0,7},{1,0},{2,1},{3,2},{4,3},{5,4},{6,5},{7,6},{8,15},{9,8},{10,9... | collective-permute-start | bytes 430088 | tf_op jit(solution)/shard_map/ppermute | solution.py:538
  42.7 0.0 collective-permute-done.8.refs_2_
  42.7 0.0 collective-permute-done.9.refs_3_
  42.7 3.9 %shard_map.75 = (f32[256,512]{1,0:T(8,128)S(1)}, f32[256,1024]{1,0:T(8,128)S(1)}, f32[8,256]{1,0:T(8,128)S(1)}, f32[256,1024]{1,0:T(8,128)}, f32[256,1024]{1,0:T(8,128)}) custom-call(f32[256,768]{1,0:T(8,128)S(1)} %get-tuple-element.76.refs_0_, f32[8,1024]{1,0:T(8,128)S(1)} %get-tuple-element.81.refs_1_.refs_2_, ...), custom_call_target="tpu_custom_call" | custom-call | flops 3000000000 | bytes 9000000 | tf_op jit(solution)/shard_map/pallas_call | solution.py:41
  46.6 1.1 %collective-permute-done.10.refs_4_ = f32[280,128]{1,0:T(8,128)S(1)} collective-permute-done((f32[280,128]{1,0:T(8,128)S(1)}, f32[280,128]{1,0:T(8,128)S(1)}, u32[]{:S(2)}, u32[]{:S(2)}) %collective-permute-start.10) | collective-permute-done | bytes 143392 | tf_op jit(solution)/shard_map/ppermute | solution.py:539
  47.7 2.0 %collective-permute-done.11.refs_5_ = f32[280,128]{1,0:T(8,128)S(1)} collective-permute-done((f32[280,128]{1,0:T(8,128)S(1)}, f32[280,128]{1,0:T(8,128)S(1)}, u32[]{:S(2)}, u32[]{:S(2)}) %collective-permute-start.11) | collective-permute-done | bytes 143392 | tf_op jit(solution)/shard_map/ppermute | solution.py:538
  49.7 1.9 %shard_map.76 = (f32[256,1024]{1,0:T(8,128)}, f32[256,1024]{1,0:T(8,128)}) custom-call(f32[8,256]{1,0:T(8,128)S(1)} %get-tuple-element.85.refs_0_, f32[256,256]{1,0:T(8,128)S(1)} %get-tuple-element.77.side.refs_1_, f32[8,1024]{1,0:T(8,128)S(1)} %get-tuple-element.81.refs_1_.refs_2_, ...), custom_call_target="tpu_custom_call", output_to_operand_aliasing={{0}: (13, {}), {1}: (14, {})} | custom-call | flops 1000000000 | bytes 3000000 | tf_op jit(solution)/shard_map/pallas_call | solution.py:41
Async XLA Ops:
  0.6 9.8 %copy-start.2 = (f32[256]{0:T(256)S(1)}, f32[256]{0:T(256)}, u32[]{:S(2)}) copy-start(f32[256]{0:T(256)} %param.9) | copy-start | bytes 3076
  2.7 11.3 %collective-permute-start = (f32[152,256]{1,0:T(8,128)S(1)}, f32[152,256]{1,0:T(8,128)S(1)}, u32[]{:S(2)}, u32[]{:S(2)}) collective-permute-start(f32[152,256]{1,0:T(8,128)S(1)} %get-tuple-element.53), channel_id=1, source_target_pairs={{8,16},{16,8},{24,32},{32,24},{40,48},{48,40},{56,64},{64,56},{72,... | collective-permute-start | bytes 466952 | tf_op jit(solution)/shard_map/ppermute | solution.py:527
  5.8 8.2 %collective-permute-start.1 = (f32[152,256]{1,0:T(8,128)S(1)}, f32[152,256]{1,0:T(8,128)S(1)}, u32[]{:S(2)}, u32[]{:S(2)}) collective-permute-start(f32[152,256]{1,0:T(8,128)S(1)} %get-tuple-element.54), channel_id=1, source_target_pairs={{0,8},{8,0},{16,24},{24,16},{32,40},{40,32},{48,56},{56,48},{64,72... | collective-permute-start | bytes 466952 | tf_op jit(solution)/shard_map/ppermute | solution.py:528
  10.5 0.7 %copy-start.1 = (f32[256]{0:T(256)S(1)}, f32[256]{0:T(256)}, u32[]{:S(2)}) copy-start(f32[256]{0:T(256)} %param.8) | copy-start | bytes 3076
  12.7 7.6 %collective-permute-start.2 = (f32[128,768]{1,0:T(8,128)S(1)}, f32[128,768]{1,0:T(8,128)S(1)}, u32[]{:S(2)}, u32[]{:S(2)}) collective-permute-start(f32[128,768]{1,0:T(8,128)S(1)} %get-tuple-element.58), channel_id=1, source_target_pairs={{8,16},{16,8},{24,32},{32,24},{40,48},{48,40},{56,64},{64,56},{72,... | collective-permute-start | bytes 1179656 | tf_op jit(solution)/shard_map/ppermute | solution.py:529
  12.8 7.5 %collective-permute-start.3 = (f32[128,768]{1,0:T(8,128)S(1)}, f32[128,768]{1,0:T(8,128)S(1)}, u32[]{:S(2)}, u32[]{:S(2)}) collective-permute-start(f32[128,768]{1,0:T(8,128)S(1)} %get-tuple-element.59), channel_id=1, source_target_pairs={{0,8},{8,0},{16,24},{24,16},{32,40},{40,32},{48,56},{56,48},{64,72... | collective-permute-start | bytes 1179656 | tf_op jit(solution)/shard_map/ppermute | solution.py:530
  13.9 6.4 %copy-start = (f32[256,1024]{1,0:T(8,128)S(1)}, f32[256,1024]{1,0:T(8,128)}, u32[]{:S(2)}) copy-start(f32[256,1024]{1,0:T(8,128)} %refs_9_.3) | copy-start | bytes 3145732
  14.5 13.3 %collective-permute-start.4 = (f32[280,128]{1,0:T(8,128)S(1)}, f32[280,128]{1,0:T(8,128)S(1)}, u32[]{:S(2)}, u32[]{:S(2)}) collective-permute-start(f32[280,128]{1,0:T(8,128)S(1)} %get-tuple-element.65), channel_id=1, source_target_pairs={{0,1},{1,2},{2,3},{3,4},{4,5},{5,6},{6,7},{7,0},{8,9},{9,10},{10,1... | collective-permute-start | bytes 430088 | tf_op jit(solution)/shard_map/ppermute | solution.py:539
  17.0 12.3 %collective-permute-start.5 = (f32[280,128]{1,0:T(8,128)S(1)}, f32[280,128]{1,0:T(8,128)S(1)}, u32[]{:S(2)}, u32[]{:S(2)}) collective-permute-start(f32[280,128]{1,0:T(8,128)S(1)} %get-tuple-element.66), channel_id=1, source_target_pairs={{0,7},{1,0},{2,1},{3,2},{4,3},{5,4},{6,5},{7,6},{8,15},{9,8},{10,9... | collective-permute-start | bytes 430088 | tf_op jit(solution)/shard_map/ppermute | solution.py:538
  31.0 5.8 %collective-permute-start.6 = (f32[152,256]{1,0:T(8,128)S(1)}, f32[152,256]{1,0:T(8,128)S(1)}, u32[]{:S(2)}, u32[]{:S(2)}) collective-permute-start(f32[152,256]{1,0:T(8,128)S(1)} %get-tuple-element.79), channel_id=1, source_target_pairs={{8,16},{16,8},{24,32},{32,24},{40,48},{48,40},{56,64},{64,56},{72,... | collective-permute-start | bytes 466952 | tf_op jit(solution)/shard_map/ppermute | solution.py:527
  31.1 5.7 %collective-permute-start.7 = (f32[152,256]{1,0:T(8,128)S(1)}, f32[152,256]{1,0:T(8,128)S(1)}, u32[]{:S(2)}, u32[]{:S(2)}) collective-permute-start(f32[152,256]{1,0:T(8,128)S(1)} %get-tuple-element.80), channel_id=1, source_target_pairs={{0,8},{8,0},{16,24},{24,16},{32,40},{40,32},{48,56},{56,48},{64,72... | collective-permute-start | bytes 466952 | tf_op jit(solution)/shard_map/ppermute | solution.py:528
  33.7 9.1 %collective-permute-start.8 = (f32[128,768]{1,0:T(8,128)S(1)}, f32[128,768]{1,0:T(8,128)S(1)}, u32[]{:S(2)}, u32[]{:S(2)}) collective-permute-start(f32[128,768]{1,0:T(8,128)S(1)} %get-tuple-element.82), channel_id=1, source_target_pairs={{8,16},{16,8},{24,32},{32,24},{40,48},{48,40},{56,64},{64,56},{72,... | collective-permute-start | bytes 1179656 | tf_op jit(solution)/shard_map/ppermute | solution.py:529
  34.3 8.5 %collective-permute-start.9 = (f32[128,768]{1,0:T(8,128)S(1)}, f32[128,768]{1,0:T(8,128)S(1)}, u32[]{:S(2)}, u32[]{:S(2)}) collective-permute-start(f32[128,768]{1,0:T(8,128)S(1)} %get-tuple-element.83), channel_id=1, source_target_pairs={{0,8},{8,0},{16,24},{24,16},{32,40},{40,32},{48,56},{56,48},{64,72... | collective-permute-start | bytes 1179656 | tf_op jit(solution)/shard_map/ppermute | solution.py:530
  37.4 10.3 %collective-permute-start.10 = (f32[280,128]{1,0:T(8,128)S(1)}, f32[280,128]{1,0:T(8,128)S(1)}, u32[]{:S(2)}, u32[]{:S(2)}) collective-permute-start(f32[280,128]{1,0:T(8,128)S(1)} %get-tuple-element.87), channel_id=1, source_target_pairs={{0,1},{1,2},{2,3},{3,4},{4,5},{5,6},{6,7},{7,0},{8,9},{9,10},{10,1... | collective-permute-start | bytes 430088 | tf_op jit(solution)/shard_map/ppermute | solution.py:539
  38.9 10.8 %collective-permute-start.11 = (f32[280,128]{1,0:T(8,128)S(1)}, f32[280,128]{1,0:T(8,128)S(1)}, u32[]{:S(2)}, u32[]{:S(2)}) collective-permute-start(f32[280,128]{1,0:T(8,128)S(1)} %get-tuple-element.88), channel_id=1, source_target_pairs={{0,7},{1,0},{2,1},{3,2},{4,3},{5,4},{6,5},{7,6},{8,15},{9,8},{10,9... | collective-permute-start | bytes 430088 | tf_op jit(solution)/shard_map/ppermute | solution.py:538

commit v5 on v4

--- a/solution.py
+++ b/solution.py
@@ -70,17 +70,17 @@
     refs[0][...], refs[1][...] = split(x)
 
 
-def band_tables(kern_rows, kern_cols, rows_hi, rows_lo, turned_hi, turned_lo, cols_hi, cols_lo):
-    for kern, refs in ((kern_rows, (turned_hi, turned_lo)), (kern_cols, (cols_hi, cols_lo))):
-        row = jnp.concatenate([jnp.zeros((1, 2 * KW), F32), kern[...]], axis=1)
-        full = jnp.broadcast_to(row, (2 * KW, 3 * KW))
-        table = pltpu.roll(full, 0, 1, stride=1, stride_axis=0)[:, :KW]
-        put_split(refs, table)
-        if kern is kern_rows:
-            put_split((rows_hi, rows_lo), table.T)
-
-
-TABLES = [shape(KW, 2 * KW, kind=BF16)] * 2 + [shape(2 * KW, KW, kind=BF16)] * 4
+def band(kern, turned, rows=None):
+    row = jnp.concatenate([jnp.zeros((1, 2 * KW), F32), kern[...]], axis=1)
+    full = jnp.broadcast_to(row, (2 * KW, 3 * KW))
+    table = pltpu.roll(full, 0, 1, stride=1, stride_axis=0)[:, :KW]
+    put_split(turned, table)
+    if rows is not None:
+        put_split(rows, table.T)
+
+
+ROWS_TABLE = [shape(KW, 2 * KW, kind=BF16)] * 2
+TURNED_TABLE = [shape(2 * KW, KW, kind=BF16)] * 2
 
 
 def flux(a, here, there):
@@ -255,17 +255,9 @@
     cost_t[2:4, :] = potential[:, FROM_R:COLS].T[EDGE - 2 : EDGE, :]
 
 
-def first_rest_kernel(dens, value, kern_rows, kern_cols, new, far, near, *refs):
-    copies = [
-        pltpu.make_async_copy(source, target, refs[8].at[n])
-        for n, (source, target) in enumerate(((kern_rows, refs[6]), (kern_cols, refs[7])))
-    ]
-    for copy in copies:
-        copy.start()
+def first_rest_kernel(dens, value, kern_rows, new, far, near, *table):
     rest_kernel(dens, value, new, far, near)
-    for copy in copies:
-        copy.wait()
-    band_tables(refs[6], refs[7], *refs[:6])
+    band(kern_rows, table[2:4], table[0:2])
 
 
 def halo_rows(ext, far, near):
@@ -352,12 +344,13 @@
     put_seams(ext, seams, ((slice(0, MID), slice(EDGE, FROM_R)),))
 
 
-def middle_kernel(*refs):
-    new, seams, far, near = refs[:4]
-    value, potential, around = refs[8:11]
-    cong_s, inner, cost_t, dens_out, value_out, ext, mix_hi, mix_lo, cong_m = refs[11:]
+def first_middle_kernel(*refs):
+    new, seams, far, near, rows_hi, rows_lo, kern_cols, value, potential, around = refs[:10]
+    cong_s, inner, cost_t, dens_out, value_out, cols_hi, cols_lo, ext, mix_hi, mix_lo, cong_m = refs[10:]
+    band(kern_cols, (cols_hi, cols_lo))
+    table = (rows_hi, rows_lo, cols_hi, cols_lo)
     middle_ext(new, seams, far, near, ext)
-    middle_mix(*refs[:8], cong_s, cong_m, ext, mix_hi, mix_lo)
+    middle_mix(new, seams, far, near, *table, cong_s, cong_m, ext, mix_hi, mix_lo)
     turned_cost(potential, cost_t)
     inner_value(value, potential, inner)
     end_rows(value, potential, around, inner)
@@ -416,24 +409,8 @@
     def column(n):
         return columns[:, n : n + 1]
 
-    lane = lax.broadcasted_iota(jnp.int32, (ROWS, 2 * EDGE), 1)
-    before = (cols_hi[0:KW, :], cols_lo[0:KW, :])
-    after = (cols_hi[KW : 2 * KW, :], cols_lo[KW : 2 * KW, :])
-    low = jnp.concatenate([left[0:ROWS, :], mixed[:, 0:EDGE]], axis=1)
-    low = jnp.where(lane == EDGE - 1, column(1), jnp.where(lane == EDGE, column(2), low))
-    low = cong[:, 0:256] + product(split(low), before)
-    high = jnp.concatenate([mixed[:, EDGE : 2 * EDGE], right[0:ROWS, :]], axis=1)
-    high = jnp.where(lane == EDGE - 1, column(5), jnp.where(lane == EDGE, column(6), high))
-    high = cong[:, 256:512] + product(split(high), after)
-
     lane = lax.broadcasted_iota(jnp.int32, (ROWS, EDGE), 1)
     row = lax.broadcasted_iota(jnp.int32, (ROWS, EDGE), 0)
-    put_value(1, inner[:, EDGE : 2 * EDGE] + DT * low[:, EDGE : 2 * EDGE])
-    put_value(2, inner[:, FROM_R - EDGE : FROM_R] + DT * high[:, 0:EDGE])
-    put_value(0, jnp.where(lane == 0, column(18), inner[:, 0:EDGE]) + DT * low[:, 0:EDGE])
-    put_value(
-        3, jnp.where(lane == EDGE - 1, column(21), inner[:, FROM_R:COLS]) + DT * high[:, EDGE : 2 * EDGE]
-    )
     for block, lanes, from_side, at, n in (
         (0, slice(0, EDGE), slice(0, EDGE), 0, 10),
         (3, slice(FROM_R, COLS), slice(EDGE, 2 * EDGE), EDGE - 1, 13),
@@ -441,6 +418,29 @@
         x = jnp.where(row == 0, seams[2:3, lanes], side[:, from_side])
         x = jnp.where(row == ROWS - 1, seams[5:6, lanes], x)
         put_dens(block, jnp.where(lane == at, column(n), x))
+    lane = lax.broadcasted_iota(jnp.int32, (ROWS, 2 * EDGE), 1)
+    known = jnp.logical_and(lane != EDGE - 1, lane != EDGE)
+    before = (cols_hi[0:KW, :], cols_lo[0:KW, :])
+    after = (cols_hi[KW : 2 * KW, :], cols_lo[KW : 2 * KW, :])
+
+    def table_row(n):
+        base = n // 16 * 16
+        rows = cols_hi[base : base + 16, :].astype(F32) + cols_lo[base : base + 16, :].astype(F32)
+        return rows[n - base : n - base + 1, :]
+
+    low = jnp.where(known, jnp.concatenate([left[0:ROWS, :], mixed[:, 0:EDGE]], axis=1), 0.0)
+    low = cong[:, 0:256] + product(split(low), before)
+    low = low + (column(1) * table_row(EDGE - 1) + column(2) * table_row(EDGE))
+    half = lax.broadcasted_iota(jnp.int32, (ROWS, EDGE), 1)
+    put_value(1, inner[:, EDGE : 2 * EDGE] + DT * low[:, EDGE : 2 * EDGE])
+    put_value(0, jnp.where(half == 0, column(18), inner[:, 0:EDGE]) + DT * low[:, 0:EDGE])
+    high = jnp.where(known, jnp.concatenate([mixed[:, EDGE : 2 * EDGE], right[0:ROWS, :]], axis=1), 0.0)
+    high = cong[:, 256:512] + product(split(high), after)
+    high = high + (column(5) * table_row(KW + EDGE - 1) + column(6) * table_row(KW + EDGE))
+    put_value(2, inner[:, FROM_R - EDGE : FROM_R] + DT * high[:, 0:EDGE])
+    put_value(
+        3, jnp.where(half == EDGE - 1, column(21), inner[:, FROM_R:COLS]) + DT * high[:, EDGE : 2 * EDGE]
+    )
 
 
 FINISH_SCRATCH = [
@@ -514,14 +514,9 @@
         last = step_index == STEPS - 1
         if step_index == 0:
             new, far_2, near_2, *table = call(
-                first_rest_kernel,
-                SECOND + TABLES,
-                [pltpu.VMEM((1, KW), F32), pltpu.VMEM((1, KW), F32), pltpu.SemaphoreType.DMA((2,))],
-                1,
-                dens, value, kern_rows[None], kern_cols[None],
-                hbm_in=(2, 3),
+                first_rest_kernel, SECOND + ROWS_TABLE + TURNED_TABLE, [], 1, dens, value, kern_rows[None]
             )
-            rows_table, turned_table, cols_table = table[0:2], table[2:4], table[4:6]
+            rows_table, turned_table = table[0:2], table[2:4]
         else:
             new, far_2, near_2 = call(rest_kernel, SECOND, [], 1, dens, value)
         far_1 = lax.ppermute(far_1, "rows", far_pairs)
@@ -545,14 +540,24 @@
         ]
         if last:
             scratch += [pltpu.VMEM((ROWS, INSIDE_N), F32), pltpu.SemaphoreType.DMA((2,))]
-        cong, inner, cost_t, *results = call(
-            last_middle_kernel if last else middle_kernel,
-            [shape(ROWS, 4 * EDGE), BLOCK, shape(8, ROWS), BLOCK, BLOCK],
-            scratch,
-            3,
-            new, seams, far_2, near_2, *rows_table, *cols_table, value, potential, around,
-            hbm_out=(3, 4) if last else (),
-        )
+        if last:
+            cong, inner, cost_t, *results = call(
+                last_middle_kernel,
+                [shape(ROWS, 4 * EDGE), BLOCK, shape(8, ROWS), BLOCK, BLOCK],
+                scratch,
+                3,
+                new, seams, far_2, near_2, *rows_table, *cols_table, value, potential, around,
+                hbm_out=(3, 4),
+            )
+        else:
+            cong, inner, cost_t, dens_out, value_out, *cols_table = call(
+                first_middle_kernel,
+                [shape(ROWS, 4 * EDGE), BLOCK, shape(8, ROWS), BLOCK, BLOCK] + TURNED_TABLE,
+                scratch,
+                3,
+                new, seams, far_2, near_2, *rows_table, kern_cols[None], value, potential, around,
+            )
+            results = [dens_out, value_out]
         operands = (cost_t, side, seams, tall, left_in, right_in, mixed, cong, inner, *turned_table, *cols_table, *results)
         if last:
             scratch = [pltpu.VMEM((ROWS, 4 * EDGE), F32), pltpu.VMEM((ROWS, 4 * EDGE), F32)]

time: 51.9 us -> 51.6 us (level)
  waiting for transfers between devices: 9.69 us -> 9 us
  local copies, waits for them, and re-layouts: 0.68 us -> 1.36 us
    ppermute x2, waiting for transfers between devices: 5.51 us -> 4.83 us  [body(): left_in = lax.ppermute(right, 'cols', to_right)]
    unnamed x6, local copies, waits for them, and re-layouts: 0.68 us -> 1.36 us
where the time goes in v5:
time: 51.6 us; the launch traced here: 51.5 us
  starting transfers between devices  24 us (47%)
  Pallas kernels  16.3 us (32%)
  waiting for transfers between devices  9 us (17%)
  local copies, waits for them, and re-layouts  1.36 us (3%)
  between operations  0.89 us (2%)
    pallas_call x9, Pallas kernels, call(): pl.pallas_call(kernel, out_shape=out_shapes, in_specs=[HBM if n in hbm_in...  16.3 us
    ppermute x2, starting transfers between devices, body(): right_in = lax.ppermute(left, 'cols', to_left)  6.47 us
    ppermute x2, starting transfers between devices, body(): near_1 = lax.ppermute(near_1, 'rows', near_pairs)  5.91 us
    ppermute x2, waiting for transfers between devices, body(): left_in = lax.ppermute(right, 'cols', to_right)  4.83 us
    ppermute x2, starting transfers between devices, body(): left_in = lax.ppermute(right, 'cols', to_right)  4.03 us
    ppermute x2, starting transfers between devices, body(): near_2 = lax.ppermute(near_2, 'rows', near_pairs)  3.65 us
    ppermute x2, waiting for transfers between devices, body(): right_in = lax.ppermute(left, 'cols', to_left)  3.53 us
    ppermute x2, starting transfers between devices, body(): far_1 = lax.ppermute(far_1, 'rows', far_pairs)  3.21 us
  transfers between devices with their start and end apart: 12, of which 5 were waited for; matrix products, arithmetic and copies ran while one was open for 0% of the time, Pallas kernels for 21%

profile of v5, /device:TPU:1, one launch (start us, length us, event | category | flops | bytes accessed | tf_op | source)
XLA Modules:
  0.0 51.5 jit_solution(18364793671481325651)
XLA Ops:
  0.6 2.0 %shard_map.68 = (f32[256,1024]{1,0:T(8,128)S(1)}, f32[256,1024]{1,0:T(8,128)S(1)}, f32[256,256]{1,0:T(8,128)S(1)}, f32[8,256]{1,0:T(8,128)S(1)}, f32[152,256]{1,0:T(8,128)S(1)}, /*index=5*/f32[152,256]{1,0:T(8,128)S(1)}) custom-call(f32[256,1024]{1,0:T(8,128)} %dens_in.1, f32[256,1024]{1,0:T(8,128)} %value_in.1), custom_call_target="tpu_custom_call" | custom-call | flops 1000000000 | bytes 3000000 | tf_op jit(solution)/shard_map/pallas_call | solution.py:41
  2.6 3.1 %collective-permute-start = (f32[152,256]{1,0:T(8,128)S(1)}, f32[152,256]{1,0:T(8,128)S(1)}, u32[]{:S(2)}, u32[]{:S(2)}) collective-permute-start(f32[152,256]{1,0:T(8,128)S(1)} %get-tuple-element.53), channel_id=1, source_target_pairs={{8,16},{16,8},{24,32},{32,24},{40,48},{48,40},{56,64},{64,56},{72,... | collective-permute-start | bytes 466952 | tf_op jit(solution)/shard_map/ppermute | solution.py:522
  5.8 4.7 %collective-permute-start.1 = (f32[152,256]{1,0:T(8,128)S(1)}, f32[152,256]{1,0:T(8,128)S(1)}, u32[]{:S(2)}, u32[]{:S(2)}) collective-permute-start(f32[152,256]{1,0:T(8,128)S(1)} %get-tuple-element.54), channel_id=1, source_target_pairs={{0,8},{8,0},{16,24},{24,16},{32,40},{40,32},{48,56},{56,48},{64,72... | collective-permute-start | bytes 466952 | tf_op jit(solution)/shard_map/ppermute | solution.py:523
  10.5 0.0 copy-start.1
  10.5 0.7 %copy-done.1 = f32[256]{0:T(256)S(1)} copy-done((f32[256]{0:T(256)S(1)}, f32[256]{0:T(256)}, u32[]{:S(2)}) %copy-start.1) | copy-done | bytes 1048
  11.1 1.4 %shard_map.69 = (f32[256,768]{1,0:T(8,128)S(1)}, f32[128,768]{1,0:T(8,128)S(1)}, f32[128,768]{1,0:T(8,128)S(1)}, bf16[256,512]{1,0:T(8,128)(2,1)S(1)}, bf16[256,...) custom-call(f32[256,1024]{1,0:T(8,128)S(1)} %get-tuple-element.48.dens, ...), custom_call_target="tpu_custom_call" | custom-call | flops 1000000000 | bytes 3000000 | tf_op jit(solution)/shard_map/pallas_call | solution.py:41
  12.6 0.1 collective-permute-start.2
  12.7 1.1 %collective-permute-start.3 = (f32[128,768]{1,0:T(8,128)S(1)}, f32[128,768]{1,0:T(8,128)S(1)}, u32[]{:S(2)}, u32[]{:S(2)}) collective-permute-start(f32[128,768]{1,0:T(8,128)S(1)} %get-tuple-element.59), channel_id=1, source_target_pairs={{0,8},{8,0},{16,24},{24,16},{32,40},{40,32},{48,56},{56,48},{64,72... | collective-permute-start | bytes 1179656 | tf_op jit(solution)/shard_map/ppermute | solution.py:525
  13.8 0.0 collective-permute-done.far
  13.8 0.0 collective-permute-done.1.near
  13.8 0.0 copy-start
  13.8 0.6 %shard_map.70 = (f32[280,128]{1,0:T(8,128)S(1)}, f32[280,128]{1,0:T(8,128)S(1)}, f32[8,1024]{1,0:T(8,128)S(1)}, f32[8,1024]{1,0:T(8,128)S(1)}, f32[8,768]{1,0:T(8,128)S(1)}, /*index=5*/f32[256,256]{1,0:T(8,128)S(1)}) custom-call(f32[256,1024]{1,0:T(8,128)S(1)} %get-tuple-element.48.dens, f32[256,1024]{1,0:T(8,128)S(1)} %get-tuple-element.49.value.refs_7_, ...), custom_call_target="tpu_custom_call" | custom-call | flops 6000000000 | bytes 18000000 | tf_op jit(solution)/shard_map/pallas_call | solution.py:41
  14.4 2.5 %collective-permute-start.4 = (f32[280,128]{1,0:T(8,128)S(1)}, f32[280,128]{1,0:T(8,128)S(1)}, u32[]{:S(2)}, u32[]{:S(2)}) collective-permute-start(f32[280,128]{1,0:T(8,128)S(1)} %get-tuple-element.63), channel_id=1, source_target_pairs={{0,1},{1,2},{2,3},{3,4},{4,5},{5,6},{6,7},{7,0},{8,9},{9,10},{10,1... | collective-permute-start | bytes 430088 | tf_op jit(solution)/shard_map/ppermute | solution.py:534
  16.9 2.6 %collective-permute-start.5 = (f32[280,128]{1,0:T(8,128)S(1)}, f32[280,128]{1,0:T(8,128)S(1)}, u32[]{:S(2)}, u32[]{:S(2)}) collective-permute-start(f32[280,128]{1,0:T(8,128)S(1)} %get-tuple-element.64), channel_id=1, source_target_pairs={{0,7},{1,0},{2,1},{3,2},{4,3},{5,4},{6,5},{7,6},{8,15},{9,8},{10,9... | collective-permute-start | bytes 430088 | tf_op jit(solution)/shard_map/ppermute | solution.py:533
  19.5 0.6 %collective-permute-done.2.refs_2_ = f32[128,768]{1,0:T(8,128)S(1)} collective-permute-done((f32[128,768]{1,0:T(8,128)S(1)}, f32[128,768]{1,0:T(8,128)S(1)}, u32[]{:S(2)}, u32[]{:S(2)}) %collective-permute-start.2) | collective-permute-done | bytes 393248 | tf_op jit(solution)/shard_map/ppermute | solution.py:524
  20.1 0.0 collective-permute-done.3.refs_3_
  20.1 0.0 copy-start.2
  20.2 0.0 copy-done
  20.2 0.7 %copy-done.2 = f32[256]{0:T(256)S(1)} copy-done((f32[256]{0:T(256)S(1)}, f32[256]{0:T(256)}, u32[]{:S(2)}) %copy-start.2) | copy-done | bytes 1048
  20.8 3.1 %shard_map.71 = (f32[256,512]{1,0:T(8,128)S(1)}, f32[256,1024]{1,0:T(8,128)S(1)}, f32[8,256]{1,0:T(8,128)S(1)}, f32[256,1024]{1,0:T(8,128)S(1)}, f32[256,1024]{1...) custom-call(f32[256,768]{1,0:T(8,128)S(1)} %get-tuple-element.50.refs_0_, ...), custom_call_target="tpu_custom_call" | custom-call | flops 3000000000 | bytes 9000000 | tf_op jit(solution)/shard_map/pallas_call | solution.py:41
  23.9 3.7 %collective-permute-done.4.refs_4_ = f32[280,128]{1,0:T(8,128)S(1)} collective-permute-done((f32[280,128]{1,0:T(8,128)S(1)}, f32[280,128]{1,0:T(8,128)S(1)}, u32[]{:S(2)}, u32[]{:S(2)}) %collective-permute-start.4) | collective-permute-done | bytes 143392 | tf_op jit(solution)/shard_map/ppermute | solution.py:534
  27.6 1.6 %collective-permute-done.5.refs_5_ = f32[280,128]{1,0:T(8,128)S(1)} collective-permute-done((f32[280,128]{1,0:T(8,128)S(1)}, f32[280,128]{1,0:T(8,128)S(1)}, u32[]{:S(2)}, u32[]{:S(2)}) %collective-permute-start.5) | collective-permute-done | bytes 143392 | tf_op jit(solution)/shard_map/ppermute | solution.py:533
  29.2 1.5 %shard_map.72 = (f32[256,1024]{1,0:T(8,128)S(1)}, f32[256,1024]{1,0:T(8,128)S(1)}, f32[256,256]{1,0:T(8,128)S(1)}, f32[8,256]{1,0:T(8,128)S(1)}, f32[152,256]{1,0:T(8,128)S(1)}, /*index=5*/f32[152,256]{1,0:T(8,128)S(1)}) custom-call(f32[8,256]{1,0:T(8,128)S(1)} %get-tuple-element.61.refs_0_, ...), custom_call_target="tpu_custom_call", output_to_operand_aliasing={{0}: (13, {}), {1}: (14, {})} | custom-call | flops 1000000000 | bytes 3000000 | tf_op jit(solution)/shard_map/pallas_call | solution.py:41
  30.7 0.1 collective-permute-start.6
  30.8 1.2 %collective-permute-start.7 = (f32[152,256]{1,0:T(8,128)S(1)}, f32[152,256]{1,0:T(8,128)S(1)}, u32[]{:S(2)}, u32[]{:S(2)}) collective-permute-start(f32[152,256]{1,0:T(8,128)S(1)} %get-tuple-element.80), channel_id=1, source_target_pairs={{0,8},{8,0},{16,24},{24,16},{32,40},{40,32},{48,56},{56,48},{64,72... | collective-permute-start | bytes 466952 | tf_op jit(solution)/shard_map/ppermute | solution.py:523
  32.0 1.3 %shard_map.73 = (f32[256,768]{1,0:T(8,128)S(1)}, f32[128,768]{1,0:T(8,128)S(1)}, f32[128,768]{1,0:T(8,128)S(1)}) custom-call(f32[256,1024]{1,0:T(8,128)S(1)} %get-tuple-element.74.dens, f32[256,1024]{1,0:T(8,128)S(1)} %get-tuple-element.75.value.refs_8_), custom_call_target="tpu_custom_call" | custom-call | flops 1000000000 | bytes 3000000 | tf_op jit(solution)/shard_map/pallas_call | solution.py:41
  33.4 0.6 %collective-permute-start.8 = (f32[128,768]{1,0:T(8,128)S(1)}, f32[128,768]{1,0:T(8,128)S(1)}, u32[]{:S(2)}, u32[]{:S(2)}) collective-permute-start(f32[128,768]{1,0:T(8,128)S(1)} %get-tuple-element.82), channel_id=1, source_target_pairs={{8,16},{16,8},{24,32},{32,24},{40,48},{48,40},{56,64},{64,56},{72,... | collective-permute-start | bytes 1179656 | tf_op jit(solution)/shard_map/ppermute | solution.py:524
  34.0 2.5 %collective-permute-start.9 = (f32[128,768]{1,0:T(8,128)S(1)}, f32[128,768]{1,0:T(8,128)S(1)}, u32[]{:S(2)}, u32[]{:S(2)}) collective-permute-start(f32[128,768]{1,0:T(8,128)S(1)} %get-tuple-element.83), channel_id=1, source_target_pairs={{0,8},{8,0},{16,24},{24,16},{32,40},{40,32},{48,56},{56,48},{64,72... | collective-permute-start | bytes 1179656 | tf_op jit(solution)/shard_map/ppermute | solution.py:525
  36.5 0.0 collective-permute-done.6.far
  36.5 0.0 collective-permute-done.7.near
  36.5 0.6 %shard_map.74 = (f32[280,128]{1,0:T(8,128)S(1)}, f32[280,128]{1,0:T(8,128)S(1)}, f32[8,1024]{1,0:T(8,128)S(1)}, f32[8,1024]{1,0:T(8,128)S(1)}, f32[8,768]{1,0:T(8,128)S(1)}, /*index=5*/f32[256,256]{1,0:T(8,128)S(1)}) custom-call(f32[256,1024]{1,0:T(8,128)S(1)} %get-tuple-element.74.dens, f32[256,1024]{1,0:T(8,128)S(1)} %get-tuple-element.75.value.refs_8_, ...), custom_call_target="tpu_custom_call" | custom-call | flops 6000000000 | bytes 18000000 | tf_op jit(solution)/shard_map/pallas_call | solution.py:41
  37.1 1.5 %collective-permute-start.10 = (f32[280,128]{1,0:T(8,128)S(1)}, f32[280,128]{1,0:T(8,128)S(1)}, u32[]{:S(2)}, u32[]{:S(2)}) collective-permute-start(f32[280,128]{1,0:T(8,128)S(1)} %get-tuple-element.87), channel_id=1, source_target_pairs={{0,1},{1,2},{2,3},{3,4},{4,5},{5,6},{6,7},{7,0},{8,9},{9,10},{10,1... | collective-permute-start | bytes 430088 | tf_op jit(solution)/shard_map/ppermute | solution.py:534
  38.6 3.8 %collective-permute-start.11 = (f32[280,128]{1,0:T(8,128)S(1)}, f32[280,128]{1,0:T(8,128)S(1)}, u32[]{:S(2)}, u32[]{:S(2)}) collective-permute-start(f32[280,128]{1,0:T(8,128)S(1)} %get-tuple-element.88), channel_id=1, source_target_pairs={{0,7},{1,0},{2,1},{3,2},{4,3},{5,4},{6,5},{7,6},{8,15},{9,8},{10,9... | collective-permute-start | bytes 430088 | tf_op jit(solution)/shard_map/ppermute | solution.py:533
  42.4 0.0 collective-permute-done.8.refs_2_
  42.4 0.0 collective-permute-done.9.refs_3_
  42.4 3.9 %shard_map.75 = (f32[256,512]{1,0:T(8,128)S(1)}, f32[256,1024]{1,0:T(8,128)S(1)}, f32[8,256]{1,0:T(8,128)S(1)}, f32[256,1024]{1,0:T(8,128)}, f32[256,1024]{1,0:T(8,128)}) custom-call(f32[256,768]{1,0:T(8,128)S(1)} %get-tuple-element.76.refs_0_, f32[8,1024]{1,0:T(8,128)S(1)} %get-tuple-element.81.refs_1_.refs_2_, ...), custom_call_target="tpu_custom_call" | custom-call | flops 3000000000 | bytes 9000000 | tf_op jit(solution)/shard_map/pallas_call | solution.py:41
  46.4 1.1 %collective-permute-done.10.refs_4_ = f32[280,128]{1,0:T(8,128)S(1)} collective-permute-done((f32[280,128]{1,0:T(8,128)S(1)}, f32[280,128]{1,0:T(8,128)S(1)}, u32[]{:S(2)}, u32[]{:S(2)}) %collective-permute-start.10) | collective-permute-done | bytes 143392 | tf_op jit(solution)/shard_map/ppermute | solution.py:534
  47.5 2.0 %collective-permute-done.11.refs_5_ = f32[280,128]{1,0:T(8,128)S(1)} collective-permute-done((f32[280,128]{1,0:T(8,128)S(1)}, f32[280,128]{1,0:T(8,128)S(1)}, u32[]{:S(2)}, u32[]{:S(2)}) %collective-permute-start.11) | collective-permute-done | bytes 143392 | tf_op jit(solution)/shard_map/ppermute | solution.py:533
  49.5 1.9 %shard_map.76 = (f32[256,1024]{1,0:T(8,128)}, f32[256,1024]{1,0:T(8,128)}) custom-call(f32[8,256]{1,0:T(8,128)S(1)} %get-tuple-element.85.refs_0_, f32[256,256]{1,0:T(8,128)S(1)} %get-tuple-element.77.side.refs_1_, f32[8,1024]{1,0:T(8,128)S(1)} %get-tuple-element.81.refs_1_.refs_2_, ...), custom_call_target="tpu_custom_call", output_to_operand_aliasing={{0}: (13, {}), {1}: (14, {})} | custom-call | flops 1000000000 | bytes 3000000 | tf_op jit(solution)/shard_map/pallas_call | solution.py:41
Async XLA Ops:
  2.6 11.1 %collective-permute-start = (f32[152,256]{1,0:T(8,128)S(1)}, f32[152,256]{1,0:T(8,128)S(1)}, u32[]{:S(2)}, u32[]{:S(2)}) collective-permute-start(f32[152,256]{1,0:T(8,128)S(1)} %get-tuple-element.53), channel_id=1, source_target_pairs={{8,16},{16,8},{24,32},{32,24},{40,48},{48,40},{56,64},{64,56},{72,... | collective-permute-start | bytes 466952 | tf_op jit(solution)/shard_map/ppermute | solution.py:522
  5.8 8.0 %collective-permute-start.1 = (f32[152,256]{1,0:T(8,128)S(1)}, f32[152,256]{1,0:T(8,128)S(1)}, u32[]{:S(2)}, u32[]{:S(2)}) collective-permute-start(f32[152,256]{1,0:T(8,128)S(1)} %get-tuple-element.54), channel_id=1, source_target_pairs={{0,8},{8,0},{16,24},{24,16},{32,40},{40,32},{48,56},{56,48},{64,72... | collective-permute-start | bytes 466952 | tf_op jit(solution)/shard_map/ppermute | solution.py:523
  10.5 0.7 %copy-start.1 = (f32[256]{0:T(256)S(1)}, f32[256]{0:T(256)}, u32[]{:S(2)}) copy-start(f32[256]{0:T(256)} %param.8) | copy-start | bytes 3076
  12.6 7.6 %collective-permute-start.2 = (f32[128,768]{1,0:T(8,128)S(1)}, f32[128,768]{1,0:T(8,128)S(1)}, u32[]{:S(2)}, u32[]{:S(2)}) collective-permute-start(f32[128,768]{1,0:T(8,128)S(1)} %get-tuple-element.58), channel_id=1, source_target_pairs={{8,16},{16,8},{24,32},{32,24},{40,48},{48,40},{56,64},{64,56},{72,... | collective-permute-start | bytes 1179656 | tf_op jit(solution)/shard_map/ppermute | solution.py:524
  12.7 7.5 %collective-permute-start.3 = (f32[128,768]{1,0:T(8,128)S(1)}, f32[128,768]{1,0:T(8,128)S(1)}, u32[]{:S(2)}, u32[]{:S(2)}) collective-permute-start(f32[128,768]{1,0:T(8,128)S(1)} %get-tuple-element.59), channel_id=1, source_target_pairs={{0,8},{8,0},{16,24},{24,16},{32,40},{40,32},{48,56},{56,48},{64,72... | collective-permute-start | bytes 1179656 | tf_op jit(solution)/shard_map/ppermute | solution.py:525
  13.8 6.4 %copy-start = (f32[256,1024]{1,0:T(8,128)S(1)}, f32[256,1024]{1,0:T(8,128)}, u32[]{:S(2)}) copy-start(f32[256,1024]{1,0:T(8,128)} %refs_9_.1) | copy-start | bytes 3145732
  14.4 13.3 %collective-permute-start.4 = (f32[280,128]{1,0:T(8,128)S(1)}, f32[280,128]{1,0:T(8,128)S(1)}, u32[]{:S(2)}, u32[]{:S(2)}) collective-permute-start(f32[280,128]{1,0:T(8,128)S(1)} %get-tuple-element.63), channel_id=1, source_target_pairs={{0,1},{1,2},{2,3},{3,4},{4,5},{5,6},{6,7},{7,0},{8,9},{9,10},{10,1... | collective-permute-start | bytes 430088 | tf_op jit(solution)/shard_map/ppermute | solution.py:534
  16.9 12.3 %collective-permute-start.5 = (f32[280,128]{1,0:T(8,128)S(1)}, f32[280,128]{1,0:T(8,128)S(1)}, u32[]{:S(2)}, u32[]{:S(2)}) collective-permute-start(f32[280,128]{1,0:T(8,128)S(1)} %get-tuple-element.64), channel_id=1, source_target_pairs={{0,7},{1,0},{2,1},{3,2},{4,3},{5,4},{6,5},{7,6},{8,15},{9,8},{10,9... | collective-permute-start | bytes 430088 | tf_op jit(solution)/shard_map/ppermute | solution.py:533
  20.1 0.7 %copy-start.2 = (f32[256]{0:T(256)S(1)}, f32[256]{0:T(256)}, u32[]{:S(2)}) copy-start(f32[256]{0:T(256)} %param.9) | copy-start | bytes 3076
  30.7 5.8 %collective-permute-start.6 = (f32[152,256]{1,0:T(8,128)S(1)}, f32[152,256]{1,0:T(8,128)S(1)}, u32[]{:S(2)}, u32[]{:S(2)}) collective-permute-start(f32[152,256]{1,0:T(8,128)S(1)} %get-tuple-element.79), channel_id=1, source_target_pairs={{8,16},{16,8},{24,32},{32,24},{40,48},{48,40},{56,64},{64,56},{72,... | collective-permute-start | bytes 466952 | tf_op jit(solution)/shard_map/ppermute | solution.py:522
  30.8 5.7 %collective-permute-start.7 = (f32[152,256]{1,0:T(8,128)S(1)}, f32[152,256]{1,0:T(8,128)S(1)}, u32[]{:S(2)}, u32[]{:S(2)}) collective-permute-start(f32[152,256]{1,0:T(8,128)S(1)} %get-tuple-element.80), channel_id=1, source_target_pairs={{0,8},{8,0},{16,24},{24,16},{32,40},{40,32},{48,56},{56,48},{64,72... | collective-permute-start | bytes 466952 | tf_op jit(solution)/shard_map/ppermute | solution.py:523
  33.4 9.1 %collective-permute-start.8 = (f32[128,768]{1,0:T(8,128)S(1)}, f32[128,768]{1,0:T(8,128)S(1)}, u32[]{:S(2)}, u32[]{:S(2)}) collective-permute-start(f32[128,768]{1,0:T(8,128)S(1)} %get-tuple-element.82), channel_id=1, source_target_pairs={{8,16},{16,8},{24,32},{32,24},{40,48},{48,40},{56,64},{64,56},{72,... | collective-permute-start | bytes 1179656 | tf_op jit(solution)/shard_map/ppermute | solution.py:524
  34.0 8.5 %collective-permute-start.9 = (f32[128,768]{1,0:T(8,128)S(1)}, f32[128,768]{1,0:T(8,128)S(1)}, u32[]{:S(2)}, u32[]{:S(2)}) collective-permute-start(f32[128,768]{1,0:T(8,128)S(1)} %get-tuple-element.83), channel_id=1, source_target_pairs={{0,8},{8,0},{16,24},{24,16},{32,40},{40,32},{48,56},{56,48},{64,72... | collective-permute-start | bytes 1179656 | tf_op jit(solution)/shard_map/ppermute | solution.py:525
  37.1 10.4 %collective-permute-start.10 = (f32[280,128]{1,0:T(8,128)S(1)}, f32[280,128]{1,0:T(8,128)S(1)}, u32[]{:S(2)}, u32[]{:S(2)}) collective-permute-start(f32[280,128]{1,0:T(8,128)S(1)} %get-tuple-element.87), channel_id=1, source_target_pairs={{0,1},{1,2},{2,3},{3,4},{4,5},{5,6},{6,7},{7,0},{8,9},{9,10},{10,1... | collective-permute-start | bytes 430088 | tf_op jit(solution)/shard_map/ppermute | solution.py:534
  38.6 10.9 %collective-permute-start.11 = (f32[280,128]{1,0:T(8,128)S(1)}, f32[280,128]{1,0:T(8,128)S(1)}, u32[]{:S(2)}, u32[]{:S(2)}) collective-permute-start(f32[280,128]{1,0:T(8,128)S(1)} %get-tuple-element.88), channel_id=1, source_target_pairs={{0,7},{1,0},{2,1},{3,2},{4,3},{5,4},{6,5},{7,6},{8,15},{9,8},{10,9... | collective-permute-start | bytes 430088 | tf_op jit(solution)/shard_map/ppermute | solution.py:533

commit v6 on v5

--- a/solution.py
+++ b/solution.py
@@ -9,6 +9,7 @@
 
 STEPS = 2
 EDGE_COST = 6
+TABLE_COST = 0.3
 FIRST_MIB = 51
 NU = 0.5
 DT = 0.1
@@ -255,8 +256,7 @@
     cost_t[2:4, :] = potential[:, FROM_R:COLS].T[EDGE - 2 : EDGE, :]
 
 
-def first_rest_kernel(dens, value, kern_rows, new, far, near, *table):
-    rest_kernel(dens, value, new, far, near)
+def rows_table_kernel(kern_rows, *table):
     band(kern_rows, table[2:4], table[0:2])
 
 
@@ -512,13 +512,10 @@
     )
     for step_index in range(STEPS):
         last = step_index == STEPS - 1
+        new, far_2, near_2 = call(rest_kernel, SECOND, [], 1, dens, value)
         if step_index == 0:
-            new, far_2, near_2, *table = call(
-                first_rest_kernel, SECOND + ROWS_TABLE + TURNED_TABLE, [], 1, dens, value, kern_rows[None]
-            )
+            table = call(rows_table_kernel, ROWS_TABLE + TURNED_TABLE, [], TABLE_COST, kern_rows[None])
             rows_table, turned_table = table[0:2], table[2:4]
-        else:
-            new, far_2, near_2 = call(rest_kernel, SECOND, [], 1, dens, value)
         far_1 = lax.ppermute(far_1, "rows", far_pairs)
         near_1 = lax.ppermute(near_1, "rows", near_pairs)
         far_2 = lax.ppermute(far_2, "rows", far_pairs)

time: 51.6 us -> 50.7 us (0.983)
  local copies, waits for them, and re-layouts: 1.36 us -> 0.69 us
    unnamed x6, local copies, waits for them, and re-layouts: 1.36 us -> 0.69 us
    pallas_call x9 -> x10, Pallas kernels: 16.3 us -> 16.3 us  [call(): pl.pallas_call(kernel, out_shape=out_shapes, in_specs=[HBM if n in hbm_in...]
  transfers between devices with their start and end apart: 12 -> 12, of which waited for: 5 -> 5; matrix products, arithmetic and copies ran while one was open for 0% -> 0% of each run, Pallas kernels for 21% -> 22%
where the time goes in v6:
time: 50.7 us; the launch traced here: 50.6 us
  starting transfers between devices  24 us (47%)
  Pallas kernels  16.3 us (32%)
  waiting for transfers between devices  8.67 us (17%)
  between operations  0.92 us (2%)
  local copies, waits for them, and re-layouts  0.69 us (1%)
    pallas_call x10, Pallas kernels, call(): pl.pallas_call(kernel, out_shape=out_shapes, in_specs=[HBM if n in hbm_in...  16.3 us
    ppermute x2, starting transfers between devices, body(): right_in = lax.ppermute(left, 'cols', to_left)  6.47 us
    ppermute x2, starting transfers between devices, body(): near_1 = lax.ppermute(near_1, 'rows', near_pairs)  5.95 us
    ppermute x2, waiting for transfers between devices, body(): left_in = lax.ppermute(right, 'cols', to_right)  5 us
    ppermute x2, starting transfers between devices, body(): left_in = lax.ppermute(right, 'cols', to_right)  4.03 us
    ppermute x2, starting transfers between devices, body(): near_2 = lax.ppermute(near_2, 'rows', near_pairs)  3.7 us
    ppermute x2, waiting for transfers between devices, body(): right_in = lax.ppermute(left, 'cols', to_left)  3.28 us
    ppermute x2, starting transfers between devices, body(): far_1 = lax.ppermute(far_1, 'rows', far_pairs)  3.21 us
  transfers between devices with their start and end apart: 12, of which 5 were waited for; matrix products, arithmetic and copies ran while one was open for 0% of the time, Pallas kernels for 22%

profile of v6, /device:TPU:1, one launch (start us, length us, event | category | flops | bytes accessed | tf_op | source)
XLA Modules:
  0.0 50.6 jit_solution(5948946836204055199)
XLA Ops:
  0.6 2.0 %shard_map.68 = (f32[256,1024]{1,0:T(8,128)S(1)}, f32[256,1024]{1,0:T(8,128)S(1)}, f32[256,256]{1,0:T(8,128)S(1)}, f32[8,256]{1,0:T(8,128)S(1)}, f32[152,256]{1,0:T(8,128)S(1)}, /*index=5*/f32[152,256]{1,0:T(8,128)S(1)}) custom-call(f32[256,1024]{1,0:T(8,128)} %dens_in.1, f32[256,1024]{1,0:T(8,128)} %value_in.1), custom_call_target="tpu_custom_call" | custom-call | flops 1000000000 | bytes 3000000 | tf_op jit(solution)/shard_map/pallas_call | solution.py:42
  2.6 3.1 %collective-permute-start = (f32[152,256]{1,0:T(8,128)S(1)}, f32[152,256]{1,0:T(8,128)S(1)}, u32[]{:S(2)}, u32[]{:S(2)}) collective-permute-start(f32[152,256]{1,0:T(8,128)S(1)} %get-tuple-element.53), channel_id=1, source_target_pairs={{8,16},{16,8},{24,32},{32,24},{40,48},{48,40},{56,64},{64,56},{72,... | collective-permute-start | bytes 466952 | tf_op jit(solution)/shard_map/ppermute | solution.py:519
  5.8 4.7 %collective-permute-start.1 = (f32[152,256]{1,0:T(8,128)S(1)}, f32[152,256]{1,0:T(8,128)S(1)}, u32[]{:S(2)}, u32[]{:S(2)}) collective-permute-start(f32[152,256]{1,0:T(8,128)S(1)} %get-tuple-element.54), channel_id=1, source_target_pairs={{0,8},{8,0},{16,24},{24,16},{32,40},{40,32},{48,56},{56,48},{64,72... | collective-permute-start | bytes 466952 | tf_op jit(solution)/shard_map/ppermute | solution.py:520
  10.5 1.2 %shard_map.69 = (f32[256,768]{1,0:T(8,128)S(1)}, f32[128,768]{1,0:T(8,128)S(1)}, f32[128,768]{1,0:T(8,128)S(1)}) custom-call(f32[256,1024]{1,0:T(8,128)S(1)} %get-tuple-element.48.dens, f32[256,1024]{1,0:T(8,128)S(1)} %get-tuple-element.49.value.refs_7_), custom_call_target="tpu_custom_call" | custom-call | flops 1000000000 | bytes 3000000 | tf_op jit(solution)/shard_map/pallas_call | solution.py:42
  11.7 0.1 collective-permute-start.2
  11.8 0.0 copy-start.1
  11.8 1.1 %collective-permute-start.3 = (f32[128,768]{1,0:T(8,128)S(1)}, f32[128,768]{1,0:T(8,128)S(1)}, u32[]{:S(2)}, u32[]{:S(2)}) collective-permute-start(f32[128,768]{1,0:T(8,128)S(1)} %get-tuple-element.59), channel_id=1, source_target_pairs={{0,8},{8,0},{16,24},{24,16},{32,40},{40,32},{48,56},{56,48},{64,72... | collective-permute-start | bytes 1179656 | tf_op jit(solution)/shard_map/ppermute | solution.py:522
  12.9 0.0 copy-done.1
  12.9 0.2 shard_map.70
  13.1 0.0 collective-permute-done.far
  13.1 0.0 collective-permute-done.1.near
  13.2 0.0 copy-start
  13.2 0.6 %shard_map.71 = (f32[280,128]{1,0:T(8,128)S(1)}, f32[280,128]{1,0:T(8,128)S(1)}, f32[8,1024]{1,0:T(8,128)S(1)}, f32[8,1024]{1,0:T(8,128)S(1)}, f32[8,768]{1,0:T(8,128)S(1)}, /*index=5*/f32[256,256]{1,0:T(8,128)S(1)}) custom-call(f32[256,1024]{1,0:T(8,128)S(1)} %get-tuple-element.48.dens, f32[256,1024]{1,0:T(8,128)S(1)} %get-tuple-element.49.value.refs_7_, ...), custom_call_target="tpu_custom_call" | custom-call | flops 6000000000 | bytes 18000000 | tf_op jit(solution)/shard_map/pallas_call | solution.py:42
  13.7 2.5 %collective-permute-start.4 = (f32[280,128]{1,0:T(8,128)S(1)}, f32[280,128]{1,0:T(8,128)S(1)}, u32[]{:S(2)}, u32[]{:S(2)}) collective-permute-start(f32[280,128]{1,0:T(8,128)S(1)} %get-tuple-element.63), channel_id=1, source_target_pairs={{0,1},{1,2},{2,3},{3,4},{4,5},{5,6},{6,7},{7,0},{8,9},{9,10},{10,1... | collective-permute-start | bytes 430088 | tf_op jit(solution)/shard_map/ppermute | solution.py:531
  16.3 2.6 %collective-permute-start.5 = (f32[280,128]{1,0:T(8,128)S(1)}, f32[280,128]{1,0:T(8,128)S(1)}, u32[]{:S(2)}, u32[]{:S(2)}) collective-permute-start(f32[280,128]{1,0:T(8,128)S(1)} %get-tuple-element.64), channel_id=1, source_target_pairs={{0,7},{1,0},{2,1},{3,2},{4,3},{5,4},{6,5},{7,6},{8,15},{9,8},{10,9... | collective-permute-start | bytes 430088 | tf_op jit(solution)/shard_map/ppermute | solution.py:530
  18.9 0.4 collective-permute-done.2.refs_2_
  19.3 0.0 collective-permute-done.3.refs_3_
  19.3 0.0 copy-start.2
  19.3 0.0 copy-done
  19.3 0.7 %copy-done.2 = f32[256]{0:T(256)S(1)} copy-done((f32[256]{0:T(256)S(1)}, f32[256]{0:T(256)}, u32[]{:S(2)}) %copy-start.2) | copy-done | bytes 1048
  20.0 3.1 %shard_map.72 = (f32[256,512]{1,0:T(8,128)S(1)}, f32[256,1024]{1,0:T(8,128)S(1)}, f32[8,256]{1,0:T(8,128)S(1)}, f32[256,1024]{1,0:T(8,128)S(1)}, f32[256,1024]{1...) custom-call(f32[256,768]{1,0:T(8,128)S(1)} %get-tuple-element.50.refs_0_, ...), custom_call_target="tpu_custom_call" | custom-call | flops 3000000000 | bytes 9000000 | tf_op jit(solution)/shard_map/pallas_call | solution.py:42
  23.1 3.9 %collective-permute-done.4.refs_4_ = f32[280,128]{1,0:T(8,128)S(1)} collective-permute-done((f32[280,128]{1,0:T(8,128)S(1)}, f32[280,128]{1,0:T(8,128)S(1)}, u32[]{:S(2)}, u32[]{:S(2)}) %collective-permute-start.4) | collective-permute-done | bytes 143392 | tf_op jit(solution)/shard_map/ppermute | solution.py:531
  27.0 1.3 %collective-permute-done.5.refs_5_ = f32[280,128]{1,0:T(8,128)S(1)} collective-permute-done((f32[280,128]{1,0:T(8,128)S(1)}, f32[280,128]{1,0:T(8,128)S(1)}, u32[]{:S(2)}, u32[]{:S(2)}) %collective-permute-start.5) | collective-permute-done | bytes 143392 | tf_op jit(solution)/shard_map/ppermute | solution.py:530
  28.3 1.5 %shard_map.73 = (f32[256,1024]{1,0:T(8,128)S(1)}, f32[256,1024]{1,0:T(8,128)S(1)}, f32[256,256]{1,0:T(8,128)S(1)}, f32[8,256]{1,0:T(8,128)S(1)}, f32[152,256]{1,0:T(8,128)S(1)}, /*index=5*/f32[152,256]{1,0:T(8,128)S(1)}) custom-call(f32[8,256]{1,0:T(8,128)S(1)} %get-tuple-element.61.refs_0_, ...), custom_call_target="tpu_custom_call", output_to_operand_aliasing={{0}: (13, {}), {1}: (14, {})} | custom-call | flops 1000000000 | bytes 3000000 | tf_op jit(solution)/shard_map/pallas_call | solution.py:42
  29.8 0.1 collective-permute-start.6
  29.9 1.3 %collective-permute-start.7 = (f32[152,256]{1,0:T(8,128)S(1)}, f32[152,256]{1,0:T(8,128)S(1)}, u32[]{:S(2)}, u32[]{:S(2)}) collective-permute-start(f32[152,256]{1,0:T(8,128)S(1)} %get-tuple-element.80), channel_id=1, source_target_pairs={{0,8},{8,0},{16,24},{24,16},{32,40},{40,32},{48,56},{56,48},{64,72... | collective-permute-start | bytes 466952 | tf_op jit(solution)/shard_map/ppermute | solution.py:520
  31.2 1.3 %shard_map.74 = (f32[256,768]{1,0:T(8,128)S(1)}, f32[128,768]{1,0:T(8,128)S(1)}, f32[128,768]{1,0:T(8,128)S(1)}) custom-call(f32[256,1024]{1,0:T(8,128)S(1)} %get-tuple-element.74.dens, f32[256,1024]{1,0:T(8,128)S(1)} %get-tuple-element.75.value.refs_8_), custom_call_target="tpu_custom_call" | custom-call | flops 1000000000 | bytes 3000000 | tf_op jit(solution)/shard_map/pallas_call | solution.py:42
  32.5 0.6 %collective-permute-start.8 = (f32[128,768]{1,0:T(8,128)S(1)}, f32[128,768]{1,0:T(8,128)S(1)}, u32[]{:S(2)}, u32[]{:S(2)}) collective-permute-start(f32[128,768]{1,0:T(8,128)S(1)} %get-tuple-element.82), channel_id=1, source_target_pairs={{8,16},{16,8},{24,32},{32,24},{40,48},{48,40},{56,64},{64,56},{72,... | collective-permute-start | bytes 1179656 | tf_op jit(solution)/shard_map/ppermute | solution.py:521
  33.1 2.6 %collective-permute-start.9 = (f32[128,768]{1,0:T(8,128)S(1)}, f32[128,768]{1,0:T(8,128)S(1)}, u32[]{:S(2)}, u32[]{:S(2)}) collective-permute-start(f32[128,768]{1,0:T(8,128)S(1)} %get-tuple-element.83), channel_id=1, source_target_pairs={{0,8},{8,0},{16,24},{24,16},{32,40},{40,32},{48,56},{56,48},{64,72... | collective-permute-start | bytes 1179656 | tf_op jit(solution)/shard_map/ppermute | solution.py:522
  35.7 0.0 collective-permute-done.6.far
  35.7 0.0 collective-permute-done.7.near
  35.7 0.6 %shard_map.75 = (f32[280,128]{1,0:T(8,128)S(1)}, f32[280,128]{1,0:T(8,128)S(1)}, f32[8,1024]{1,0:T(8,128)S(1)}, f32[8,1024]{1,0:T(8,128)S(1)}, f32[8,768]{1,0:T(8,128)S(1)}, /*index=5*/f32[256,256]{1,0:T(8,128)S(1)}) custom-call(f32[256,1024]{1,0:T(8,128)S(1)} %get-tuple-element.74.dens, f32[256,1024]{1,0:T(8,128)S(1)} %get-tuple-element.75.value.refs_8_, ...), custom_call_target="tpu_custom_call" | custom-call | flops 6000000000 | bytes 18000000 | tf_op jit(solution)/shard_map/pallas_call | solution.py:42
  36.2 1.5 %collective-permute-start.10 = (f32[280,128]{1,0:T(8,128)S(1)}, f32[280,128]{1,0:T(8,128)S(1)}, u32[]{:S(2)}, u32[]{:S(2)}) collective-permute-start(f32[280,128]{1,0:T(8,128)S(1)} %get-tuple-element.87), channel_id=1, source_target_pairs={{0,1},{1,2},{2,3},{3,4},{4,5},{5,6},{6,7},{7,0},{8,9},{9,10},{10,1... | collective-permute-start | bytes 430088 | tf_op jit(solution)/shard_map/ppermute | solution.py:531
  37.7 3.8 %collective-permute-start.11 = (f32[280,128]{1,0:T(8,128)S(1)}, f32[280,128]{1,0:T(8,128)S(1)}, u32[]{:S(2)}, u32[]{:S(2)}) collective-permute-start(f32[280,128]{1,0:T(8,128)S(1)} %get-tuple-element.88), channel_id=1, source_target_pairs={{0,7},{1,0},{2,1},{3,2},{4,3},{5,4},{6,5},{7,6},{8,15},{9,8},{10,9... | collective-permute-start | bytes 430088 | tf_op jit(solution)/shard_map/ppermute | solution.py:530
  41.6 0.0 collective-permute-done.8.refs_2_
  41.6 0.0 collective-permute-done.9.refs_3_
  41.6 3.9 %shard_map.76 = (f32[256,512]{1,0:T(8,128)S(1)}, f32[256,1024]{1,0:T(8,128)S(1)}, f32[8,256]{1,0:T(8,128)S(1)}, f32[256,1024]{1,0:T(8,128)}, f32[256,1024]{1,0:T(8,128)}) custom-call(f32[256,768]{1,0:T(8,128)S(1)} %get-tuple-element.76.refs_0_, f32[8,1024]{1,0:T(8,128)S(1)} %get-tuple-element.81.refs_1_.refs_2_, ...), custom_call_target="tpu_custom_call" | custom-call | flops 3000000000 | bytes 9000000 | tf_op jit(solution)/shard_map/pallas_call | solution.py:42
  45.5 1.1 %collective-permute-done.10.refs_4_ = f32[280,128]{1,0:T(8,128)S(1)} collective-permute-done((f32[280,128]{1,0:T(8,128)S(1)}, f32[280,128]{1,0:T(8,128)S(1)}, u32[]{:S(2)}, u32[]{:S(2)}) %collective-permute-start.10) | collective-permute-done | bytes 143392 | tf_op jit(solution)/shard_map/ppermute | solution.py:531
  46.6 2.0 %collective-permute-done.11.refs_5_ = f32[280,128]{1,0:T(8,128)S(1)} collective-permute-done((f32[280,128]{1,0:T(8,128)S(1)}, f32[280,128]{1,0:T(8,128)S(1)}, u32[]{:S(2)}, u32[]{:S(2)}) %collective-permute-start.11) | collective-permute-done | bytes 143392 | tf_op jit(solution)/shard_map/ppermute | solution.py:530
  48.6 1.9 %shard_map.77 = (f32[256,1024]{1,0:T(8,128)}, f32[256,1024]{1,0:T(8,128)}) custom-call(f32[8,256]{1,0:T(8,128)S(1)} %get-tuple-element.85.refs_0_, f32[256,256]{1,0:T(8,128)S(1)} %get-tuple-element.77.side.refs_1_, f32[8,1024]{1,0:T(8,128)S(1)} %get-tuple-element.81.refs_1_.refs_2_, ...), custom_call_target="tpu_custom_call", output_to_operand_aliasing={{0}: (13, {}), {1}: (14, {})} | custom-call | flops 1000000000 | bytes 3000000 | tf_op jit(solution)/shard_map/pallas_call | solution.py:42
Async XLA Ops:
  2.6 10.5 %collective-permute-start = (f32[152,256]{1,0:T(8,128)S(1)}, f32[152,256]{1,0:T(8,128)S(1)}, u32[]{:S(2)}, u32[]{:S(2)}) collective-permute-start(f32[152,256]{1,0:T(8,128)S(1)} %get-tuple-element.53), channel_id=1, source_target_pairs={{8,16},{16,8},{24,32},{32,24},{40,48},{48,40},{56,64},{64,56},{72,... | collective-permute-start | bytes 466952 | tf_op jit(solution)/shard_map/ppermute | solution.py:519
  5.8 7.4 %collective-permute-start.1 = (f32[152,256]{1,0:T(8,128)S(1)}, f32[152,256]{1,0:T(8,128)S(1)}, u32[]{:S(2)}, u32[]{:S(2)}) collective-permute-start(f32[152,256]{1,0:T(8,128)S(1)} %get-tuple-element.54), channel_id=1, source_target_pairs={{0,8},{8,0},{16,24},{24,16},{32,40},{40,32},{48,56},{56,48},{64,72... | collective-permute-start | bytes 466952 | tf_op jit(solution)/shard_map/ppermute | solution.py:520
  11.7 7.6 %collective-permute-start.2 = (f32[128,768]{1,0:T(8,128)S(1)}, f32[128,768]{1,0:T(8,128)S(1)}, u32[]{:S(2)}, u32[]{:S(2)}) collective-permute-start(f32[128,768]{1,0:T(8,128)S(1)} %get-tuple-element.58), channel_id=1, source_target_pairs={{8,16},{16,8},{24,32},{32,24},{40,48},{48,40},{56,64},{64,56},{72,... | collective-permute-start | bytes 1179656 | tf_op jit(solution)/shard_map/ppermute | solution.py:521
  11.8 1.1 %copy-start.1 = (f32[256]{0:T(256)S(1)}, f32[256]{0:T(256)}, u32[]{:S(2)}) copy-start(f32[256]{0:T(256)} %param.8) | copy-start | bytes 3076
  11.8 7.5 %collective-permute-start.3 = (f32[128,768]{1,0:T(8,128)S(1)}, f32[128,768]{1,0:T(8,128)S(1)}, u32[]{:S(2)}, u32[]{:S(2)}) collective-permute-start(f32[128,768]{1,0:T(8,128)S(1)} %get-tuple-element.59), channel_id=1, source_target_pairs={{0,8},{8,0},{16,24},{24,16},{32,40},{40,32},{48,56},{56,48},{64,72... | collective-permute-start | bytes 1179656 | tf_op jit(solution)/shard_map/ppermute | solution.py:522
  13.2 6.1 %copy-start = (f32[256,1024]{1,0:T(8,128)S(1)}, f32[256,1024]{1,0:T(8,128)}, u32[]{:S(2)}) copy-start(f32[256,1024]{1,0:T(8,128)} %refs_9_.1) | copy-start | bytes 3145732
  13.7 13.2 %collective-permute-start.4 = (f32[280,128]{1,0:T(8,128)S(1)}, f32[280,128]{1,0:T(8,128)S(1)}, u32[]{:S(2)}, u32[]{:S(2)}) collective-permute-start(f32[280,128]{1,0:T(8,128)S(1)} %get-tuple-element.63), channel_id=1, source_target_pairs={{0,1},{1,2},{2,3},{3,4},{4,5},{5,6},{6,7},{7,0},{8,9},{9,10},{10,1... | collective-permute-start | bytes 430088 | tf_op jit(solution)/shard_map/ppermute | solution.py:531
  16.3 12.0 %collective-permute-start.5 = (f32[280,128]{1,0:T(8,128)S(1)}, f32[280,128]{1,0:T(8,128)S(1)}, u32[]{:S(2)}, u32[]{:S(2)}) collective-permute-start(f32[280,128]{1,0:T(8,128)S(1)} %get-tuple-element.64), channel_id=1, source_target_pairs={{0,7},{1,0},{2,1},{3,2},{4,3},{5,4},{6,5},{7,6},{8,15},{9,8},{10,9... | collective-permute-start | bytes 430088 | tf_op jit(solution)/shard_map/ppermute | solution.py:530
  19.3 0.7 %copy-start.2 = (f32[256]{0:T(256)S(1)}, f32[256]{0:T(256)}, u32[]{:S(2)}) copy-start(f32[256]{0:T(256)} %param.9) | copy-start | bytes 3076
  29.8 5.9 %collective-permute-start.6 = (f32[152,256]{1,0:T(8,128)S(1)}, f32[152,256]{1,0:T(8,128)S(1)}, u32[]{:S(2)}, u32[]{:S(2)}) collective-permute-start(f32[152,256]{1,0:T(8,128)S(1)} %get-tuple-element.79), channel_id=1, source_target_pairs={{8,16},{16,8},{24,32},{32,24},{40,48},{48,40},{56,64},{64,56},{72,... | collective-permute-start | bytes 466952 | tf_op jit(solution)/shard_map/ppermute | solution.py:519
  29.9 5.8 %collective-permute-start.7 = (f32[152,256]{1,0:T(8,128)S(1)}, f32[152,256]{1,0:T(8,128)S(1)}, u32[]{:S(2)}, u32[]{:S(2)}) collective-permute-start(f32[152,256]{1,0:T(8,128)S(1)} %get-tuple-element.80), channel_id=1, source_target_pairs={{0,8},{8,0},{16,24},{24,16},{32,40},{40,32},{48,56},{56,48},{64,72... | collective-permute-start | bytes 466952 | tf_op jit(solution)/shard_map/ppermute | solution.py:520
  32.5 9.1 %collective-permute-start.8 = (f32[128,768]{1,0:T(8,128)S(1)}, f32[128,768]{1,0:T(8,128)S(1)}, u32[]{:S(2)}, u32[]{:S(2)}) collective-permute-start(f32[128,768]{1,0:T(8,128)S(1)} %get-tuple-element.82), channel_id=1, source_target_pairs={{8,16},{16,8},{24,32},{32,24},{40,48},{48,40},{56,64},{64,56},{72,... | collective-permute-start | bytes 1179656 | tf_op jit(solution)/shard_map/ppermute | solution.py:521
  33.1 8.5 %collective-permute-start.9 = (f32[128,768]{1,0:T(8,128)S(1)}, f32[128,768]{1,0:T(8,128)S(1)}, u32[]{:S(2)}, u32[]{:S(2)}) collective-permute-start(f32[128,768]{1,0:T(8,128)S(1)} %get-tuple-element.83), channel_id=1, source_target_pairs={{0,8},{8,0},{16,24},{24,16},{32,40},{40,32},{48,56},{56,48},{64,72... | collective-permute-start | bytes 1179656 | tf_op jit(solution)/shard_map/ppermute | solution.py:522
  36.2 10.4 %collective-permute-start.10 = (f32[280,128]{1,0:T(8,128)S(1)}, f32[280,128]{1,0:T(8,128)S(1)}, u32[]{:S(2)}, u32[]{:S(2)}) collective-permute-start(f32[280,128]{1,0:T(8,128)S(1)} %get-tuple-element.87), channel_id=1, source_target_pairs={{0,1},{1,2},{2,3},{3,4},{4,5},{5,6},{6,7},{7,0},{8,9},{9,10},{10,1... | collective-permute-start | bytes 430088 | tf_op jit(solution)/shard_map/ppermute | solution.py:531
  37.7 10.8 %collective-permute-start.11 = (f32[280,128]{1,0:T(8,128)S(1)}, f32[280,128]{1,0:T(8,128)S(1)}, u32[]{:S(2)}, u32[]{:S(2)}) collective-permute-start(f32[280,128]{1,0:T(8,128)S(1)} %get-tuple-element.88), channel_id=1, source_target_pairs={{0,7},{1,0},{2,1},{3,2},{4,3},{5,4},{6,5},{7,6},{8,15},{9,8},{10,9... | collective-permute-start | bytes 430088 | tf_op jit(solution)/shard_map/ppermute | solution.py:530

commit v7 on v6

--- a/solution.py
+++ b/solution.py
@@ -379,7 +379,7 @@
 
 
 def finish(
-    cost_t, side, seams, tall, left, right, mixed, cong, inner, turned_hi, turned_lo, cols_hi, cols_lo,
+    cost_t, side, seams, tall, right, left, mixed, cong, inner, turned_hi, turned_lo, cols_hi, cols_lo,
     put_dens, put_value, dens_t, value_t, turn,
 ):
     for ref, n in ((dens_t, 0), (value_t, 1)):
@@ -555,7 +555,7 @@
                 new, seams, far_2, near_2, *rows_table, kern_cols[None], value, potential, around,
             )
             results = [dens_out, value_out]
-        operands = (cost_t, side, seams, tall, left_in, right_in, mixed, cong, inner, *turned_table, *cols_table, *results)
+        operands = (cost_t, side, seams, tall, right_in, left_in, mixed, cong, inner, *turned_table, *cols_table, *results)
         if last:
             scratch = [pltpu.VMEM((ROWS, 4 * EDGE), F32), pltpu.VMEM((ROWS, 4 * EDGE), F32)]
             return tuple(

time: 50.7 us -> 52 us (1.026)
  waiting for transfers between devices: 8.67 us -> 12.2 us
  starting transfers between devices: 24 us -> 21.7 us
    ppermute x2, waiting for transfers between devices: 5 us -> 8.89 us  [body(): left_in = lax.ppermute(right, 'cols', to_right)]
    ppermute x2, starting transfers between devices: 4.03 us -> 2.75 us  [body(): left_in = lax.ppermute(right, 'cols', to_right)]
    ppermute x2, waiting for transfers between devices: 3.28 us -> 2.14 us  [body(): right_in = lax.ppermute(left, 'cols', to_left)]
    ppermute x2, starting transfers between devices: 6.47 us -> 5.46 us  [body(): right_in = lax.ppermute(left, 'cols', to_left)]
    ppermute x2, waiting for transfers between devices: 0.38 us -> 1.16 us  [body(): far_2 = lax.ppermute(far_2, 'rows', far_pairs)]
  transfers between devices with their start and end apart: 12 -> 12, of which waited for: 5 -> 5; matrix products, arithmetic and copies ran while one was open for 0% -> 0% of each run, Pallas kernels for 22% -> 21%
where the time goes in v7:
time: 52 us; the launch traced here: 51.8 us
  starting transfers between devices  21.7 us (42%)
  Pallas kernels  16.3 us (31%)
  waiting for transfers between devices  12.2 us (23%)
  between operations  0.93 us (2%)
  local copies, waits for them, and re-layouts  0.69 us (1%)
    pallas_call x10, Pallas kernels, call(): pl.pallas_call(kernel, out_shape=out_shapes, in_specs=[HBM if n in hbm_in...  16.3 us
    ppermute x2, waiting for transfers between devices, body(): left_in = lax.ppermute(right, 'cols', to_right)  8.89 us
    ppermute x2, starting transfers between devices, body(): near_1 = lax.ppermute(near_1, 'rows', near_pairs)  5.95 us
    ppermute x2, starting transfers between devices, body(): right_in = lax.ppermute(left, 'cols', to_left)  5.46 us
    ppermute x2, starting transfers between devices, body(): near_2 = lax.ppermute(near_2, 'rows', near_pairs)  3.7 us
    ppermute x2, starting transfers between devices, body(): far_1 = lax.ppermute(far_1, 'rows', far_pairs)  3.21 us
    ppermute x2, starting transfers between devices, body(): left_in = lax.ppermute(right, 'cols', to_right)  2.75 us
    ppermute x2, waiting for transfers between devices, body(): right_in = lax.ppermute(left, 'cols', to_left)  2.14 us
  transfers between devices with their start and end apart: 12, of which 5 were waited for; matrix products, arithmetic and copies ran while one was open for 0% of the time, Pallas kernels for 21%

profile of v7, /device:TPU:1, one launch (start us, length us, event | category | flops | bytes accessed | tf_op | source)
XLA Modules:
  0.0 51.8 jit_solution(9307526016945828022)
XLA Ops:
  0.6 2.0 %shard_map.68 = (f32[256,1024]{1,0:T(8,128)S(1)}, f32[256,1024]{1,0:T(8,128)S(1)}, f32[256,256]{1,0:T(8,128)S(1)}, f32[8,256]{1,0:T(8,128)S(1)}, f32[152,256]{1,0:T(8,128)S(1)}, /*index=5*/f32[152,256]{1,0:T(8,128)S(1)}) custom-call(f32[256,1024]{1,0:T(8,128)} %dens_in.1, f32[256,1024]{1,0:T(8,128)} %value_in.1), custom_call_target="tpu_custom_call" | custom-call | flops 1000000000 | bytes 3000000 | tf_op jit(solution)/shard_map/pallas_call | solution.py:42
  2.6 3.1 %collective-permute-start = (f32[152,256]{1,0:T(8,128)S(1)}, f32[152,256]{1,0:T(8,128)S(1)}, u32[]{:S(2)}, u32[]{:S(2)}) collective-permute-start(f32[152,256]{1,0:T(8,128)S(1)} %get-tuple-element.53), channel_id=1, source_target_pairs={{8,16},{16,8},{24,32},{32,24},{40,48},{48,40},{56,64},{64,56},{72,... | collective-permute-start | bytes 466952 | tf_op jit(solution)/shard_map/ppermute | solution.py:519
  5.8 4.7 %collective-permute-start.1 = (f32[152,256]{1,0:T(8,128)S(1)}, f32[152,256]{1,0:T(8,128)S(1)}, u32[]{:S(2)}, u32[]{:S(2)}) collective-permute-start(f32[152,256]{1,0:T(8,128)S(1)} %get-tuple-element.54), channel_id=1, source_target_pairs={{0,8},{8,0},{16,24},{24,16},{32,40},{40,32},{48,56},{56,48},{64,72... | collective-permute-start | bytes 466952 | tf_op jit(solution)/shard_map/ppermute | solution.py:520
  10.5 1.2 %shard_map.69 = (f32[256,768]{1,0:T(8,128)S(1)}, f32[128,768]{1,0:T(8,128)S(1)}, f32[128,768]{1,0:T(8,128)S(1)}) custom-call(f32[256,1024]{1,0:T(8,128)S(1)} %get-tuple-element.48.dens, f32[256,1024]{1,0:T(8,128)S(1)} %get-tuple-element.49.value.refs_7_), custom_call_target="tpu_custom_call" | custom-call | flops 1000000000 | bytes 3000000 | tf_op jit(solution)/shard_map/pallas_call | solution.py:42
  11.7 0.1 collective-permute-start.2
  11.8 0.0 copy-start.1
  11.8 1.1 %collective-permute-start.3 = (f32[128,768]{1,0:T(8,128)S(1)}, f32[128,768]{1,0:T(8,128)S(1)}, u32[]{:S(2)}, u32[]{:S(2)}) collective-permute-start(f32[128,768]{1,0:T(8,128)S(1)} %get-tuple-element.59), channel_id=1, source_target_pairs={{0,8},{8,0},{16,24},{24,16},{32,40},{40,32},{48,56},{56,48},{64,72... | collective-permute-start | bytes 1179656 | tf_op jit(solution)/shard_map/ppermute | solution.py:522
  12.9 0.0 copy-done.1
  12.9 0.2 shard_map.70
  13.1 0.0 collective-permute-done.far
  13.1 0.0 collective-permute-done.1.near
  13.2 0.0 copy-start
  13.2 0.6 %shard_map.71 = (f32[280,128]{1,0:T(8,128)S(1)}, f32[280,128]{1,0:T(8,128)S(1)}, f32[8,1024]{1,0:T(8,128)S(1)}, f32[8,1024]{1,0:T(8,128)S(1)}, f32[8,768]{1,0:T(8,128)S(1)}, /*index=5*/f32[256,256]{1,0:T(8,128)S(1)}) custom-call(f32[256,1024]{1,0:T(8,128)S(1)} %get-tuple-element.48.dens, f32[256,1024]{1,0:T(8,128)S(1)} %get-tuple-element.49.value.refs_7_, ...), custom_call_target="tpu_custom_call" | custom-call | flops 6000000000 | bytes 18000000 | tf_op jit(solution)/shard_map/pallas_call | solution.py:42
  13.7 5.0 %collective-permute-start.4 = (f32[280,128]{1,0:T(8,128)S(1)}, f32[280,128]{1,0:T(8,128)S(1)}, u32[]{:S(2)}, u32[]{:S(2)}) collective-permute-start(f32[280,128]{1,0:T(8,128)S(1)} %get-tuple-element.63), channel_id=1, source_target_pairs={{0,7},{1,0},{2,1},{3,2},{4,3},{5,4},{6,5},{7,6},{8,15},{9,8},{10,9... | collective-permute-start | bytes 430088 | tf_op jit(solution)/shard_map/ppermute | solution.py:530
  18.7 0.0 collective-permute-start.5
  18.7 0.6 %collective-permute-done.2.refs_2_ = f32[128,768]{1,0:T(8,128)S(1)} collective-permute-done((f32[128,768]{1,0:T(8,128)S(1)}, f32[128,768]{1,0:T(8,128)S(1)}, u32[]{:S(2)}, u32[]{:S(2)}) %collective-permute-start.2) | collective-permute-done | bytes 393248 | tf_op jit(solution)/shard_map/ppermute | solution.py:521
  19.3 0.0 collective-permute-done.3.refs_3_
  19.3 0.0 copy-start.2
  19.3 0.0 copy-done
  19.3 0.7 %copy-done.2 = f32[256]{0:T(256)S(1)} copy-done((f32[256]{0:T(256)S(1)}, f32[256]{0:T(256)}, u32[]{:S(2)}) %copy-start.2) | copy-done | bytes 1048
  20.0 3.1 %shard_map.72 = (f32[256,512]{1,0:T(8,128)S(1)}, f32[256,1024]{1,0:T(8,128)S(1)}, f32[8,256]{1,0:T(8,128)S(1)}, f32[256,1024]{1,0:T(8,128)S(1)}, f32[256,1024]{1...) custom-call(f32[256,768]{1,0:T(8,128)S(1)} %get-tuple-element.50.refs_0_, ...), custom_call_target="tpu_custom_call" | custom-call | flops 3000000000 | bytes 9000000 | tf_op jit(solution)/shard_map/pallas_call | solution.py:42
  23.1 2.1 %collective-permute-done.4.refs_4_ = f32[280,128]{1,0:T(8,128)S(1)} collective-permute-done((f32[280,128]{1,0:T(8,128)S(1)}, f32[280,128]{1,0:T(8,128)S(1)}, u32[]{:S(2)}, u32[]{:S(2)}) %collective-permute-start.4) | collective-permute-done | bytes 143392 | tf_op jit(solution)/shard_map/ppermute | solution.py:530
  25.2 5.5 %collective-permute-done.5.refs_5_ = f32[280,128]{1,0:T(8,128)S(1)} collective-permute-done((f32[280,128]{1,0:T(8,128)S(1)}, f32[280,128]{1,0:T(8,128)S(1)}, u32[]{:S(2)}, u32[]{:S(2)}) %collective-permute-start.5) | collective-permute-done | bytes 143392 | tf_op jit(solution)/shard_map/ppermute | solution.py:531
  30.7 1.5 %shard_map.73 = (f32[256,1024]{1,0:T(8,128)S(1)}, f32[256,1024]{1,0:T(8,128)S(1)}, f32[256,256]{1,0:T(8,128)S(1)}, f32[8,256]{1,0:T(8,128)S(1)}, f32[152,256]{1,0:T(8,128)S(1)}, /*index=5*/f32[152,256]{1,0:T(8,128)S(1)}) custom-call(f32[8,256]{1,0:T(8,128)S(1)} %get-tuple-element.61.refs_0_, ...), custom_call_target="tpu_custom_call", output_to_operand_aliasing={{0}: (13, {}), {1}: (14, {})} | custom-call | flops 1000000000 | bytes 3000000 | tf_op jit(solution)/shard_map/pallas_call | solution.py:42
  32.2 0.1 collective-permute-start.6
  32.3 1.3 %collective-permute-start.7 = (f32[152,256]{1,0:T(8,128)S(1)}, f32[152,256]{1,0:T(8,128)S(1)}, u32[]{:S(2)}, u32[]{:S(2)}) collective-permute-start(f32[152,256]{1,0:T(8,128)S(1)} %get-tuple-element.80), channel_id=1, source_target_pairs={{0,8},{8,0},{16,24},{24,16},{32,40},{40,32},{48,56},{56,48},{64,72... | collective-permute-start | bytes 466952 | tf_op jit(solution)/shard_map/ppermute | solution.py:520
  33.6 1.3 %shard_map.74 = (f32[256,768]{1,0:T(8,128)S(1)}, f32[128,768]{1,0:T(8,128)S(1)}, f32[128,768]{1,0:T(8,128)S(1)}) custom-call(f32[256,1024]{1,0:T(8,128)S(1)} %get-tuple-element.74.dens, f32[256,1024]{1,0:T(8,128)S(1)} %get-tuple-element.75.value.refs_8_), custom_call_target="tpu_custom_call" | custom-call | flops 1000000000 | bytes 3000000 | tf_op jit(solution)/shard_map/pallas_call | solution.py:42
  34.9 0.6 %collective-permute-start.8 = (f32[128,768]{1,0:T(8,128)S(1)}, f32[128,768]{1,0:T(8,128)S(1)}, u32[]{:S(2)}, u32[]{:S(2)}) collective-permute-start(f32[128,768]{1,0:T(8,128)S(1)} %get-tuple-element.82), channel_id=1, source_target_pairs={{8,16},{16,8},{24,32},{32,24},{40,48},{48,40},{56,64},{64,56},{72,... | collective-permute-start | bytes 1179656 | tf_op jit(solution)/shard_map/ppermute | solution.py:521
  35.5 2.6 %collective-permute-start.9 = (f32[128,768]{1,0:T(8,128)S(1)}, f32[128,768]{1,0:T(8,128)S(1)}, u32[]{:S(2)}, u32[]{:S(2)}) collective-permute-start(f32[128,768]{1,0:T(8,128)S(1)} %get-tuple-element.83), channel_id=1, source_target_pairs={{0,8},{8,0},{16,24},{24,16},{32,40},{40,32},{48,56},{56,48},{64,72... | collective-permute-start | bytes 1179656 | tf_op jit(solution)/shard_map/ppermute | solution.py:522
  38.1 0.0 collective-permute-done.6.far
  38.1 0.0 collective-permute-done.7.near
  38.1 0.6 %shard_map.75 = (f32[280,128]{1,0:T(8,128)S(1)}, f32[280,128]{1,0:T(8,128)S(1)}, f32[8,1024]{1,0:T(8,128)S(1)}, f32[8,1024]{1,0:T(8,128)S(1)}, f32[8,768]{1,0:T(8,128)S(1)}, /*index=5*/f32[256,256]{1,0:T(8,128)S(1)}) custom-call(f32[256,1024]{1,0:T(8,128)S(1)} %get-tuple-element.74.dens, f32[256,1024]{1,0:T(8,128)S(1)} %get-tuple-element.75.value.refs_8_, ...), custom_call_target="tpu_custom_call" | custom-call | flops 6000000000 | bytes 18000000 | tf_op jit(solution)/shard_map/pallas_call | solution.py:42
  38.7 0.5 collective-permute-start.10
  39.2 2.7 %collective-permute-start.11 = (f32[280,128]{1,0:T(8,128)S(1)}, f32[280,128]{1,0:T(8,128)S(1)}, u32[]{:S(2)}, u32[]{:S(2)}) collective-permute-start(f32[280,128]{1,0:T(8,128)S(1)} %get-tuple-element.88), channel_id=1, source_target_pairs={{0,1},{1,2},{2,3},{3,4},{4,5},{5,6},{6,7},{7,0},{8,9},{9,10},{10,1... | collective-permute-start | bytes 430088 | tf_op jit(solution)/shard_map/ppermute | solution.py:531
  41.9 0.6 %collective-permute-done.8.refs_2_ = f32[128,768]{1,0:T(8,128)S(1)} collective-permute-done((f32[128,768]{1,0:T(8,128)S(1)}, f32[128,768]{1,0:T(8,128)S(1)}, u32[]{:S(2)}, u32[]{:S(2)}) %collective-permute-start.8) | collective-permute-done | bytes 393248 | tf_op jit(solution)/shard_map/ppermute | solution.py:521
  42.5 0.0 collective-permute-done.9.refs_3_
  42.5 3.9 %shard_map.76 = (f32[256,512]{1,0:T(8,128)S(1)}, f32[256,1024]{1,0:T(8,128)S(1)}, f32[8,256]{1,0:T(8,128)S(1)}, f32[256,1024]{1,0:T(8,128)}, f32[256,1024]{1,0:T(8,128)}) custom-call(f32[256,768]{1,0:T(8,128)S(1)} %get-tuple-element.76.refs_0_, f32[8,1024]{1,0:T(8,128)S(1)} %get-tuple-element.81.refs_1_.refs_2_, ...), custom_call_target="tpu_custom_call" | custom-call | flops 3000000000 | bytes 9000000 | tf_op jit(solution)/shard_map/pallas_call | solution.py:42
  46.4 0.0 collective-permute-done.10.refs_4_
  46.5 3.4 %collective-permute-done.11.refs_5_ = f32[280,128]{1,0:T(8,128)S(1)} collective-permute-done((f32[280,128]{1,0:T(8,128)S(1)}, f32[280,128]{1,0:T(8,128)S(1)}, u32[]{:S(2)}, u32[]{:S(2)}) %collective-permute-start.11) | collective-permute-done | bytes 143392 | tf_op jit(solution)/shard_map/ppermute | solution.py:531
  49.8 1.9 %shard_map.77 = (f32[256,1024]{1,0:T(8,128)}, f32[256,1024]{1,0:T(8,128)}) custom-call(f32[8,256]{1,0:T(8,128)S(1)} %get-tuple-element.85.refs_0_, f32[256,256]{1,0:T(8,128)S(1)} %get-tuple-element.77.side.refs_1_, f32[8,1024]{1,0:T(8,128)S(1)} %get-tuple-element.81.refs_1_.refs_2_, ...), custom_call_target="tpu_custom_call", output_to_operand_aliasing={{0}: (13, {}), {1}: (14, {})} | custom-call | flops 1000000000 | bytes 3000000 | tf_op jit(solution)/shard_map/pallas_call | solution.py:42
Async XLA Ops:
  2.6 10.5 %collective-permute-start = (f32[152,256]{1,0:T(8,128)S(1)}, f32[152,256]{1,0:T(8,128)S(1)}, u32[]{:S(2)}, u32[]{:S(2)}) collective-permute-start(f32[152,256]{1,0:T(8,128)S(1)} %get-tuple-element.53), channel_id=1, source_target_pairs={{8,16},{16,8},{24,32},{32,24},{40,48},{48,40},{56,64},{64,56},{72,... | collective-permute-start | bytes 466952 | tf_op jit(solution)/shard_map/ppermute | solution.py:519
  5.8 7.4 %collective-permute-start.1 = (f32[152,256]{1,0:T(8,128)S(1)}, f32[152,256]{1,0:T(8,128)S(1)}, u32[]{:S(2)}, u32[]{:S(2)}) collective-permute-start(f32[152,256]{1,0:T(8,128)S(1)} %get-tuple-element.54), channel_id=1, source_target_pairs={{0,8},{8,0},{16,24},{24,16},{32,40},{40,32},{48,56},{56,48},{64,72... | collective-permute-start | bytes 466952 | tf_op jit(solution)/shard_map/ppermute | solution.py:520
  11.7 7.6 %collective-permute-start.2 = (f32[128,768]{1,0:T(8,128)S(1)}, f32[128,768]{1,0:T(8,128)S(1)}, u32[]{:S(2)}, u32[]{:S(2)}) collective-permute-start(f32[128,768]{1,0:T(8,128)S(1)} %get-tuple-element.58), channel_id=1, source_target_pairs={{8,16},{16,8},{24,32},{32,24},{40,48},{48,40},{56,64},{64,56},{72,... | collective-permute-start | bytes 1179656 | tf_op jit(solution)/shard_map/ppermute | solution.py:521
  11.8 1.1 %copy-start.1 = (f32[256]{0:T(256)S(1)}, f32[256]{0:T(256)}, u32[]{:S(2)}) copy-start(f32[256]{0:T(256)} %param.8) | copy-start | bytes 3076
  11.8 7.5 %collective-permute-start.3 = (f32[128,768]{1,0:T(8,128)S(1)}, f32[128,768]{1,0:T(8,128)S(1)}, u32[]{:S(2)}, u32[]{:S(2)}) collective-permute-start(f32[128,768]{1,0:T(8,128)S(1)} %get-tuple-element.59), channel_id=1, source_target_pairs={{0,8},{8,0},{16,24},{24,16},{32,40},{40,32},{48,56},{56,48},{64,72... | collective-permute-start | bytes 1179656 | tf_op jit(solution)/shard_map/ppermute | solution.py:522
  13.2 6.1 %copy-start = (f32[256,1024]{1,0:T(8,128)S(1)}, f32[256,1024]{1,0:T(8,128)}, u32[]{:S(2)}) copy-start(f32[256,1024]{1,0:T(8,128)} %refs_9_.1) | copy-start | bytes 3145732
  13.7 11.5 %collective-permute-start.4 = (f32[280,128]{1,0:T(8,128)S(1)}, f32[280,128]{1,0:T(8,128)S(1)}, u32[]{:S(2)}, u32[]{:S(2)}) collective-permute-start(f32[280,128]{1,0:T(8,128)S(1)} %get-tuple-element.63), channel_id=1, source_target_pairs={{0,7},{1,0},{2,1},{3,2},{4,3},{5,4},{6,5},{7,6},{8,15},{9,8},{10,9... | collective-permute-start | bytes 430088 | tf_op jit(solution)/shard_map/ppermute | solution.py:530
  18.7 12.0 %collective-permute-start.5 = (f32[280,128]{1,0:T(8,128)S(1)}, f32[280,128]{1,0:T(8,128)S(1)}, u32[]{:S(2)}, u32[]{:S(2)}) collective-permute-start(f32[280,128]{1,0:T(8,128)S(1)} %get-tuple-element.64), channel_id=1, source_target_pairs={{0,1},{1,2},{2,3},{3,4},{4,5},{5,6},{6,7},{7,0},{8,9},{9,10},{10,1... | collective-permute-start | bytes 430088 | tf_op jit(solution)/shard_map/ppermute | solution.py:531
  19.3 0.7 %copy-start.2 = (f32[256]{0:T(256)S(1)}, f32[256]{0:T(256)}, u32[]{:S(2)}) copy-start(f32[256]{0:T(256)} %param.9) | copy-start | bytes 3076
  32.2 5.9 %collective-permute-start.6 = (f32[152,256]{1,0:T(8,128)S(1)}, f32[152,256]{1,0:T(8,128)S(1)}, u32[]{:S(2)}, u32[]{:S(2)}) collective-permute-start(f32[152,256]{1,0:T(8,128)S(1)} %get-tuple-element.79), channel_id=1, source_target_pairs={{8,16},{16,8},{24,32},{32,24},{40,48},{48,40},{56,64},{64,56},{72,... | collective-permute-start | bytes 466952 | tf_op jit(solution)/shard_map/ppermute | solution.py:519
  32.3 5.8 %collective-permute-start.7 = (f32[152,256]{1,0:T(8,128)S(1)}, f32[152,256]{1,0:T(8,128)S(1)}, u32[]{:S(2)}, u32[]{:S(2)}) collective-permute-start(f32[152,256]{1,0:T(8,128)S(1)} %get-tuple-element.80), channel_id=1, source_target_pairs={{0,8},{8,0},{16,24},{24,16},{32,40},{40,32},{48,56},{56,48},{64,72... | collective-permute-start | bytes 466952 | tf_op jit(solution)/shard_map/ppermute | solution.py:520
  34.9 7.6 %collective-permute-start.8 = (f32[128,768]{1,0:T(8,128)S(1)}, f32[128,768]{1,0:T(8,128)S(1)}, u32[]{:S(2)}, u32[]{:S(2)}) collective-permute-start(f32[128,768]{1,0:T(8,128)S(1)} %get-tuple-element.82), channel_id=1, source_target_pairs={{8,16},{16,8},{24,32},{32,24},{40,48},{48,40},{56,64},{64,56},{72,... | collective-permute-start | bytes 1179656 | tf_op jit(solution)/shard_map/ppermute | solution.py:521
  35.5 7.0 %collective-permute-start.9 = (f32[128,768]{1,0:T(8,128)S(1)}, f32[128,768]{1,0:T(8,128)S(1)}, u32[]{:S(2)}, u32[]{:S(2)}) collective-permute-start(f32[128,768]{1,0:T(8,128)S(1)} %get-tuple-element.83), channel_id=1, source_target_pairs={{0,8},{8,0},{16,24},{24,16},{32,40},{40,32},{48,56},{56,48},{64,72... | collective-permute-start | bytes 1179656 | tf_op jit(solution)/shard_map/ppermute | solution.py:522
  38.7 7.8 %collective-permute-start.10 = (f32[280,128]{1,0:T(8,128)S(1)}, f32[280,128]{1,0:T(8,128)S(1)}, u32[]{:S(2)}, u32[]{:S(2)}) collective-permute-start(f32[280,128]{1,0:T(8,128)S(1)} %get-tuple-element.87), channel_id=1, source_target_pairs={{0,7},{1,0},{2,1},{3,2},{4,3},{5,4},{6,5},{7,6},{8,15},{9,8},{10,9... | collective-permute-start | bytes 430088 | tf_op jit(solution)/shard_map/ppermute | solution.py:530
  39.2 10.7 %collective-permute-start.11 = (f32[280,128]{1,0:T(8,128)S(1)}, f32[280,128]{1,0:T(8,128)S(1)}, u32[]{:S(2)}, u32[]{:S(2)}) collective-permute-start(f32[280,128]{1,0:T(8,128)S(1)} %get-tuple-element.88), channel_id=1, source_target_pairs={{0,1},{1,2},{2,3},{3,4},{4,5},{5,6},{6,7},{7,0},{8,9},{9,10},{10,1... | collective-permute-start | bytes 430088 | tf_op jit(solution)/shard_map/ppermute | solution.py:531

commit v8 on v6

--- a/solution.py
+++ b/solution.py
@@ -196,11 +196,11 @@
 def prepare_sides(dens, value, side, own_t, far, near, wait_middle=None):
     core = core_index()
     side_density(dens, value, side)
-    if wait_middle is not None:
-        wait_middle()
     for n, ref in enumerate((dens, value)):
         own_t[4 * n : 4 * n + 2, :] = ref[:, 0:EDGE].T[0:2, :]
         own_t[4 * n + 2 : 4 * n + 4, :] = ref[:, FROM_R:COLS].T[EDGE - 2 : EDGE, :]
+    if wait_middle is not None:
+        wait_middle()
     for one, bottom in ((far, core), (near, 1 - core)):
         one[0:HALF, :] = side[pl.ds(pl.multiple_of(bottom * HALF, 8), HALF), :]
         for n, ref in enumerate((dens, value)):

time: 50.7 us -> 50.7 us (level)
  no operation moved by 1% of the time
where the time goes in v8:
time: 50.7 us; the launch traced here: 50.6 us
  starting transfers between devices  24 us (47%)
  Pallas kernels  16.3 us (32%)
  waiting for transfers between devices  8.67 us (17%)
  between operations  0.92 us (2%)
  local copies, waits for them, and re-layouts  0.69 us (1%)
    pallas_call x10, Pallas kernels, call(): pl.pallas_call(kernel, out_shape=out_shapes, in_specs=[HBM if n in hbm_in...  16.3 us
    ppermute x2, starting transfers between devices, body(): right_in = lax.ppermute(left, 'cols', to_left)  6.47 us
    ppermute x2, starting transfers between devices, body(): near_1 = lax.ppermute(near_1, 'rows', near_pairs)  5.95 us
    ppermute x2, waiting for transfers between devices, body(): left_in = lax.ppermute(right, 'cols', to_right)  4.99 us
    ppermute x2, starting transfers between devices, body(): left_in = lax.ppermute(right, 'cols', to_right)  4.02 us
    ppermute x2, starting transfers between devices, body(): near_2 = lax.ppermute(near_2, 'rows', near_pairs)  3.7 us
    ppermute x2, waiting for transfers between devices, body(): right_in = lax.ppermute(left, 'cols', to_left)  3.28 us
    ppermute x2, starting transfers between devices, body(): far_1 = lax.ppermute(far_1, 'rows', far_pairs)  3.21 us
  transfers between devices with their start and end apart: 12, of which 5 were waited for; matrix products, arithmetic and copies ran while one was open for 0% of the time, Pallas kernels for 22%

profile of v8, /device:TPU:1, one launch (start us, length us, event | category | flops | bytes accessed | tf_op | source)
XLA Modules:
  0.0 50.6 jit_solution(16457281644128567918)
XLA Ops:
  0.6 2.0 %shard_map.68 = (f32[256,1024]{1,0:T(8,128)S(1)}, f32[256,1024]{1,0:T(8,128)S(1)}, f32[256,256]{1,0:T(8,128)S(1)}, f32[8,256]{1,0:T(8,128)S(1)}, f32[152,256]{1,0:T(8,128)S(1)}, /*index=5*/f32[152,256]{1,0:T(8,128)S(1)}) custom-call(f32[256,1024]{1,0:T(8,128)} %dens_in.1, f32[256,1024]{1,0:T(8,128)} %value_in.1), custom_call_target="tpu_custom_call" | custom-call | flops 1000000000 | bytes 3000000 | tf_op jit(solution)/shard_map/pallas_call | solution.py:42
  2.6 3.1 %collective-permute-start = (f32[152,256]{1,0:T(8,128)S(1)}, f32[152,256]{1,0:T(8,128)S(1)}, u32[]{:S(2)}, u32[]{:S(2)}) collective-permute-start(f32[152,256]{1,0:T(8,128)S(1)} %get-tuple-element.53), channel_id=1, source_target_pairs={{8,16},{16,8},{24,32},{32,24},{40,48},{48,40},{56,64},{64,56},{72,... | collective-permute-start | bytes 466952 | tf_op jit(solution)/shard_map/ppermute | solution.py:519
  5.7 4.7 %collective-permute-start.1 = (f32[152,256]{1,0:T(8,128)S(1)}, f32[152,256]{1,0:T(8,128)S(1)}, u32[]{:S(2)}, u32[]{:S(2)}) collective-permute-start(f32[152,256]{1,0:T(8,128)S(1)} %get-tuple-element.54), channel_id=1, source_target_pairs={{0,8},{8,0},{16,24},{24,16},{32,40},{40,32},{48,56},{56,48},{64,72... | collective-permute-start | bytes 466952 | tf_op jit(solution)/shard_map/ppermute | solution.py:520
  10.4 1.2 %shard_map.69 = (f32[256,768]{1,0:T(8,128)S(1)}, f32[128,768]{1,0:T(8,128)S(1)}, f32[128,768]{1,0:T(8,128)S(1)}) custom-call(f32[256,1024]{1,0:T(8,128)S(1)} %get-tuple-element.48.dens, f32[256,1024]{1,0:T(8,128)S(1)} %get-tuple-element.49.value.refs_7_), custom_call_target="tpu_custom_call" | custom-call | flops 1000000000 | bytes 3000000 | tf_op jit(solution)/shard_map/pallas_call | solution.py:42
  11.7 0.1 collective-permute-start.2
  11.8 0.0 copy-start.1
  11.8 1.1 %collective-permute-start.3 = (f32[128,768]{1,0:T(8,128)S(1)}, f32[128,768]{1,0:T(8,128)S(1)}, u32[]{:S(2)}, u32[]{:S(2)}) collective-permute-start(f32[128,768]{1,0:T(8,128)S(1)} %get-tuple-element.59), channel_id=1, source_target_pairs={{0,8},{8,0},{16,24},{24,16},{32,40},{40,32},{48,56},{56,48},{64,72... | collective-permute-start | bytes 1179656 | tf_op jit(solution)/shard_map/ppermute | solution.py:522
  12.9 0.0 copy-done.1
  12.9 0.2 shard_map.70
  13.1 0.0 collective-permute-done.far
  13.1 0.0 collective-permute-done.1.near
  13.1 0.0 copy-start
  13.1 0.6 %shard_map.71 = (f32[280,128]{1,0:T(8,128)S(1)}, f32[280,128]{1,0:T(8,128)S(1)}, f32[8,1024]{1,0:T(8,128)S(1)}, f32[8,1024]{1,0:T(8,128)S(1)}, f32[8,768]{1,0:T(8,128)S(1)}, /*index=5*/f32[256,256]{1,0:T(8,128)S(1)}) custom-call(f32[256,1024]{1,0:T(8,128)S(1)} %get-tuple-element.48.dens, f32[256,1024]{1,0:T(8,128)S(1)} %get-tuple-element.49.value.refs_7_, ...), custom_call_target="tpu_custom_call" | custom-call | flops 6000000000 | bytes 18000000 | tf_op jit(solution)/shard_map/pallas_call | solution.py:42
  13.7 2.5 %collective-permute-start.4 = (f32[280,128]{1,0:T(8,128)S(1)}, f32[280,128]{1,0:T(8,128)S(1)}, u32[]{:S(2)}, u32[]{:S(2)}) collective-permute-start(f32[280,128]{1,0:T(8,128)S(1)} %get-tuple-element.63), channel_id=1, source_target_pairs={{0,1},{1,2},{2,3},{3,4},{4,5},{5,6},{6,7},{7,0},{8,9},{9,10},{10,1... | collective-permute-start | bytes 430088 | tf_op jit(solution)/shard_map/ppermute | solution.py:531
  16.2 2.6 %collective-permute-start.5 = (f32[280,128]{1,0:T(8,128)S(1)}, f32[280,128]{1,0:T(8,128)S(1)}, u32[]{:S(2)}, u32[]{:S(2)}) collective-permute-start(f32[280,128]{1,0:T(8,128)S(1)} %get-tuple-element.64), channel_id=1, source_target_pairs={{0,7},{1,0},{2,1},{3,2},{4,3},{5,4},{6,5},{7,6},{8,15},{9,8},{10,9... | collective-permute-start | bytes 430088 | tf_op jit(solution)/shard_map/ppermute | solution.py:530
  18.9 0.4 collective-permute-done.2.refs_2_
  19.2 0.0 collective-permute-done.3.refs_3_
  19.2 0.0 copy-start.2
  19.2 0.0 copy-done
  19.3 0.7 %copy-done.2 = f32[256]{0:T(256)S(1)} copy-done((f32[256]{0:T(256)S(1)}, f32[256]{0:T(256)}, u32[]{:S(2)}) %copy-start.2) | copy-done | bytes 1048
  19.9 3.1 %shard_map.72 = (f32[256,512]{1,0:T(8,128)S(1)}, f32[256,1024]{1,0:T(8,128)S(1)}, f32[8,256]{1,0:T(8,128)S(1)}, f32[256,1024]{1,0:T(8,128)S(1)}, f32[256,1024]{1...) custom-call(f32[256,768]{1,0:T(8,128)S(1)} %get-tuple-element.50.refs_0_, ...), custom_call_target="tpu_custom_call" | custom-call | flops 3000000000 | bytes 9000000 | tf_op jit(solution)/shard_map/pallas_call | solution.py:42
  23.0 3.9 %collective-permute-done.4.refs_4_ = f32[280,128]{1,0:T(8,128)S(1)} collective-permute-done((f32[280,128]{1,0:T(8,128)S(1)}, f32[280,128]{1,0:T(8,128)S(1)}, u32[]{:S(2)}, u32[]{:S(2)}) %collective-permute-start.4) | collective-permute-done | bytes 143392 | tf_op jit(solution)/shard_map/ppermute | solution.py:531
  26.9 1.3 %collective-permute-done.5.refs_5_ = f32[280,128]{1,0:T(8,128)S(1)} collective-permute-done((f32[280,128]{1,0:T(8,128)S(1)}, f32[280,128]{1,0:T(8,128)S(1)}, u32[]{:S(2)}, u32[]{:S(2)}) %collective-permute-start.5) | collective-permute-done | bytes 143392 | tf_op jit(solution)/shard_map/ppermute | solution.py:530
  28.2 1.5 %shard_map.73 = (f32[256,1024]{1,0:T(8,128)S(1)}, f32[256,1024]{1,0:T(8,128)S(1)}, f32[256,256]{1,0:T(8,128)S(1)}, f32[8,256]{1,0:T(8,128)S(1)}, f32[152,256]{1,0:T(8,128)S(1)}, /*index=5*/f32[152,256]{1,0:T(8,128)S(1)}) custom-call(f32[8,256]{1,0:T(8,128)S(1)} %get-tuple-element.61.refs_0_, ...), custom_call_target="tpu_custom_call", output_to_operand_aliasing={{0}: (13, {}), {1}: (14, {})} | custom-call | flops 1000000000 | bytes 3000000 | tf_op jit(solution)/shard_map/pallas_call | solution.py:42
  29.8 0.1 collective-permute-start.6
  29.9 1.3 %collective-permute-start.7 = (f32[152,256]{1,0:T(8,128)S(1)}, f32[152,256]{1,0:T(8,128)S(1)}, u32[]{:S(2)}, u32[]{:S(2)}) collective-permute-start(f32[152,256]{1,0:T(8,128)S(1)} %get-tuple-element.80), channel_id=1, source_target_pairs={{0,8},{8,0},{16,24},{24,16},{32,40},{40,32},{48,56},{56,48},{64,72... | collective-permute-start | bytes 466952 | tf_op jit(solution)/shard_map/ppermute | solution.py:520
  31.1 1.3 %shard_map.74 = (f32[256,768]{1,0:T(8,128)S(1)}, f32[128,768]{1,0:T(8,128)S(1)}, f32[128,768]{1,0:T(8,128)S(1)}) custom-call(f32[256,1024]{1,0:T(8,128)S(1)} %get-tuple-element.74.dens, f32[256,1024]{1,0:T(8,128)S(1)} %get-tuple-element.75.value.refs_8_), custom_call_target="tpu_custom_call" | custom-call | flops 1000000000 | bytes 3000000 | tf_op jit(solution)/shard_map/pallas_call | solution.py:42
  32.4 0.6 %collective-permute-start.8 = (f32[128,768]{1,0:T(8,128)S(1)}, f32[128,768]{1,0:T(8,128)S(1)}, u32[]{:S(2)}, u32[]{:S(2)}) collective-permute-start(f32[128,768]{1,0:T(8,128)S(1)} %get-tuple-element.82), channel_id=1, source_target_pairs={{8,16},{16,8},{24,32},{32,24},{40,48},{48,40},{56,64},{64,56},{72,... | collective-permute-start | bytes 1179656 | tf_op jit(solution)/shard_map/ppermute | solution.py:521
  33.0 2.6 %collective-permute-start.9 = (f32[128,768]{1,0:T(8,128)S(1)}, f32[128,768]{1,0:T(8,128)S(1)}, u32[]{:S(2)}, u32[]{:S(2)}) collective-permute-start(f32[128,768]{1,0:T(8,128)S(1)} %get-tuple-element.83), channel_id=1, source_target_pairs={{0,8},{8,0},{16,24},{24,16},{32,40},{40,32},{48,56},{56,48},{64,72... | collective-permute-start | bytes 1179656 | tf_op jit(solution)/shard_map/ppermute | solution.py:522
  35.6 0.0 collective-permute-done.6.far
  35.6 0.0 collective-permute-done.7.near
  35.6 0.6 %shard_map.75 = (f32[280,128]{1,0:T(8,128)S(1)}, f32[280,128]{1,0:T(8,128)S(1)}, f32[8,1024]{1,0:T(8,128)S(1)}, f32[8,1024]{1,0:T(8,128)S(1)}, f32[8,768]{1,0:T(8,128)S(1)}, /*index=5*/f32[256,256]{1,0:T(8,128)S(1)}) custom-call(f32[256,1024]{1,0:T(8,128)S(1)} %get-tuple-element.74.dens, f32[256,1024]{1,0:T(8,128)S(1)} %get-tuple-element.75.value.refs_8_, ...), custom_call_target="tpu_custom_call" | custom-call | flops 6000000000 | bytes 18000000 | tf_op jit(solution)/shard_map/pallas_call | solution.py:42
  36.2 1.5 %collective-permute-start.10 = (f32[280,128]{1,0:T(8,128)S(1)}, f32[280,128]{1,0:T(8,128)S(1)}, u32[]{:S(2)}, u32[]{:S(2)}) collective-permute-start(f32[280,128]{1,0:T(8,128)S(1)} %get-tuple-element.87), channel_id=1, source_target_pairs={{0,1},{1,2},{2,3},{3,4},{4,5},{5,6},{6,7},{7,0},{8,9},{9,10},{10,1... | collective-permute-start | bytes 430088 | tf_op jit(solution)/shard_map/ppermute | solution.py:531
  37.7 3.8 %collective-permute-start.11 = (f32[280,128]{1,0:T(8,128)S(1)}, f32[280,128]{1,0:T(8,128)S(1)}, u32[]{:S(2)}, u32[]{:S(2)}) collective-permute-start(f32[280,128]{1,0:T(8,128)S(1)} %get-tuple-element.88), channel_id=1, source_target_pairs={{0,7},{1,0},{2,1},{3,2},{4,3},{5,4},{6,5},{7,6},{8,15},{9,8},{10,9... | collective-permute-start | bytes 430088 | tf_op jit(solution)/shard_map/ppermute | solution.py:530
  41.5 0.0 collective-permute-done.8.refs_2_
  41.5 0.0 collective-permute-done.9.refs_3_
  41.5 3.9 %shard_map.76 = (f32[256,512]{1,0:T(8,128)S(1)}, f32[256,1024]{1,0:T(8,128)S(1)}, f32[8,256]{1,0:T(8,128)S(1)}, f32[256,1024]{1,0:T(8,128)}, f32[256,1024]{1,0:T(8,128)}) custom-call(f32[256,768]{1,0:T(8,128)S(1)} %get-tuple-element.76.refs_0_, f32[8,1024]{1,0:T(8,128)S(1)} %get-tuple-element.81.refs_1_.refs_2_, ...), custom_call_target="tpu_custom_call" | custom-call | flops 3000000000 | bytes 9000000 | tf_op jit(solution)/shard_map/pallas_call | solution.py:42
  45.5 1.1 %collective-permute-done.10.refs_4_ = f32[280,128]{1,0:T(8,128)S(1)} collective-permute-done((f32[280,128]{1,0:T(8,128)S(1)}, f32[280,128]{1,0:T(8,128)S(1)}, u32[]{:S(2)}, u32[]{:S(2)}) %collective-permute-start.10) | collective-permute-done | bytes 143392 | tf_op jit(solution)/shard_map/ppermute | solution.py:531
  46.6 2.0 %collective-permute-done.11.refs_5_ = f32[280,128]{1,0:T(8,128)S(1)} collective-permute-done((f32[280,128]{1,0:T(8,128)S(1)}, f32[280,128]{1,0:T(8,128)S(1)}, u32[]{:S(2)}, u32[]{:S(2)}) %collective-permute-start.11) | collective-permute-done | bytes 143392 | tf_op jit(solution)/shard_map/ppermute | solution.py:530
  48.5 1.9 %shard_map.77 = (f32[256,1024]{1,0:T(8,128)}, f32[256,1024]{1,0:T(8,128)}) custom-call(f32[8,256]{1,0:T(8,128)S(1)} %get-tuple-element.85.refs_0_, f32[256,256]{1,0:T(8,128)S(1)} %get-tuple-element.77.side.refs_1_, f32[8,1024]{1,0:T(8,128)S(1)} %get-tuple-element.81.refs_1_.refs_2_, ...), custom_call_target="tpu_custom_call", output_to_operand_aliasing={{0}: (13, {}), {1}: (14, {})} | custom-call | flops 1000000000 | bytes 3000000 | tf_op jit(solution)/shard_map/pallas_call | solution.py:42
Async XLA Ops:
  2.6 10.5 %collective-permute-start = (f32[152,256]{1,0:T(8,128)S(1)}, f32[152,256]{1,0:T(8,128)S(1)}, u32[]{:S(2)}, u32[]{:S(2)}) collective-permute-start(f32[152,256]{1,0:T(8,128)S(1)} %get-tuple-element.53), channel_id=1, source_target_pairs={{8,16},{16,8},{24,32},{32,24},{40,48},{48,40},{56,64},{64,56},{72,... | collective-permute-start | bytes 466952 | tf_op jit(solution)/shard_map/ppermute | solution.py:519
  5.7 7.4 %collective-permute-start.1 = (f32[152,256]{1,0:T(8,128)S(1)}, f32[152,256]{1,0:T(8,128)S(1)}, u32[]{:S(2)}, u32[]{:S(2)}) collective-permute-start(f32[152,256]{1,0:T(8,128)S(1)} %get-tuple-element.54), channel_id=1, source_target_pairs={{0,8},{8,0},{16,24},{24,16},{32,40},{40,32},{48,56},{56,48},{64,72... | collective-permute-start | bytes 466952 | tf_op jit(solution)/shard_map/ppermute | solution.py:520
  11.7 7.6 %collective-permute-start.2 = (f32[128,768]{1,0:T(8,128)S(1)}, f32[128,768]{1,0:T(8,128)S(1)}, u32[]{:S(2)}, u32[]{:S(2)}) collective-permute-start(f32[128,768]{1,0:T(8,128)S(1)} %get-tuple-element.58), channel_id=1, source_target_pairs={{8,16},{16,8},{24,32},{32,24},{40,48},{48,40},{56,64},{64,56},{72,... | collective-permute-start | bytes 1179656 | tf_op jit(solution)/shard_map/ppermute | solution.py:521
  11.8 1.1 %copy-start.1 = (f32[256]{0:T(256)S(1)}, f32[256]{0:T(256)}, u32[]{:S(2)}) copy-start(f32[256]{0:T(256)} %param.8) | copy-start | bytes 3076
  11.8 7.5 %collective-permute-start.3 = (f32[128,768]{1,0:T(8,128)S(1)}, f32[128,768]{1,0:T(8,128)S(1)}, u32[]{:S(2)}, u32[]{:S(2)}) collective-permute-start(f32[128,768]{1,0:T(8,128)S(1)} %get-tuple-element.59), channel_id=1, source_target_pairs={{0,8},{8,0},{16,24},{24,16},{32,40},{40,32},{48,56},{56,48},{64,72... | collective-permute-start | bytes 1179656 | tf_op jit(solution)/shard_map/ppermute | solution.py:522
  13.1 6.1 %copy-start = (f32[256,1024]{1,0:T(8,128)S(1)}, f32[256,1024]{1,0:T(8,128)}, u32[]{:S(2)}) copy-start(f32[256,1024]{1,0:T(8,128)} %refs_9_.1) | copy-start | bytes 3145732
  13.7 13.2 %collective-permute-start.4 = (f32[280,128]{1,0:T(8,128)S(1)}, f32[280,128]{1,0:T(8,128)S(1)}, u32[]{:S(2)}, u32[]{:S(2)}) collective-permute-start(f32[280,128]{1,0:T(8,128)S(1)} %get-tuple-element.63), channel_id=1, source_target_pairs={{0,1},{1,2},{2,3},{3,4},{4,5},{5,6},{6,7},{7,0},{8,9},{9,10},{10,1... | collective-permute-start | bytes 430088 | tf_op jit(solution)/shard_map/ppermute | solution.py:531
  16.2 12.0 %collective-permute-start.5 = (f32[280,128]{1,0:T(8,128)S(1)}, f32[280,128]{1,0:T(8,128)S(1)}, u32[]{:S(2)}, u32[]{:S(2)}) collective-permute-start(f32[280,128]{1,0:T(8,128)S(1)} %get-tuple-element.64), channel_id=1, source_target_pairs={{0,7},{1,0},{2,1},{3,2},{4,3},{5,4},{6,5},{7,6},{8,15},{9,8},{10,9... | collective-permute-start | bytes 430088 | tf_op jit(solution)/shard_map/ppermute | solution.py:530
  19.2 0.7 %copy-start.2 = (f32[256]{0:T(256)S(1)}, f32[256]{0:T(256)}, u32[]{:S(2)}) copy-start(f32[256]{0:T(256)} %param.9) | copy-start | bytes 3076
  29.8 5.9 %collective-permute-start.6 = (f32[152,256]{1,0:T(8,128)S(1)}, f32[152,256]{1,0:T(8,128)S(1)}, u32[]{:S(2)}, u32[]{:S(2)}) collective-permute-start(f32[152,256]{1,0:T(8,128)S(1)} %get-tuple-element.79), channel_id=1, source_target_pairs={{8,16},{16,8},{24,32},{32,24},{40,48},{48,40},{56,64},{64,56},{72,... | collective-permute-start | bytes 466952 | tf_op jit(solution)/shard_map/ppermute | solution.py:519
  29.9 5.8 %collective-permute-start.7 = (f32[152,256]{1,0:T(8,128)S(1)}, f32[152,256]{1,0:T(8,128)S(1)}, u32[]{:S(2)}, u32[]{:S(2)}) collective-permute-start(f32[152,256]{1,0:T(8,128)S(1)} %get-tuple-element.80), channel_id=1, source_target_pairs={{0,8},{8,0},{16,24},{24,16},{32,40},{40,32},{48,56},{56,48},{64,72... | collective-permute-start | bytes 466952 | tf_op jit(solution)/shard_map/ppermute | solution.py:520
  32.4 9.1 %collective-permute-start.8 = (f32[128,768]{1,0:T(8,128)S(1)}, f32[128,768]{1,0:T(8,128)S(1)}, u32[]{:S(2)}, u32[]{:S(2)}) collective-permute-start(f32[128,768]{1,0:T(8,128)S(1)} %get-tuple-element.82), channel_id=1, source_target_pairs={{8,16},{16,8},{24,32},{32,24},{40,48},{48,40},{56,64},{64,56},{72,... | collective-permute-start | bytes 1179656 | tf_op jit(solution)/shard_map/ppermute | solution.py:521
  33.0 8.5 %collective-permute-start.9 = (f32[128,768]{1,0:T(8,128)S(1)}, f32[128,768]{1,0:T(8,128)S(1)}, u32[]{:S(2)}, u32[]{:S(2)}) collective-permute-start(f32[128,768]{1,0:T(8,128)S(1)} %get-tuple-element.83), channel_id=1, source_target_pairs={{0,8},{8,0},{16,24},{24,16},{32,40},{40,32},{48,56},{56,48},{64,72... | collective-permute-start | bytes 1179656 | tf_op jit(solution)/shard_map/ppermute | solution.py:522
  36.2 10.4 %collective-permute-start.10 = (f32[280,128]{1,0:T(8,128)S(1)}, f32[280,128]{1,0:T(8,128)S(1)}, u32[]{:S(2)}, u32[]{:S(2)}) collective-permute-start(f32[280,128]{1,0:T(8,128)S(1)} %get-tuple-element.87), channel_id=1, source_target_pairs={{0,1},{1,2},{2,3},{3,4},{4,5},{5,6},{6,7},{7,0},{8,9},{9,10},{10,1... | collective-permute-start | bytes 430088 | tf_op jit(solution)/shard_map/ppermute | solution.py:531
  37.7 10.8 %collective-permute-start.11 = (f32[280,128]{1,0:T(8,128)S(1)}, f32[280,128]{1,0:T(8,128)S(1)}, u32[]{:S(2)}, u32[]{:S(2)}) collective-permute-start(f32[280,128]{1,0:T(8,128)S(1)} %get-tuple-element.88), channel_id=1, source_target_pairs={{0,7},{1,0},{2,1},{3,2},{4,3},{5,4},{6,5},{7,6},{8,15},{9,8},{10,9... | collective-permute-start | bytes 430088 | tf_op jit(solution)/shard_map/ppermute | solution.py:530
